TPU v7x, 32 devices: a whole 2x2x4 slice. The times are simulated.
32 devices in a mesh: depth: 16 (over z, x, core), shot: 2 (over y).
Axes of the slice: x: 2, y: 2, z: 4, core: 2. Of those that a mesh axis runs over, the one named last changes fastest.
Arguments:
- courant: float32 [256, 64, 128], P('depth'), may hold values from 0.04 to 0.2
- wave_before: float32 [2, 256, 64, 128], P('shot', 'depth'), may hold values from -10 to 10
- wave_current: float32 [2, 256, 64, 128], P('shot', 'depth'), may hold values from -10 to 10
- adjoint_after: float32 [2, 256, 64, 128], P('shot', 'depth'), may hold values from -10 to 10
- adjoint_current: float32 [2, 256, 64, 128], P('shot', 'depth'), may hold values from -10 to 10
- source_cell: int32 [2], P('shot'), may hold values from 0 to 2097151
- wavelet: float32 [2, 4], P('shot'), may hold values from -15 to 15
- receiver_cell: int32 [2, 256], P('shot'), may hold values from 0 to 2097151
- residual: float32 [2, 4, 256], P('shot'), may hold values from -12 to 12
- history: float32 [2, 5, 256, 64, 128], P(None, None, 'depth', 'shot'), may hold values from -23 to 23, as said below
Outputs:
- gradient: float32 [256, 64, 128], P('depth', 'shot')
- direction: float32 [256, 64, 128], P('depth', 'shot')
- courant_next: float32 [256, 64, 128], P('depth')
Inputs may be any that keep to these rules, and one draw needn't show every extreme that they name: In every pair the sum over all cells of history[0] times history[1] is positive.
All inputs are finite; a program needn't handle non-finite values.
Results may differ from a plain program's by a relative error of at most 0.00026.
Values sent between devices are 32-bit elements; how exact they have to be, the bound alone decides.
No kernel may reach another device: no remote copies, remote signals or barrier semaphores. Data moves between devices by JAX's collectives and lax.ppermute only.
A program may use at most 128 MiB of HBM per device.

v0:
```python
import jax
import jax.numpy as jnp
from jax import lax
from jax.sharding import PartitionSpec as P

STEPS = 4
PAIRS = 5


coefficients = (-205.0 / 72.0, 8.0 / 5.0, -1.0 / 5.0, 8.0 / 315.0, -1.0 / 560.0)


def with_halo(cells, sides, width):
    for axis, dim in sides:
        count = lax.axis_size(axis)
        ends = count - 1
        head = lax.slice_in_dim(cells, 0, width, axis=dim)
        tail = lax.slice_in_dim(cells, cells.shape[dim] - width, cells.shape[dim], axis=dim)
        cells = jnp.concatenate(
            [
                lax.ppermute(tail, axis, [(i, (i + 1) % count) for i in range(ends)]),
                cells,
                lax.ppermute(head, axis, [((i + 1) % count, i) for i in range(ends)]),
            ],
            axis=dim,
        )
    return cells


def laplace_core(extended):
    interior = extended[4:-4]
    count_rows = interior.shape[0]
    width_x = interior.shape[1]
    width_y = interior.shape[2]
    padded = jnp.pad(interior, ((0, 0), (4, 4), (4, 4)))
    summed = 3.0 * coefficients[0] * interior
    for reach in range(1, 5):
        weight = coefficients[reach]
        summed = summed + weight * (
            extended[4 + reach : 4 + reach + count_rows]
            + extended[4 - reach : 4 - reach + count_rows]
        )
        summed = summed + weight * (
            padded[:, 4 + reach : 4 + reach + width_x, 4 : 4 + width_y]
            + padded[:, 4 - reach : 4 - reach + width_x, 4 : 4 + width_y]
        )
        summed = summed + weight * (
            padded[:, 4 : 4 + width_x, 4 + reach : 4 + reach + width_y]
            + padded[:, 4 : 4 + width_x, 4 - reach : 4 - reach + width_y]
        )
    return summed


def inject(volume, cell_ids, values, offset):
    count_rows = volume.shape[0]
    plane_size = volume.shape[1] * volume.shape[2]
    depth_row = cell_ids // plane_size - offset
    remainder = cell_ids % plane_size
    inside = (depth_row >= 0) & (depth_row < count_rows)
    row_safe = jnp.clip(depth_row, 0, count_rows - 1)
    return volume.at[row_safe, remainder // volume.shape[2], remainder % volume.shape[2]].add(
        jnp.where(inside, values, jnp.zeros_like(values))
    )


def per_device(
    courant,
    wave_before,
    wave_current,
    adjoint_after,
    adjoint_current,
    source_cell,
    wavelet,
    receiver_cell,
    residual,
    history,
):
    slab_rows = courant.shape[0]
    first_row = lax.axis_index("depth") * slab_rows
    shot_count = lax.axis_size("shot")
    summed = jnp.zeros(courant.shape, jnp.float32)
    laplacians = []
    wave_old = wave_before[0]
    wave_now = wave_current[0]
    for moment in range(STEPS):
        extended = with_halo(wave_now, (("depth", 0),), 4)
        laplacian = laplace_core(extended)
        wave_new = 2.0 * wave_now - wave_old + courant * laplacian
        wave_new = inject(wave_new, source_cell, wavelet[0, moment : moment + 1], first_row)
        laplacians.append(laplacian)
        wave_old, wave_now = (wave_now, wave_new)
    adjoint_old = adjoint_after[0]
    adjoint_now = adjoint_current[0]
    for moment in reversed(range(STEPS)):
        extended = with_halo(courant * adjoint_now, (("depth", 0),), 4)
        adjoint_new = 2.0 * adjoint_now - adjoint_old + laplace_core(extended)
        adjoint_new = inject(adjoint_new, receiver_cell[0], residual[0, moment], first_row)
        summed = summed + adjoint_new * laplacians[moment]
        adjoint_old, adjoint_now = (adjoint_now, adjoint_new)
    grad_piece = lax.psum_scatter(summed, "shot", scatter_dimension=1, tiled=True) * (
        1.0 / (shot_count * STEPS)
    )
    displaced = history[0]
    changes = history[1]
    pair_dots = jnp.sum(displaced * changes, axis=(1, 2, 3))
    last_square = jnp.sum(changes[PAIRS - 1] * changes[PAIRS - 1])
    curvature, last_square = lax.psum((pair_dots, last_square), ("depth", "shot"))
    inverse = 1.0 / curvature
    search = grad_piece
    alphas = [None] * PAIRS
    for number in reversed(range(PAIRS)):
        alphas[number] = inverse[number] * lax.psum(
            jnp.sum(displaced[number] * search), ("depth", "shot")
        )
        search = search - alphas[number] * changes[number]
    scaled = curvature[PAIRS - 1] / last_square * search
    for number in range(PAIRS):
        correction = inverse[number] * lax.psum(
            jnp.sum(changes[number] * scaled), ("depth", "shot")
        )
        scaled = scaled + (alphas[number] - correction) * displaced[number]
    direction = -scaled
    piece_width = grad_piece.shape[1]
    own_courant = lax.dynamic_slice_in_dim(
        courant, lax.axis_index("shot") * piece_width, piece_width, 1
    )
    next_piece = own_courant + 0.05 * direction
    courant_next = lax.all_gather(next_piece, "shot", axis=1, tiled=True)
    return (grad_piece, direction, courant_next)


def solution(mesh):
    return jax.shard_map(
        per_device,
        mesh=mesh,
        in_specs=(
            P("depth", None, None),
            P("shot", "depth", None, None),
            P("shot", "depth", None, None),
            P("shot", "depth", None, None),
            P("shot", "depth", None, None),
            P("shot"),
            P("shot", None),
            P("shot", None),
            P("shot", None, None),
            P(None, None, "depth", "shot", None),
        ),
        out_specs=(P("depth", "shot", None), P("depth", "shot", None), P("depth", None, None)),
        check_vma=False,
    )
```

profile of v0, /device:TPU:0, one launch (start us, length us, event | category | flops | bytes accessed | tf_op | source)
XLA Modules:
  0.0 684.7 jit_solution(16988413947042508864)
XLA Ops:
  7.3 1.8 slice_bitcast_fusion.1
  9.1 1.3 collective-permute-start.2
  10.3 3.0 collective-permute-start.3
  13.4 1.3 bitcast_multiply_fusion
  14.7 1.4 collective-permute-start
  16.1 5.7 collective-permute-start.1
  26.5 2.2 fusion.184
  28.7 24.0 %scatter_fusion = f32[16,64,128]{2,1,0:T(8,128)S(1)} fusion(f32[16,64,128]{2,1,0:T(8,128)S(1)} %fusion.184, s32[256]{0:T(256)S(1)} %bitcast.166, f32[256]{0:T(256)} %get-tuple-element.95), kind=kCustom, calls=%fused_computation | custom fusion | flops 256 | bytes 6144 | tf_op jit(solution)/shard_map/scatter-add | solution.py:61
  52.7 3.7 fusion.344
  57.1 1.3 collective-permute-start.10
  58.4 3.6 collective-permute-start.11
  65.4 1.3 collective-permute-start.4
  66.7 4.9 collective-permute-start.5
  71.6 8.4 %fusion.59 = f32[16,64,128]{2,1,0:T(8,128)S(1)} fusion(f32[16,64,128]{2,1,0:T(8,128)} %copy-done.10, f32[4,64,128]{2,1,0:T(8,128)S(1)} %collective-permute-done.11, f32[4,64,128]{2,1,0:T(8,128)S(1)} %collective-permute-done.10, f32[1,16,64,128]{3,2,1,0:T(8,128)S(1)} %copy-done.6, f32[16,64,128]{2,1,0:T(8,128)S(1)} %scatter_fusion), kind=kLoop, calls=%fused_computation.288 | loop fusion | flops 6291456 | bytes 2359296 | tf_op jit(solution)/shard_map/add | solution.py:96
  80.0 15.2 %scatter_fusion.1 = f32[16,64,128]{2,1,0:T(8,128)S(1)} fusion(f32[16,64,128]{2,1,0:T(8,128)S(1)} %fusion.59, s32[256]{0:T(256)S(1)} %bitcast.167, f32[256]{0:T(256)S(1)} %get-tuple-element.94), kind=kCustom, calls=%fused_computation.1 | custom fusion | flops 256 | bytes 6144 | tf_op jit(solution)/shard_map/scatter-add | solution.py:61
  95.3 3.9 multiply_add_fusion.1
  101.7 1.3 collective-permute-start.12
  103.0 4.3 collective-permute-start.13
  108.1 1.3 collective-permute-start.6
  109.4 4.6 collective-permute-start.7
  114.0 7.9 %fusion.34 = f32[16,64,128]{2,1,0:T(8,128)S(1)} fusion(f32[16,64,128]{2,1,0:T(8,128)} %copy-done.11, f32[4,64,128]{2,1,0:T(8,128)} %collective-permute-done.13, f32[4,64,128]{2,1,0:T(8,128)S(1)} %collective-permute-done.12, f32[16,64,128]{2,1,0:T(8,128)S(1)} %scatter_fusion, f32[16,64,128]{2,1,0:T(8,128)S(1)} %scatter_fusion.1), kind=kLoop, calls=%fused_computation.263 | loop fusion | flops 6291456 | bytes 2359296 | tf_op jit(solution)/shard_map/add | solution.py:96
  122.0 15.2 %scatter_fusion.2 = f32[16,64,128]{2,1,0:T(8,128)S(1)} fusion(f32[16,64,128]{2,1,0:T(8,128)S(1)} %fusion.34, s32[256]{0:T(256)S(1)} %bitcast.168, f32[256]{0:T(256)S(1)} %get-tuple-element.93), kind=kCustom, calls=%fused_computation.2 | custom fusion | flops 256 | bytes 6144 | tf_op jit(solution)/shard_map/scatter-add | solution.py:61
  137.3 9.3 %multiply_add_fusion = (f32[16,64,128]{2,1,0:T(8,128)S(1)}, f32[16,64,128]{2,1,0:T(8,128)}, f32[16,64,128]{2,1,0:T(8,128)S(1)}) fusion(f32[16,64,128]{2,1,0:T(8,128)S(1)} %copy-done.3, f32[16,64,128]{2,1,0:T(8,128)S(1)} %scatter-add.44, f32[16,64,128]{2,1,0:T(8,128)} %copy-done.8, f32[4,64,128]{2,1,0:T(8,128)S(1)} %collective-permute-done.7, ...), kind=kLoop, calls=%fused_computation.595 | loop fusion | flops 6553600 | bytes 3932160 | tf_op jit(solution)/shard_map/add | solution.py:88
  149.1 1.3 collective-permute-start.14
  150.4 5.1 collective-permute-start.15
  155.7 1.3 collective-permute-start.8
  157.0 5.2 collective-permute-start.9
  162.2 10.5 %fusion.9 = f32[16,64,128]{2,1,0:T(8,128)} fusion(f32[16,64,128]{2,1,0:T(8,128)} %copy-done.9, f32[4,64,128]{2,1,0:T(8,128)S(1)} %collective-permute-done.15, f32[4,64,128]{2,1,0:T(8,128)S(1)} %collective-permute-done.14, f32[16,64,128]{2,1,0:T(8,128)S(1)} %scatter_fusion.1, f32[16,64,128]{2,1,0:T(8,128)S(1)} %scatter_fusion.2), kind=kLoop, calls=%fused_computation.238 | loop fusion | flops 6291456 | bytes 2359296 | tf_op jit(solution)/shard_map/add | solution.py:96
  172.7 34.5 %scatter_fusion.3 = f32[16,64,128]{2,1,0:T(8,128)} fusion(f32[16,64,128]{2,1,0:T(8,128)} %fusion.9, s32[256]{0:T(256)S(1)} %bitcast.169, f32[256]{0:T(256)S(1)} %get-tuple-element.57), kind=kCustom, calls=%fused_computation.3 | custom fusion | flops 256 | bytes 6144 | tf_op jit(solution)/shard_map/scatter-add | solution.py:61
  207.2 10.2 %fusion.87 = f32[16,64,128]{2,1,0:T(8,128)} fusion(f32[16,64,128]{2,1,0:T(8,128)S(1)} %scatter_fusion, f32[16,64,128]{2,1,0:T(8,128)} %copy-done.7, f32[4,64,128]{2,1,0:T(8,128)S(1)} %collective-permute-done.9, f32[4,64,128]{2,1,0:T(8,128)S(1)} %collective-permute-done.8, f32[16,64,128]{2,1,0:T(8,128)} %scatter_fusion.3, ...), kind=kLoop, calls=%fused_computation.316 | loop fusion | flops 6815744 | bytes 4980736 | tf_op jit(solution)/shard_map/add | solution.py:98
  217.7 20.1 %reduce-scatter.2.cloned.1.call-done = f32[16,32,128]{2,1,0:T(8,128)} async-done(((f32[16,64,128]{2,1,0:T(8,128)}), f32[16,32,128]{2,1,0:T(8,128)}) %reduce-scatter.2.cloned.1.call-update) | async-done | bytes 262160 | tf_op jit(solution)/shard_map/reduce_scatter | solution.py:100
  237.8 1.6 fusion.362
  239.5 39.5 %all-reduce.9 = (f32[5]{0:T(128)S(1)}, f32[]{:T(128)}) all-reduce(f32[5]{0:T(128)S(1)} %multiply_reduce_fusion, f32[]{:T(128)} %get-tuple-element.55), channel_id=1, replica_groups=mesh['depth'=16,'shot'=2] {'depth','shot'}, use_global_device_ids=true, to_apply=%region_7.8 | all-reduce | flops 6 | bytes 48 | tf_op jit(solution)/shard_map/psum | solution.py:107
  282.3 41.4 %psum.87 = f32[]{:T(128)} all-reduce(f32[]{:T(128)} %fusion.360), channel_id=1, replica_groups=mesh['depth'=16,'shot'=2] {'depth','shot'}, use_global_device_ids=true, to_apply=%region_13.14 | all-reduce | flops 1 | bytes 8 | tf_op jit(solution)/shard_map/psum | solution.py:112
  325.5 39.5 %psum.88 = f32[]{:T(128)} all-reduce(f32[]{:T(128)} %get-tuple-element.53), channel_id=1, replica_groups=mesh['depth'=16,'shot'=2] {'depth','shot'}, use_global_device_ids=true, to_apply=%region_15.16 | all-reduce | flops 1 | bytes 8 | tf_op jit(solution)/shard_map/psum | solution.py:112
  367.1 41.3 %psum.89 = f32[]{:T(128)} all-reduce(f32[]{:T(128)} %get-tuple-element.40), channel_id=1, replica_groups=mesh['depth'=16,'shot'=2] {'depth','shot'}, use_global_device_ids=true, to_apply=%region_17.18 | all-reduce | flops 1 | bytes 8 | tf_op jit(solution)/shard_map/psum | solution.py:112
  410.3 39.8 %all-reduce.8 = (f32[]{:T(128)}, f32[]{:T(128)}) all-reduce(f32[]{:T(128)} %get-tuple-element.51, f32[]{:T(128)} %get-tuple-element.39), channel_id=1, replica_groups=mesh['depth'=16,'shot'=2] {'depth','shot'}, use_global_device_ids=true, to_apply=%region_19.20 | all-reduce | flops 2 | bytes 16 | tf_op jit(solution)/shard_map/psum | solution.py:112
  453.3 41.4 %psum.91 = f32[]{:T(128)} all-reduce(f32[]{:T(128)} %fusion.347), channel_id=1, replica_groups=mesh['depth'=16,'shot'=2] {'depth','shot'}, use_global_device_ids=true, to_apply=%region_21.22 | all-reduce | flops 1 | bytes 8 | tf_op jit(solution)/shard_map/psum | solution.py:118
  495.9 1.5 fusion.351
  497.4 39.5 %psum.92 = f32[]{:T(128)} all-reduce(f32[]{:T(128)} %get-tuple-element.49), channel_id=1, replica_groups=mesh['depth'=16,'shot'=2] {'depth','shot'}, use_global_device_ids=true, to_apply=%region_23.24 | all-reduce | flops 1 | bytes 8 | tf_op jit(solution)/shard_map/psum | solution.py:118
  538.2 1.6 fusion.355
  539.8 41.4 %psum.93 = f32[]{:T(128)} all-reduce(f32[]{:T(128)} %fusion.355), channel_id=1, replica_groups=mesh['depth'=16,'shot'=2] {'depth','shot'}, use_global_device_ids=true, to_apply=%region_25.26 | all-reduce | flops 1 | bytes 8 | tf_op jit(solution)/shard_map/psum | solution.py:118
  582.5 1.6 fusion.359
  584.2 39.5 %psum.94 = f32[]{:T(128)} all-reduce(f32[]{:T(128)} %get-tuple-element.47), channel_id=1, replica_groups=mesh['depth'=16,'shot'=2] {'depth','shot'}, use_global_device_ids=true, to_apply=%region_27.28 | all-reduce | flops 1 | bytes 8 | tf_op jit(solution)/shard_map/psum | solution.py:118
  625.5 41.4 %psum.95 = f32[]{:T(128)} all-reduce(f32[]{:T(128)} %fusion.367), channel_id=1, replica_groups=mesh['depth'=16,'shot'=2] {'depth','shot'}, use_global_device_ids=true, to_apply=%region_29.30 | all-reduce | flops 1 | bytes 8 | tf_op jit(solution)/shard_map/psum | solution.py:118
  668.2 0.8 multiply_add_fusion.2
  669.0 8.1 %all_gather.3 = f32[16,64,128]{2,1,0:T(8,128)S(1)} all-gather(f32[16,32,128]{2,1,0:T(8,128)S(1)} %get-tuple-element.45), channel_id=1, replica_groups=mesh['depth'=16,'shot'=2] {'shot'}, dimensions={1}, use_global_device_ids=true | all-gather | bytes 786432 | tf_op jit(solution)/shard_map/all_gather | solution.py:128
  677.1 0.8 copy.22
  (83 shorter events, 12.4 us)
Async XLA Ops:
  7.2 18.6 %copy-start.17 = (s32[3]{0:T(128)S(1)}, s32[3]{0:T(128)}, u32[]{:S(2)}) copy-start(s32[3]{0:T(128)} %constant.251.clone.1) | copy-start | bytes 40
  7.2 19.3 %copy-start.6 = (f32[1,16,64,128]{3,2,1,0:T(8,128)S(1)}, f32[1,16,64,128]{3,2,1,0:T(8,128)}, u32[]{:S(2)}) copy-start(f32[1,16,64,128]{3,2,1,0:T(8,128)} %param.20) | copy-start | bytes 1572868
  7.2 14.7 %copy-start.15 = (f32[1,4,256]{2,1,0:T(4,128)S(1)}, f32[1,4,256]{2,1,0:T(4,128)}, u32[]{:S(2)}) copy-start(f32[1,4,256]{2,1,0:T(4,128)} %param.24) | copy-start | bytes 12292
  7.2 14.7 %copy-start.16 = (s32[1,256]{1,0:T(1,128)S(1)}, s32[1,256]{1,0:T(1,128)}, u32[]{:S(2)}) copy-start(s32[1,256]{1,0:T(1,128)} %param.23) | copy-start | bytes 3076
  7.2 15.3 %copy-start.14 = (f32[1,4]{1,0:T(1,128)S(1)}, f32[1,4]{1,0:T(1,128)}, u32[]{:S(2)}) copy-start(f32[1,4]{1,0:T(1,128)} %param.22) | copy-start | bytes 52
  7.2 19.2 %copy-start.13 = (f32[1,16,64,128]{3,2,1,0:T(8,128)S(1)}, f32[1,16,64,128]{3,2,1,0:T(8,128)}, u32[]{:S(2)}) copy-start(f32[1,16,64,128]{3,2,1,0:T(8,128)} %param.19) | copy-start | bytes 1572868
  7.2 230.6 %reduce-scatter.2.cloned.1.call-start = ((), (), s32[]{:S(2)}) async-start(), calls=%async_computation.1 | async-start | bytes 786432 | tf_op jit(solution)/shard_map/reduce_scatter | solution.py:100
  9.1 43.6 %collective-permute-start.2 = (f32[4,64,128]{2,1,0:T(8,128)}, f32[4,64,128]{2,1,0:T(8,128)S(1)}, u32[]{:S(2)}, u32[]{:S(2)}) collective-permute-start(f32[4,64,128]{2,1,0:T(8,128)} %get-tuple-element.80), channel_id=1, source_target_pairs={{2,0},{4,2},{6,4},{8,6},{10,8},{12,10},{14,12},{16,14},{18,16},{20... | collective-permute-start | bytes 393224 | tf_op jit(solution)/shard_map/ppermute | solution.py:23
  10.3 42.3 %collective-permute-start.3 = (f32[4,64,128]{2,1,0:T(8,128)}, f32[4,64,128]{2,1,0:T(8,128)S(1)}, u32[]{:S(2)}, u32[]{:S(2)}) collective-permute-start(f32[4,64,128]{2,1,0:T(8,128)} %get-tuple-element.81), channel_id=1, source_target_pairs={{0,2},{2,4},{4,6},{6,8},{8,10},{10,12},{12,14},{14,16},{16,18},{18... | collective-permute-start | bytes 393224 | tf_op jit(solution)/shard_map/ppermute | solution.py:21
  14.7 38.0 %copy-start.3 = (f32[16,64,128]{2,1,0:T(8,128)S(1)}, f32[16,64,128]{2,1,0:T(8,128)}, u32[]{:S(2)}) copy-start(f32[16,64,128]{2,1,0:T(8,128)} %param.16) | copy-start | bytes 1572868
  14.7 38.0 %copy-start.5 = (f32[1,16,64,128]{3,2,1,0:T(8,128)S(1)}, f32[1,16,64,128]{3,2,1,0:T(8,128)}, u32[]{:S(2)}) copy-start(f32[1,16,64,128]{3,2,1,0:T(8,128)} %param.18) | copy-start | bytes 1572868
  14.7 11.7 %collective-permute-start = (f32[4,64,128]{2,1,0:T(8,128)S(1)}, f32[4,64,128]{2,1,0:T(8,128)S(1)}, u32[]{:S(2)}, u32[]{:S(2)}) collective-permute-start(f32[4,64,128]{2,1,0:T(8,128)S(1)} %get-tuple-element.82), channel_id=1, source_target_pairs={{2,0},{4,2},{6,4},{8,6},{10,8},{12,10},{14,12},{16,14},{18,16},{20... | collective-permute-start | bytes 393224 | tf_op jit(solution)/shard_map/ppermute | solution.py:23
  16.1 10.3 %collective-permute-start.1 = (f32[4,64,128]{2,1,0:T(8,128)S(1)}, f32[4,64,128]{2,1,0:T(8,128)}, u32[]{:S(2)}, u32[]{:S(2)}) collective-permute-start(f32[4,64,128]{2,1,0:T(8,128)S(1)} %get-tuple-element.83), channel_id=1, source_target_pairs={{0,2},{2,4},{4,6},{6,8},{8,10},{10,12},{12,14},{14,16},{16,18},{18... | collective-permute-start | bytes 393224 | tf_op jit(solution)/shard_map/ppermute | solution.py:21
  56.4 15.2 %copy-start.10 = (f32[16,64,128]{2,1,0:T(8,128)}, f32[16,64,128]{2,1,0:T(8,128)S(1)}, u32[]{:S(2)}) copy-start(f32[16,64,128]{2,1,0:T(8,128)S(1)} %get-tuple-element.73) | copy-start | bytes 1572868
  57.1 14.4 %collective-permute-start.10 = (f32[4,64,128]{2,1,0:T(8,128)}, f32[4,64,128]{2,1,0:T(8,128)S(1)}, u32[]{:S(2)}, u32[]{:S(2)}) collective-permute-start(f32[4,64,128]{2,1,0:T(8,128)} %get-tuple-element.71), channel_id=1, source_target_pairs={{2,0},{4,2},{6,4},{8,6},{10,8},{12,10},{14,12},{16,14},{18,16},{20... | collective-permute-start | bytes 393224 | tf_op jit(solution)/shard_map/ppermute | solution.py:23
  58.4 13.2 %collective-permute-start.11 = (f32[4,64,128]{2,1,0:T(8,128)}, f32[4,64,128]{2,1,0:T(8,128)S(1)}, u32[]{:S(2)}, u32[]{:S(2)}) collective-permute-start(f32[4,64,128]{2,1,0:T(8,128)} %get-tuple-element.72), channel_id=1, source_target_pairs={{0,2},{2,4},{4,6},{6,8},{8,10},{10,12},{12,14},{14,16},{16,18},{18... | collective-permute-start | bytes 393224 | tf_op jit(solution)/shard_map/ppermute | solution.py:21
  65.4 29.9 %collective-permute-start.4 = (f32[4,64,128]{2,1,0:T(8,128)}, f32[4,64,128]{2,1,0:T(8,128)S(1)}, u32[]{:S(2)}, u32[]{:S(2)}) collective-permute-start(f32[4,64,128]{2,1,0:T(8,128)} %get-tuple-element.78), channel_id=1, source_target_pairs={{2,0},{4,2},{6,4},{8,6},{10,8},{12,10},{14,12},{16,14},{18,16},{20... | collective-permute-start | bytes 393224 | tf_op jit(solution)/shard_map/ppermute | solution.py:23
  66.7 28.6 %collective-permute-start.5 = (f32[4,64,128]{2,1,0:T(8,128)}, f32[4,64,128]{2,1,0:T(8,128)}, u32[]{:S(2)}, u32[]{:S(2)}) collective-permute-start(f32[4,64,128]{2,1,0:T(8,128)} %get-tuple-element.79), channel_id=1, source_target_pairs={{0,2},{2,4},{4,6},{6,8},{8,10},{10,12},{12,14},{14,16},{16,18},{18... | collective-permute-start | bytes 393224 | tf_op jit(solution)/shard_map/ppermute | solution.py:21
  95.2 67.0 %copy-start.1 = (f32[16,64,128]{2,1,0:T(8,128)}, f32[16,64,128]{2,1,0:T(8,128)S(1)}, u32[]{:S(2)}) copy-start(f32[16,64,128]{2,1,0:T(8,128)S(1)} %scatter_fusion.1) | copy-start | bytes 1572868
  99.1 3.8 copy-start.11
  101.7 12.4 %collective-permute-start.12 = (f32[4,64,128]{2,1,0:T(8,128)S(1)}, f32[4,64,128]{2,1,0:T(8,128)S(1)}, u32[]{:S(2)}, u32[]{:S(2)}) collective-permute-start(f32[4,64,128]{2,1,0:T(8,128)S(1)} %get-tuple-element.68), channel_id=1, source_target_pairs={{2,0},{4,2},{6,4},{8,6},{10,8},{12,10},{14,12},{16,14},{18,16},{20... | collective-permute-start | bytes 393224 | tf_op jit(solution)/shard_map/ppermute | solution.py:23
  103.0 11.1 %collective-permute-start.13 = (f32[4,64,128]{2,1,0:T(8,128)S(1)}, f32[4,64,128]{2,1,0:T(8,128)}, u32[]{:S(2)}, u32[]{:S(2)}) collective-permute-start(f32[4,64,128]{2,1,0:T(8,128)S(1)} %get-tuple-element.69), channel_id=1, source_target_pairs={{0,2},{2,4},{4,6},{6,8},{8,10},{10,12},{12,14},{14,16},{16,18},{18... | collective-permute-start | bytes 393224 | tf_op jit(solution)/shard_map/ppermute | solution.py:21
  107.3 29.9 %copy-start.8 = (f32[16,64,128]{2,1,0:T(8,128)}, f32[16,64,128]{2,1,0:T(8,128)S(1)}, u32[]{:S(2)}) copy-start(f32[16,64,128]{2,1,0:T(8,128)S(1)} %scatter-add.45) | copy-start | bytes 1572868
  108.1 29.1 %collective-permute-start.6 = (f32[4,64,128]{2,1,0:T(8,128)}, f32[4,64,128]{2,1,0:T(8,128)S(1)}, u32[]{:S(2)}, u32[]{:S(2)}) collective-permute-start(f32[4,64,128]{2,1,0:T(8,128)} %get-tuple-element.76), channel_id=1, source_target_pairs={{2,0},{4,2},{6,4},{8,6},{10,8},{12,10},{14,12},{16,14},{18,16},{20... | collective-permute-start | bytes 393224 | tf_op jit(solution)/shard_map/ppermute | solution.py:23
  109.4 27.8 %collective-permute-start.7 = (f32[4,64,128]{2,1,0:T(8,128)}, f32[4,64,128]{2,1,0:T(8,128)S(1)}, u32[]{:S(2)}, u32[]{:S(2)}) collective-permute-start(f32[4,64,128]{2,1,0:T(8,128)} %get-tuple-element.77), channel_id=1, source_target_pairs={{0,2},{2,4},{4,6},{6,8},{8,10},{10,12},{12,14},{14,16},{16,18},{18... | collective-permute-start | bytes 393224 | tf_op jit(solution)/shard_map/ppermute | solution.py:21
  137.2 35.5 %copy-start.2 = (f32[16,64,128]{2,1,0:T(8,128)}, f32[16,64,128]{2,1,0:T(8,128)S(1)}, u32[]{:S(2)}) copy-start(f32[16,64,128]{2,1,0:T(8,128)S(1)} %scatter_fusion.2) | copy-start | bytes 1572868
  146.5 3.9 copy-start.9
  149.1 13.1 %collective-permute-start.14 = (f32[4,64,128]{2,1,0:T(8,128)S(1)}, f32[4,64,128]{2,1,0:T(8,128)S(1)}, u32[]{:S(2)}, u32[]{:S(2)}) collective-permute-start(f32[4,64,128]{2,1,0:T(8,128)S(1)} %get-tuple-element.65), channel_id=1, source_target_pairs={{2,0},{4,2},{6,4},{8,6},{10,8},{12,10},{14,12},{16,14},{18,16},{20... | collective-permute-start | bytes 393224 | tf_op jit(solution)/shard_map/ppermute | solution.py:23
  150.4 11.8 %collective-permute-start.15 = (f32[4,64,128]{2,1,0:T(8,128)S(1)}, f32[4,64,128]{2,1,0:T(8,128)S(1)}, u32[]{:S(2)}, u32[]{:S(2)}) collective-permute-start(f32[4,64,128]{2,1,0:T(8,128)S(1)} %get-tuple-element.66), channel_id=1, source_target_pairs={{0,2},{2,4},{4,6},{6,8},{8,10},{10,12},{12,14},{14,16},{16,18},{18... | collective-permute-start | bytes 393224 | tf_op jit(solution)/shard_map/ppermute | solution.py:21
  155.7 51.6 %copy-start.7 = (f32[16,64,128]{2,1,0:T(8,128)}, f32[16,64,128]{2,1,0:T(8,128)S(1)}, u32[]{:S(2)}) copy-start(f32[16,64,128]{2,1,0:T(8,128)S(1)} %scatter-add.46) | copy-start | bytes 1572868
  155.7 51.5 %collective-permute-start.8 = (f32[4,64,128]{2,1,0:T(8,128)S(1)}, f32[4,64,128]{2,1,0:T(8,128)S(1)}, u32[]{:S(2)}, u32[]{:S(2)}) collective-permute-start(f32[4,64,128]{2,1,0:T(8,128)S(1)} %get-tuple-element.74), channel_id=1, source_target_pairs={{2,0},{4,2},{6,4},{8,6},{10,8},{12,10},{14,12},{16,14},{18,16},{20... | collective-permute-start | bytes 393224 | tf_op jit(solution)/shard_map/ppermute | solution.py:23
  157.0 50.2 %collective-permute-start.9 = (f32[4,64,128]{2,1,0:T(8,128)S(1)}, f32[4,64,128]{2,1,0:T(8,128)S(1)}, u32[]{:S(2)}, u32[]{:S(2)}) collective-permute-start(f32[4,64,128]{2,1,0:T(8,128)S(1)} %get-tuple-element.75), channel_id=1, source_target_pairs={{0,2},{2,4},{4,6},{6,8},{8,10},{10,12},{12,14},{14,16},{16,18},{18... | collective-permute-start | bytes 393224 | tf_op jit(solution)/shard_map/ppermute | solution.py:21
  207.2 10.2 %copy-start = (f32[2,5,16,32,128]{4,3,2,1,0:T(8,128)S(1)}, f32[2,5,16,32,128]{4,3,2,1,0:T(8,128)}, u32[]{:S(2)}) copy-start(f32[2,5,16,32,128]{4,3,2,1,0:T(8,128)} %param.25) | copy-start | bytes 7864324
  239.4 170.1 %copy-start.12 = (f32[16,32,128]{2,1,0:T(8,128)}, f32[16,32,128]{2,1,0:T(8,128)S(1)}, u32[]{:S(2)}) copy-start(f32[16,32,128]{2,1,0:T(8,128)S(1)} %get-tuple-element.102) | copy-start | bytes 786436
  410.3 257.9 %copy-start.4 = (f32[16,64,128]{2,1,0:T(8,128)S(1)}, f32[16,64,128]{2,1,0:T(8,128)}, u32[]{:S(2)}) copy-start(f32[16,64,128]{2,1,0:T(8,128)} %param.16) | copy-start | bytes 1572868
Sparse Core Ops, SparseCore 0:
  217.6 20.2 reduce-scatter.1
where the time goes:
time: 688 us; the launch traced here: 685 us
  blocking collectives  413 us (60%)
  other arithmetic  159 us (23%)
  starting transfers between devices  46.9 us (7%)
  between operations  36.7 us (5%)
  waiting for transfers between devices  20.2 us (3%)
  local copies, waits for them, and re-layouts  9.24 us (1%)
    psum x5, blocking collectives, per_device(): lax.psum(jnp.sum(changes[number] * scaled), ('depth', 'shot'))  203 us
    psum x4, blocking collectives, per_device(): lax.psum(jnp.sum(displaced[number] * search), ('depth', 'shot'))  162 us
    scatter-add x4, other arithmetic, inject(): volume.at[row_safe, remainder // volume.shape[2], remainder % volume.shap...  88.9 us
    psum x1, blocking collectives, per_device(): lax.psum((pair_dots, last_square), ('depth', 'shot'))  39.5 us
    ppermute x8, starting transfers between devices, with_halo(): lax.ppermute(tail, axis, [(i, (i + 1) % count) for i in range(ends)])  36.4 us
    add x4, other arithmetic, per_device(): adjoint_new = 2.0 * adjoint_now - adjoint_old + laplace_core(extended)  29.1 us
    reduce_scatter x1, waiting for transfers between devices, per_device(): lax.psum_scatter(summed, 'shot', scatter_dimension=1, tiled=True)  20.1 us
    add x3, other arithmetic, per_device(): wave_new = 2.0 * wave_now - wave_old + courant * laplacian  16.8 us
  transfers between devices with their start and end apart: 17, of which 1 were waited for; matrix products, arithmetic and copies ran while one was open for 18% of the time, Pallas kernels for 0%

commit v1 on v0

v1 whole, which is shorter than its diff:
```python
import functools

import jax
import jax.numpy as jnp
from jax import lax
from jax.experimental import pallas as pl
from jax.experimental.pallas import tpu as pltpu
from jax.sharding import PartitionSpec as P

STEPS = 4
PAIRS = 5
REACH = 4
PAD = 8
CHUNK = 16
coefficients = (-205.0 / 72.0, 8.0 / 5.0, -1.0 / 5.0, 8.0 / 315.0, -1.0 / 560.0)

F32 = jnp.float32
VM = pl.BlockSpec(memory_space=pltpu.VMEM)
SM = pl.BlockSpec(memory_space=pltpu.SMEM)
PARAMS = pltpu.CompilerParams(vmem_limit_bytes=16 << 20)


def shape(*dims):
    return jax.ShapeDtypeStruct(dims, F32)


def natural_row(row, rows, odd):
    return jnp.where(odd == 1, rows - 1 - row, row)


def odd_depth():
    return lax.rem(lax.axis_index("depth"), 2)


def lane_ids(width):
    return lax.broadcasted_iota(jnp.int32, (1, width), 1)


def laplace_chunk(ref, row, start, size):
    rows, width = ref.shape[0], ref.shape[2]
    core = ref[row, PAD + start : PAD + start + size, :]
    lane = lax.broadcasted_iota(jnp.int32, (size, width), 1)
    total = (3.0 * coefficients[0]) * core
    for reach in range(1, REACH + 1):
        near = (
            ref[row, PAD + start + reach : PAD + start + reach + size, :]
            + ref[row, PAD + start - reach : PAD + start - reach + size, :]
        )
        if row - reach >= 0:
            near = near + ref[row - reach, PAD + start : PAD + start + size, :]
        if row + reach < rows:
            near = near + ref[row + reach, PAD + start : PAD + start + size, :]
        near = near + jnp.where(lane >= reach, pltpu.roll(core, reach, 1), 0.0)
        near = near + jnp.where(lane < width - reach, pltpu.roll(core, width - reach, 1), 0.0)
        total = total + coefficients[reach] * near
    return total


def zero_pads(ref):
    rows, padded, width = ref.shape
    for row in range(rows):
        ref[row, :PAD, :] = jnp.zeros((PAD, width), F32)
        ref[row, padded - PAD :, :] = jnp.zeros((PAD, width), F32)


def first_send_kernel(wave, adjoint, courant, out_core, out_chip):
    rows = wave.shape[0]
    odd = odd_depth()
    for row in range(REACH):
        near = natural_row(rows - REACH + row, rows, odd)
        far = natural_row(row, rows, odd)
        out_core[row] = wave[near]
        out_core[REACH + row] = courant[near] * adjoint[near]
        out_chip[row] = wave[far]
        out_chip[REACH + row] = courant[far] * adjoint[far]


def prepare_kernel(wave, wave_old, adjoint, adjoint_old, courant, o_wave, o_wave_old, o_adj, o_adj_old, o_cour, o_prod):
    rows, across, width = wave.shape
    odd = odd_depth()
    zero_pads(o_wave)
    zero_pads(o_wave_old)
    zero_pads(o_prod)
    for row in range(rows):
        src = natural_row(row, rows, odd)
        o_wave[row, PAD : PAD + across, :] = wave[src]
        o_wave_old[row, PAD : PAD + across, :] = wave_old[src]
        o_adj[row] = adjoint[src]
        o_adj_old[row] = adjoint_old[src]
        o_cour[row] = courant[src]
        o_prod[row, PAD : PAD + across, :] = courant[src] * adjoint[src]


def split_cell(cell, rows, across, width):
    depth_row = cell // (across * width) - lax.axis_index("depth") * rows
    rest = cell % (across * width)
    inside = (depth_row >= 0) & (depth_row < rows)
    row = jnp.where(odd_depth() == 1, rows - 1 - depth_row, depth_row)
    return inside, row, rest // width, rest % width


def receiver_kernel(keys, places, residual, out):
    cells = out.shape[1]
    width = out.shape[2]
    count = keys.shape[1]
    hot = (lax.broadcasted_iota(jnp.int32, (cells, count), 0) == keys[...]).astype(jnp.bfloat16)
    lanes = lax.broadcasted_iota(jnp.int32, (width, count), 0) == places[...]
    for moment in range(STEPS):
        value = jnp.where(lanes, residual[moment : moment + 1, :], 0.0)
        high = value.astype(jnp.bfloat16)
        left = value - high.astype(F32)
        middle = left.astype(jnp.bfloat16)
        low = (left - middle.astype(F32)).astype(jnp.bfloat16)
        pieces = [
            lax.dot_general(hot, piece, (((1,), (1,)), ((), ())), preferred_element_type=F32)
            for piece in (low, middle, high)
        ]
        out[moment] = (pieces[0] + pieces[1]) + pieces[2]


def local_kernel(
    moment, cell, wavelet, wave, wave_old, prod, adj, adj_old, courant, injected, o_lap, o_wave, o_adj, o_prod
):
    rows, across, width = adj.shape
    zero_pads(o_wave)
    zero_pads(o_prod)
    for row in range(rows):
        for start in range(0, across, CHUNK):
            part = (row, pl.ds(start, CHUNK), slice(None))
            wide = (row, pl.ds(PAD + start, CHUNK), slice(None))
            lap = laplace_chunk(wave, row, start, CHUNK)
            o_lap[part] = lap
            o_wave[wide] = 2.0 * wave[wide] - wave_old[wide] + courant[part] * lap
            new = 2.0 * adj[part] - adj_old[part] + laplace_chunk(prod, row, start, CHUNK)
            new = new + injected[STEPS - 1 - moment, row * across + start : row * across + start + CHUNK, :]
            o_adj[part] = new
            o_prod[wide] = courant[part] * new
    inside, row, place, lane = split_cell(cell[0], rows, across, width)

    @pl.when(inside)
    def _():
        spot = (row, pl.ds(PAD + place, 1), slice(None))
        o_wave[spot] = o_wave[spot] + jnp.where(lane_ids(width) == lane, wavelet[0, moment], 0.0)


def halo_terms(core_ref, chip_ref, field, rows):
    base = field * REACH
    for place in range(REACH):
        chip_term = core_term = None
        for reach in range(place + 1, REACH + 1):
            one = coefficients[reach] * chip_ref[base + reach - place - 1]
            two = coefficients[reach] * core_ref[base + REACH - reach + place]
            chip_term = one if chip_term is None else chip_term + one
            core_term = two if core_term is None else core_term + two
        yield place, chip_term
        yield rows - 1 - place, core_term


def join_kernel(
    from_core, from_chip, courant, lap, wave, adj, prod, o_lap, o_wave, o_adj, o_prod, to_core, to_chip
):
    rows, across, width = adj.shape
    inner = slice(PAD, PAD + across)

    def send(row, field, value):
        if row < REACH:
            to_chip[field * REACH + row] = value
        else:
            to_core[field * REACH + row - (rows - REACH)] = value

    for row, term in halo_terms(from_core, from_chip, 0, rows):
        o_lap[row] = lap[row] + term
        new = wave[row, inner, :] + courant[row] * term
        o_wave[row, inner, :] = new
        send(row, 0, new)
    for row, term in halo_terms(from_core, from_chip, 1, rows):
        new = adj[row] + term
        o_adj[row] = new
        new = courant[row] * new
        o_prod[row, inner, :] = new
        send(row, 1, new)


def last_local_kernel(
    scale, wave, prod, adj, adj_old, injected, lap1, lap2, lap3, adj4, adj3, o_inner, o_part, o_lap, o_adj
):
    rows, across, width = adj.shape
    for row in range(rows):
        inner = REACH <= row < rows - REACH
        place = row - REACH if inner else (row if row < REACH else row - (rows - 2 * REACH))
        for start in range(0, across, CHUNK):
            part = (row, pl.ds(start, CHUNK), slice(None))
            put = (place, pl.ds(start, CHUNK), slice(None))
            lap = laplace_chunk(wave, row, start, CHUNK)
            new = 2.0 * adj[part] - adj_old[part] + laplace_chunk(prod, row, start, CHUNK)
            new = new + injected[0, row * across + start : row * across + start + CHUNK, :]
            known = adj[part] * lap2[part] + adj3[part] * lap3[part]
            if inner:
                o_inner[put] = scale * (known + adj4[part] * lap + new * lap1[part])
            else:
                o_part[put] = known
                o_lap[put] = lap
                o_adj[put] = new


def last_join_kernel(scale, from_core, from_chip, known, lap, adj, lap1, adj4, o_outer):
    rows = lap1.shape[0]

    def place(row):
        return row if row < REACH else row - (rows - 2 * REACH)

    waves = dict(halo_terms(from_core, from_chip, 0, rows))
    adjs = dict(halo_terms(from_core, from_chip, 1, rows))
    for row in waves:
        at = place(row)
        last_lap = lap[at] + waves[row]
        last_adj = adj[at] + adjs[row]
        o_outer[at] = scale * (known[at] + adj4[row] * last_lap + last_adj * lap1[row])


def fold(value):
    total = value[:8]
    for start in range(8, value.shape[0], 8):
        total = total + value[start : start + 8]
    return total


PRODUCTS = [(0, a, 1, b) for a in range(PAIRS) for b in range(a, PAIRS)] + [
    (1, a, 1, b) for a in range(PAIRS) for b in range(a, PAIRS)
]
SLOT = {key: PRODUCTS.index(key) for key in PRODUCTS}
FIRST_DOT = len(PRODUCTS)


def gram_kernel(history, out):
    pairs, rows, piece = history.shape[1], history.shape[2], history.shape[3]
    width = history.shape[4]
    for group in range(0, len(PRODUCTS), 10):
        members = PRODUCTS[group : group + 10]

        def body(row, sums, members=members):
            new = list(sums)
            for start in range(0, piece, 8):
                part = {}
                for a, i, b, j in members:
                    for key in ((a, i), (b, j)):
                        if key not in part:
                            part[key] = history[key[0], key[1], row, start : start + 8, :]
                for n, (a, i, b, j) in enumerate(members):
                    new[n] = new[n] + part[a, i] * part[b, j]
            return tuple(new)

        sums = lax.fori_loop(0, rows, body, tuple(jnp.zeros((8, width), F32) for _ in members))
        for n in range(len(members)):
            out[group + n] = sums[n]


def gradient_dots(rows_of, grad, pieces, sums):
    rows = pieces[0].shape[2]
    piece = pieces[0].shape[3]
    count = len(pieces)
    odd = odd_depth()
    for place, row in enumerate(rows_of):
        source = natural_row(row, rows, odd)
        for turn, ref in enumerate(pieces):
            offset = lax.rem(lax.axis_index("shot") + turn, count) * piece
            value = grad[place, pl.ds(pl.multiple_of(offset, piece), piece), :]
            for kind in range(2):
                for pair in range(PAIRS):
                    n = kind * PAIRS + pair
                    sums[n] = sums[n] + fold(ref[kind, pair, source] * value)
    return sums


def inner_rows(rows):
    return list(range(REACH, rows - REACH))


def outer_rows(rows):
    return list(range(REACH)) + list(range(rows - REACH, rows))


def inner_dots_kernel(count, grad, *refs):
    pieces, out = refs[:count], refs[count]
    sums = [jnp.zeros((8, grad.shape[2]), F32) for _ in range(2 * PAIRS)]
    sums = gradient_dots(inner_rows(pieces[0].shape[2]), grad, pieces, sums)
    for n in range(2 * PAIRS):
        out[n] = sums[n]


def outer_dots_kernel(count, grad, inner, gram, *refs):
    pieces, out = refs[:count], refs[count]
    sums = [inner[n] for n in range(2 * PAIRS)]
    sums = gradient_dots(outer_rows(pieces[0].shape[2]), grad, pieces, sums)
    lane = lane_ids(out.shape[1])
    line = jnp.zeros((1, out.shape[1]), F32)
    for n in range(FIRST_DOT + 2 * PAIRS):
        value = gram[n] if n < FIRST_DOT else sums[n - FIRST_DOT]
        line = line + jnp.where(lane == n, jnp.sum(value, axis=(0, 1), keepdims=True), 0.0)
    out[...] = jnp.broadcast_to(line, out.shape)


def weights(line):
    lane = lane_ids(line.shape[1])

    def number(n):
        return jnp.sum(jnp.where(lane == n, line, 0.0), axis=(0, 1), keepdims=True)

    values = [number(n) for n in range(FIRST_DOT + 2 * PAIRS)]

    def sy(a, b):
        return values[SLOT[0, a, 1, b]]

    def yy(a, b):
        return values[SLOT[1, min(a, b), 1, max(a, b)]]

    s_grad = values[FIRST_DOT : FIRST_DOT + PAIRS]
    y_grad = values[FIRST_DOT + PAIRS :]
    rho = [1.0 / sy(i, i) for i in range(PAIRS)]
    alpha = [None] * PAIRS
    for i in reversed(range(PAIRS)):
        dot = s_grad[i]
        for j in range(PAIRS - 1, i, -1):
            dot = dot - alpha[j] * sy(i, j)
        alpha[i] = rho[i] * dot
    scale = sy(PAIRS - 1, PAIRS - 1) / yy(PAIRS - 1, PAIRS - 1)
    s_weight = [None] * PAIRS
    for i in range(PAIRS):
        dot = y_grad[i]
        for j in range(PAIRS):
            dot = dot - alpha[j] * yy(i, j)
        dot = scale * dot
        for j in range(i):
            dot = dot + s_weight[j] * sy(j, i)
        s_weight[i] = alpha[i] - rho[i] * dot
    return scale, [-(scale * a) for a in alpha], s_weight


def finish_kernel(count, lines, courant, inner, outer, *refs):
    others = refs[: 2 * (count - 1)]
    pieces = refs[2 * (count - 1) : 2 * (count - 1) + count]
    o_grad, o_direction, o_next = refs[2 * (count - 1) + count :]
    rows, across, width = courant.shape
    piece = across // count
    odd = odd_depth()
    total = lines[0:8]
    for start in range(8, lines.shape[0], 8):
        total = total + lines[start : start + 8]
    scale, y_weight, s_weight = weights(jnp.sum(total, axis=0, keepdims=True))
    wide = [jnp.broadcast_to(v, (8, width)) for v in [scale] + s_weight + y_weight]
    inner_list, outer_list = inner_rows(rows), outer_rows(rows)
    for row in range(rows):
        source = natural_row(row, rows, odd)
        half = 0 if row in inner_list else 1
        place = (inner_list if half == 0 else outer_list).index(row)
        for turn, ref in enumerate(pieces):
            offset = lax.rem(lax.axis_index("shot") + turn, count) * piece
            for start in range(0, piece, 8):
                at = pl.ds(pl.multiple_of(offset + start, 8), 8)
                grad = (inner if half == 0 else outer)[place, at, :]
                for other in range(count - 1):
                    grad = grad + others[2 * other + half][place, at, :]
                move = wide[0] * grad
                for pair in range(PAIRS):
                    move = move + wide[1 + pair] * ref[0, pair, source, start : start + 8, :]
                    move = move + wide[1 + PAIRS + pair] * ref[1, pair, source, start : start + 8, :]
                move = -move
                if turn == 0:
                    o_grad[source, start : start + 8, :] = grad
                    o_direction[source, start : start + 8, :] = move
                o_next[source, at, :] = courant[source, at, :] + 0.05 * move


def call(kernel, name, outs, *args, specs=None, aliases=None, cost=1 << 20):
    return pl.pallas_call(
        kernel,
        name=name,
        out_shape=outs,
        in_specs=specs or [VM] * len(args),
        out_specs=jax.tree.map(lambda _: VM, outs),
        input_output_aliases=aliases or {},
        compiler_params=PARAMS,
        cost_estimate=pl.CostEstimate(flops=cost, bytes_accessed=cost, transcendentals=0),
    )(*args)


def per_device(
    courant,
    wave_before,
    wave_current,
    adjoint_after,
    adjoint_current,
    source_cell,
    wavelet,
    receiver_cell,
    residual,
    history,
):
    rows, across, width = courant.shape
    depths = lax.axis_size("depth")
    shots = lax.axis_size("shot")
    devices = depths * shots
    slab = shape(rows, across, width)
    padded = shape(rows, across + 2 * PAD, width)
    halo = shape(2 * REACH, across, width)
    on_chip = [(i, i ^ 1) for i in range(depths)]
    off_chip = [(i, i + 1 if i % 2 else i - 1) for i in range(1, depths - 1)]

    def exchange(to_core, to_chip):
        return lax.ppermute(to_core, "depth", on_chip), lax.ppermute(to_chip, "depth", off_chip)

    def to_shot(value, turn):
        return lax.ppermute(value, "shot", [((i + turn) % shots, i) for i in range(shots)])

    wave_old, wave = wave_before[0], wave_current[0]
    adj_old, adj = adjoint_after[0], adjoint_current[0]
    to_core, to_chip = call(first_send_kernel, "first_send", [halo, halo], wave, adj, courant)
    halos = exchange(to_core, to_chip)
    pieces = [history] + [to_shot(history, turn) for turn in range(1, shots)]
    wave, wave_old, adj, adj_old, cour, prod = call(
        prepare_kernel,
        "prepare",
        [padded, padded, slab, slab, slab, padded],
        wave,
        wave_old,
        adj,
        adj_old,
        courant,
    )
    inside, row, place, lane = split_cell(receiver_cell, rows, across, width)
    keys = jnp.where(inside, row * across + place, -1)
    injected = call(
        receiver_kernel, "receivers", shape(STEPS, rows * across, width), keys, lane, residual[0]
    )
    gram = call(gram_kernel, "gram", shape(len(PRODUCTS), 8, width), history)

    laps, adjs = [], []
    for moment in range(STEPS - 1):
        lap, new_wave, new_adj, new_prod = call(
            functools.partial(local_kernel, moment),
            f"local_{moment}",
            [slab, padded, slab, padded],
            source_cell,
            wavelet,
            wave,
            wave_old,
            prod,
            adj,
            adj_old,
            cour,
            injected,
            specs=[SM, SM] + [VM] * 7,
        )
        lap, new_wave, new_adj, new_prod, to_core, to_chip = call(
            join_kernel,
            f"join_{moment}",
            [slab, padded, slab, padded, halo, halo],
            *halos,
            cour,
            lap,
            new_wave,
            new_adj,
            new_prod,
            aliases={3: 0, 4: 1, 5: 2, 6: 3},
        )
        halos = exchange(to_core, to_chip)
        laps.append(lap)
        adjs.append(new_adj)
        wave_old, wave = wave, new_wave
        adj_old, adj = adj, new_adj
        prod = new_prod

    scale = 1.0 / (shots * STEPS)
    part = shape(rows - 2 * REACH, across, width)
    outer_part = shape(2 * REACH, across, width)
    inner, known, lap, last = call(
        functools.partial(last_local_kernel, scale),
        "last_local",
        [part, outer_part, outer_part, outer_part],
        wave,
        prod,
        adj,
        adj_old,
        injected,
        laps[0],
        laps[1],
        laps[2],
        adjs[0],
        adjs[1],
    )
    inner_others = [to_shot(inner, turn) for turn in range(1, shots)]
    inner_dots = call(
        functools.partial(inner_dots_kernel, shots),
        "inner_dots",
        shape(2 * PAIRS, 8, width),
        inner,
        *pieces,
    )
    outer = call(
        functools.partial(last_join_kernel, scale),
        "last_join",
        outer_part,
        *halos,
        known,
        lap,
        last,
        laps[0],
        adjs[0],
    )
    outer_others = [to_shot(outer, turn) for turn in range(1, shots)]
    line = call(
        functools.partial(outer_dots_kernel, shots),
        "outer_dots",
        shape(devices, 128),
        outer,
        inner_dots,
        gram,
        *pieces,
    )
    lines = lax.all_to_all(line, ("depth", "shot"), 0, 0, tiled=True)
    others = [value for pair in zip(inner_others, outer_others) for value in pair]
    own = shape(rows, across // shots, width)
    return tuple(
        call(
            functools.partial(finish_kernel, shots),
            "finish",
            [own, own, slab],
            lines,
            courant,
            inner,
            outer,
            *others,
            *pieces,
        )
    )


def solution(mesh):
    return jax.shard_map(
        per_device,
        mesh=mesh,
        in_specs=(
            P("depth", None, None),
            P("shot", "depth", None, None),
            P("shot", "depth", None, None),
            P("shot", "depth", None, None),
            P("shot", "depth", None, None),
            P("shot"),
            P("shot", None),
            P("shot", None),
            P("shot", None, None),
            P(None, None, "depth", "shot", None),
        ),
        out_specs=(P("depth", "shot", None), P("depth", "shot", None), P("depth", None, None)),
        check_vma=False,
    )
```

time: 688 us -> 84.3 us (0.12)
  blocking collectives: 413 us -> 0 us
  other arithmetic: 159 us -> 0.72 us
  between operations: 36.7 us -> 1.53 us
  Pallas kernels: 0 us -> 23.6 us
  starting transfers between devices: 46.9 us -> 30.6 us
    psum x10 -> x0, blocking collectives: 405 us -> none  [the longest x5 203 us: per_device(): lax.psum(jnp.sum(changes[number] * scaled), ('depth', 'shot'))]
    scatter-add x4 -> x0, other arithmetic: 88.9 us -> none  [inject(): volume.at[row_safe, remainder // volume.shape[2], remainder % volume.shap...]
    add x9 -> x0, other arithmetic: 56.9 us -> none  [the longest x4 29.1 us: per_device(): adjoint_new = 2.0 * adjoint_now - adjoint_old + laplace_core(extended)]
    pallas_call x0 -> x15, Pallas kernels: none -> 23.6 us  [call(): pl.pallas_call(kernel, name=name, out_shape=outs, in_specs=specs or [VM]...]
    ppermute x16 -> x11, starting transfers between devices: 46.8 us -> 24.2 us  [the longest x4 16.3 us: exchange(): lax.ppermute(to_core, 'depth', on_chip)]
    reduce_scatter x1 -> x0, waiting for transfers between devices: 20.1 us -> none  [per_device(): lax.psum_scatter(summed, 'shot', scatter_dimension=1, tiled=True)]
    ppermute x16 -> x11, waiting for transfers between devices: 0.04 us -> 11.7 us  [the longest x3 11.7 us: to_shot(): lax.ppermute(value, 'shot', [((i + turn) % shots, i) for i in range(shots)])]
    reduce_sum x11 -> x0, other arithmetic: 10.7 us -> none  [the longest x5 6.08 us: per_device(): jnp.sum(changes[number] * scaled)]
  transfers between devices with their start and end apart: 17 -> 12, of which waited for: 1 -> 2; matrix products, arithmetic and copies ran while one was open for 18% -> 1% of each run, Pallas kernels for 0% -> 24%
where the time goes in v1:
time: 84.3 us; the launch traced here: 83.6 us
  starting transfers between devices  30.6 us (36%)
  Pallas kernels  23.6 us (28%)
  waiting for transfers between devices  18.8 us (22%)
  local copies, waits for them, and re-layouts  8.35 us (10%)
  between operations  1.53 us (2%)
    pallas_call x15, Pallas kernels, call(): pl.pallas_call(kernel, name=name, out_shape=outs, in_specs=specs or [VM]...  23.6 us
    ppermute x4, starting transfers between devices, exchange(): lax.ppermute(to_core, 'depth', on_chip)  16.3 us
    ppermute x3, waiting for transfers between devices, to_shot(): lax.ppermute(value, 'shot', [((i + turn) % shots, i) for i in range(shots)])  11.7 us
    unnamed x26, local copies, waits for them, and re-layouts  8.35 us
    all_to_all x1, waiting for transfers between devices, per_device(): lines = lax.all_to_all(line, ('depth', 'shot'), 0, 0, tiled=True)  7.1 us
    all_to_all x1, starting transfers between devices, per_device(): lines = lax.all_to_all(line, ('depth', 'shot'), 0, 0, tiled=True)  6.38 us
    ppermute x3, starting transfers between devices, to_shot(): lax.ppermute(value, 'shot', [((i + turn) % shots, i) for i in range(shots)])  5.12 us
    ppermute x4, starting transfers between devices, exchange(): lax.ppermute(to_chip, 'depth', off_chip)  2.85 us
  transfers between devices with their start and end apart: 12, of which 2 were waited for; matrix products, arithmetic and copies ran while one was open for 1% of the time, Pallas kernels for 24%

profile of v1, /device:TPU:0, one launch (start us, length us, event | category | flops | bytes accessed | tf_op | source)
XLA Modules:
  0.0 83.6 jit_solution(2133666373971080989)
XLA Ops:
  0.6 0.0 copy-start.12
  0.6 3.0 %collective-permute-start.8 = (f32[2,5,16,32,128]{4,3,2,1,0:T(8,128)}, f32[2,5,16,32,128]{4,3,2,1,0:T(8,128)}, u32[]{:S(2)}, u32[]{:S(2)}) collective-permute-start(f32[2,5,16,32,128]{4,3,2,1,0:T(8,128)} %refs_2_.1), channel_id=1, source_target_pairs={{1,0},{0,1},{3,2},{2,3},{5,4},{4,5},{7,6},{6,7},{9,8},{8,9},{11,10... | collective-permute-start | bytes 7864328 | tf_op jit(solution)/shard_map/ppermute | solution.py:413
  3.7 1.0 %copy-done.1 = f32[16,64,128]{2,1,0:T(8,128)S(1)} copy-done((f32[16,64,128]{2,1,0:T(8,128)S(1)}, f32[16,64,128]{2,1,0:T(8,128)}, u32[]{:S(2)}) %copy-start.1) | copy-done | bytes 524312
  4.7 1.0 %copy-done.4 = f32[1,16,64,128]{3,2,1,0:T(8,128)S(1)} copy-done((f32[1,16,64,128]{3,2,1,0:T(8,128)S(1)}, f32[1,16,64,128]{3,2,1,0:T(8,128)}, u32[]{:S(2)}) %copy-start.4) | copy-done | bytes 524312
  5.8 1.0 %copy-done.6 = f32[1,16,64,128]{3,2,1,0:T(8,128)S(1)} copy-done((f32[1,16,64,128]{3,2,1,0:T(8,128)S(1)}, f32[1,16,64,128]{3,2,1,0:T(8,128)}, u32[]{:S(2)}) %copy-start.6) | copy-done | bytes 524312
  6.8 0.0 copy-start.10
  6.9 0.1 collective-permute-start
  6.9 0.7 collective-permute-start.1
  7.6 0.7 and_select_fusion
  9.0 0.0 copy-start.2
  9.0 1.0 %copy-done.2 = f32[16,64,128]{2,1,0:T(8,128)S(1)} copy-done((f32[16,64,128]{2,1,0:T(8,128)S(1)}, f32[16,64,128]{2,1,0:T(8,128)}, u32[]{:S(2)}) %copy-start.2) | copy-done | bytes 524312
  10.0 1.0 %copy-done.5 = f32[1,16,64,128]{3,2,1,0:T(8,128)S(1)} copy-done((f32[1,16,64,128]{3,2,1,0:T(8,128)S(1)}, f32[1,16,64,128]{3,2,1,0:T(8,128)}, u32[]{:S(2)}) %copy-start.5) | copy-done | bytes 524312
  11.1 1.0 %copy-done.7 = f32[1,16,64,128]{3,2,1,0:T(8,128)S(1)} copy-done((f32[1,16,64,128]{3,2,1,0:T(8,128)S(1)}, f32[1,16,64,128]{3,2,1,0:T(8,128)}, u32[]{:S(2)}) %copy-start.7) | copy-done | bytes 524312
  12.1 1.0 %copy-done.8 = f32[1,16,64,128]{3,2,1,0:T(8,128)S(1)} copy-done((f32[1,16,64,128]{3,2,1,0:T(8,128)S(1)}, f32[1,16,64,128]{3,2,1,0:T(8,128)}, u32[]{:S(2)}) %copy-start.8) | copy-done | bytes 524312
  13.2 1.0 %copy-done.9 = f32[1,16,64,128]{3,2,1,0:T(8,128)S(1)} copy-done((f32[1,16,64,128]{3,2,1,0:T(8,128)S(1)}, f32[1,16,64,128]{3,2,1,0:T(8,128)}, u32[]{:S(2)}) %copy-start.9) | copy-done | bytes 524312
  14.2 0.2 prepare.1
  14.5 1.8 %receivers.1.injected = f32[4,1024,128]{2,1,0:T(8,128)S(1)} custom-call(s32[1,256]{1,0:T(1,128)S(1)} %and_select_fusion.3.keys, s32[1,256]{1,0:T(1,128)S(1)} %get-tuple-element.87.places, f32[4,256]{1,0:T(4,128)S(1)} %bitcast.16), custom_call_target="tpu_custom_call" | custom-call | flops 1048576 | bytes 1048576 | tf_op jit(solution)/shard_map/receivers/pallas_call | solution.py:375
  16.3 2.8 %local_0.1 = (f32[16,64,128]{2,1,0:T(8,128)S(1)}, f32[16,80,128]{2,1,0:T(8,128)S(1)}, f32[16,64,128]{2,1,0:T(8,128)S(1)}, f32[16,80,128]{2,1,0:T(8,128)S(1)}) custom-call(s32[1]{0:T(128)S(6)} %copy.38.cell, f32[1,4]{1,0:T(1,128)S(1)} %copy-done.10, f32[16,80,128]{2,1,0:T(8,128)S(1)} %get-tuple-element.48.wave.wave_old, ...), custom_call_target="tpu_custom_call" | custom-call | flops 1048576 | bytes 1048576 | tf_op jit(solution)/shard_map/local_0/pallas_call | solution.py:375
  19.1 0.0 collective-permute-done.from_core
  19.1 0.0 collective-permute-done.1.from_chip
  19.2 0.3 join_0.1
  19.4 2.9 %collective-permute-start.2 = (f32[8,64,128]{2,1,0:T(8,128)S(1)}, f32[8,64,128]{2,1,0:T(8,128)S(1)}, u32[]{:S(2)}, u32[]{:S(2)}) collective-permute-start(f32[8,64,128]{2,1,0:T(8,128)S(1)} %get-tuple-element.57), channel_id=1, source_target_pairs={{0,2},{2,0},{4,6},{6,4},{8,10},{10,8},{12,14},{14,12},{16,18},{18,... | collective-permute-start | bytes 786440 | tf_op jit(solution)/shard_map/ppermute | solution.py:410
  22.3 0.7 collective-permute-start.3
  23.0 2.8 %local_1.1 = (f32[16,64,128]{2,1,0:T(8,128)S(1)}, f32[16,80,128]{2,1,0:T(8,128)S(1)}, f32[16,64,128]{2,1,0:T(8,128)S(1)}, f32[16,80,128]{2,1,0:T(8,128)S(1)}) custom-call(s32[1]{0:T(128)S(6)} %copy.38.cell, f32[1,4]{1,0:T(1,128)S(1)} %copy-done.10, f32[16,80,128]{2,1,0:T(8,128)S(1)} %get-tuple-element.59.wave.wave_old, ...), custom_call_target="tpu_custom_call" | custom-call | flops 1048576 | bytes 1048576 | tf_op jit(solution)/shard_map/local_1/pallas_call | solution.py:375
  25.9 0.0 collective-permute-done.3.from_chip
  25.9 0.3 join_1.1
  26.2 6.2 %collective-permute-start.4 = (f32[8,64,128]{2,1,0:T(8,128)S(1)}, f32[8,64,128]{2,1,0:T(8,128)S(1)}, u32[]{:S(2)}, u32[]{:S(2)}) collective-permute-start(f32[8,64,128]{2,1,0:T(8,128)S(1)} %get-tuple-element.66), channel_id=1, source_target_pairs={{0,2},{2,0},{4,6},{6,4},{8,10},{10,8},{12,14},{14,12},{16,18},{18,... | collective-permute-start | bytes 786440 | tf_op jit(solution)/shard_map/ppermute | solution.py:410
  32.3 0.7 collective-permute-start.5
  33.0 2.8 %local_2.1 = (f32[16,64,128]{2,1,0:T(8,128)S(1)}, f32[16,80,128]{2,1,0:T(8,128)S(1)}, f32[16,64,128]{2,1,0:T(8,128)S(1)}, f32[16,80,128]{2,1,0:T(8,128)S(1)}) custom-call(s32[1]{0:T(128)S(6)} %copy.38.cell, f32[1,4]{1,0:T(1,128)S(1)} %copy-done.10, f32[16,80,128]{2,1,0:T(8,128)S(1)} %get-tuple-element.68.wave, ...), custom_call_target="tpu_custom_call" | custom-call | flops 1048576 | bytes 1048576 | tf_op jit(solution)/shard_map/local_2/pallas_call | solution.py:375
  35.8 0.0 collective-permute-done.4.from_core
  35.8 0.0 collective-permute-done.5.from_chip
  35.8 0.3 join_2.1
  36.1 7.1 %collective-permute-start.6 = (f32[8,64,128]{2,1,0:T(8,128)S(1)}, f32[8,64,128]{2,1,0:T(8,128)S(1)}, u32[]{:S(2)}, u32[]{:S(2)}) collective-permute-start(f32[8,64,128]{2,1,0:T(8,128)S(1)} %get-tuple-element.75), channel_id=1, source_target_pairs={{0,2},{2,0},{4,6},{6,4},{8,10},{10,8},{12,14},{14,12},{16,18},{18,... | collective-permute-start | bytes 786440 | tf_op jit(solution)/shard_map/ppermute | solution.py:410
  43.2 0.8 %collective-permute-start.7 = (f32[8,64,128]{2,1,0:T(8,128)S(1)}, f32[8,64,128]{2,1,0:T(8,128)S(1)}, u32[]{:S(2)}, u32[]{:S(2)}) collective-permute-start(f32[8,64,128]{2,1,0:T(8,128)S(1)} %get-tuple-element.76), channel_id=1, source_target_pairs={{2,4},{4,2},{6,8},{8,6},{10,12},{12,10},{14,16},{16,14},{18,20},{2... | collective-permute-start | bytes 786440 | tf_op jit(solution)/shard_map/ppermute | solution.py:410
  44.1 3.0 %last_local.1 = (f32[8,64,128]{2,1,0:T(8,128)}, f32[8,64,128]{2,1,0:T(8,128)S(1)}, f32[8,64,128]{2,1,0:T(8,128)S(1)}, f32[8,64,128]{2,1,0:T(8,128)S(1)}) custom-call(f32[16,80,128]{2,1,0:T(8,128)S(1)} %get-tuple-element.77.wave, f32[16,80,128]{2,1,0:T(8,128)S(1)} %get-tuple-element.78.prod, f32[16,64,128]{2,1,0:T(8,128)S(1)} %get-tuple-element.79.adj, ...), custom_call_target="tpu_custom_call" | custom-call | flops 1048576 | bytes 1048576 | tf_op jit(solution)/shard_map/last_local/pallas_call | solution.py:375
  47.0 0.5 collective-permute-start.9
  47.5 0.0 collective-permute-done.6.from_core
  47.6 0.2 last_join.1.grad.outer
  47.7 1.6 %collective-permute-start.10 = (f32[8,64,128]{2,1,0:T(8,128)S(1)}, f32[8,64,128]{2,1,0:T(8,128)}, u32[]{:S(2)}, u32[]{:S(2)}) collective-permute-start(f32[8,64,128]{2,1,0:T(8,128)S(1)} %last_join.1.grad.outer), channel_id=1, source_target_pairs={{1,0},{0,1},{3,2},{2,3},{5,4},{4,5},{7,6},{6,7},{9,8},{8,9},{11,10... | collective-permute-start | bytes 786440 | tf_op jit(solution)/shard_map/ppermute | solution.py:413
  49.3 0.7 gram.1
  50.0 11.6 %collective-permute-done.8.refs_1_.refs_3_ = f32[2,5,16,32,128]{4,3,2,1,0:T(8,128)} collective-permute-done((f32[2,5,16,32,128]{4,3,2,1,0:T(8,128)}, f32[2,5,16,32,128]{4,3,2,1,0:T(8,128)}, u32[]{:S(2)}, u32[]{:S(2)}) %collective-permute-start.8) | collective-permute-done | bytes 2621472 | tf_op jit(solution)/shard_map/ppermute | solution.py:413
  61.7 2.0 %inner_dots.1.inner = f32[10,8,128]{2,1,0:T(8,128)S(1)} custom-call(f32[8,64,128]{2,1,0:T(8,128)} %get-tuple-element.86.grad.inner, f32[2,5,16,32,128]{4,3,2,1,0:T(8,128)S(1)} %copy-done, f32[2,5,16,32,128]{4,3,2,1,0:T(8,128)} %collective-permute-done.8.refs_1_.refs_3_), custom_call_target="tpu_custom_call" | custom-call | flops 1048576 | bytes 1048576 | tf_op jit(solution)/shard_map/inner_dots/pallas_call | solution.py:375
  63.7 0.0 copy-start.3
  63.7 2.8 %outer_dots.1 = f32[32,128]{1,0:T(8,128)} custom-call(f32[8,64,128]{2,1,0:T(8,128)S(1)} %last_join.1.grad.outer, f32[10,8,128]{2,1,0:T(8,128)S(1)} %inner_dots.1.inner, f32[30,8,128]{2,1,0:T(8,128)S(1)} %gram.1, f32[2,5,16,32,128]{4,3,2,1,0:T(8,128)S(1)} %copy-done, f32[2,5,16,32,128]{4,3,2,1,0:T(8,128)} %collective-permute-done.8.refs_1_.refs_3_), custom_call_target="tpu_custom_call" | custom-call | flops 1048576 | bytes 1048576 | tf_op jit(solution)/shard_map/outer_dots/pallas_call | solution.py:375
  66.5 6.4 %all-to-all-start = ((f32[32,1,128]{2,1,0:T(1,128)}), f32[32,1,128]{2,1,0:T(1,128)S(1)}, u32[]{:S(2)}, u32[]{:S(2)}) async-start(f32[32,1,128]{2,1,0:T(1,128)} %bitcast.6), calls=%async_computation | async-start | bytes 32768 | tf_op jit(solution)/shard_map/all_to_all | solution.py:520
  72.9 0.0 collective-permute-done.9.refs_0_
  72.9 7.1 %all-to-all-done = f32[32,1,128]{2,1,0:T(1,128)S(1)} async-done(((f32[32,1,128]{2,1,0:T(1,128)}), f32[32,1,128]{2,1,0:T(1,128)S(1)}, u32[]{:S(2)}, u32[]{:S(2)}) %all-to-all-start) | async-done | bytes 16416 | tf_op jit(solution)/shard_map/all_to_all | solution.py:520
  80.0 3.6 %finish.1 = (f32[16,32,128]{2,1,0:T(8,128)}, f32[16,32,128]{2,1,0:T(8,128)}, f32[16,64,128]{2,1,0:T(8,128)}) custom-call(f32[32,128]{1,0:T(8,128)S(1)} %bitcast.15, f32[16,64,128]{2,1,0:T(8,128)S(1)} %copy-done.3, f32[8,64,128]{2,1,0:T(8,128)} %get-tuple-element.86.grad.inner, f32[8,64,128]{2,1,0:T(8,128)S(1)} %last_join.1.grad.outer, ...), custom_call_target="tpu_custom_call" | custom-call | flops 1048576 | bytes 1048576 | tf_op jit(solution)/shard_map/finish/pallas_call | solution.py:375
  (19 shorter events, 0.1 us)
Async XLA Ops:
  0.6 13.8 %copy-start.12 = (s32[1,256]{1,0:T(1,128)S(1)}, s32[1,256]{1,0:T(1,128)}, u32[]{:S(2)}) copy-start(s32[1,256]{1,0:T(1,128)} %param.17) | copy-start | bytes 3076
  0.6 61.0 %collective-permute-start.8 = (f32[2,5,16,32,128]{4,3,2,1,0:T(8,128)}, f32[2,5,16,32,128]{4,3,2,1,0:T(8,128)}, u32[]{:S(2)}, u32[]{:S(2)}) collective-permute-start(f32[2,5,16,32,128]{4,3,2,1,0:T(8,128)} %refs_2_.1), channel_id=1, source_target_pairs={{1,0},{0,1},{3,2},{2,3},{5,4},{4,5},{7,6},{6,7},{9,8},{8,9},{11,10... | collective-permute-start | bytes 7864328 | tf_op jit(solution)/shard_map/ppermute | solution.py:413
  3.7 1.0 %copy-start.1 = (f32[16,64,128]{2,1,0:T(8,128)S(1)}, f32[16,64,128]{2,1,0:T(8,128)}, u32[]{:S(2)}) copy-start(f32[16,64,128]{2,1,0:T(8,128)} %courant.5) | copy-start | bytes 1572868
  4.7 1.0 %copy-start.4 = (f32[1,16,64,128]{3,2,1,0:T(8,128)S(1)}, f32[1,16,64,128]{3,2,1,0:T(8,128)}, u32[]{:S(2)}) copy-start(f32[1,16,64,128]{3,2,1,0:T(8,128)} %param.12) | copy-start | bytes 1572868
  5.8 1.0 %copy-start.6 = (f32[1,16,64,128]{3,2,1,0:T(8,128)S(1)}, f32[1,16,64,128]{3,2,1,0:T(8,128)}, u32[]{:S(2)}) copy-start(f32[1,16,64,128]{3,2,1,0:T(8,128)} %param.14) | copy-start | bytes 1572868
  6.8 7.7 %copy-start.11 = (f32[1,4,256]{2,1,0:T(4,128)S(1)}, f32[1,4,256]{2,1,0:T(4,128)}, u32[]{:S(2)}) copy-start(f32[1,4,256]{2,1,0:T(4,128)} %param.18) | copy-start | bytes 12292
  6.8 9.4 %copy-start.10 = (f32[1,4]{1,0:T(1,128)S(1)}, f32[1,4]{1,0:T(1,128)}, u32[]{:S(2)}) copy-start(f32[1,4]{1,0:T(1,128)} %wavelet.5) | copy-start | bytes 52
  6.9 12.3 %collective-permute-start = (f32[8,64,128]{2,1,0:T(8,128)S(1)}, f32[8,64,128]{2,1,0:T(8,128)S(1)}, u32[]{:S(2)}, u32[]{:S(2)}) collective-permute-start(f32[8,64,128]{2,1,0:T(8,128)S(1)} %get-tuple-element.45), channel_id=1, source_target_pairs={{0,2},{2,0},{4,6},{6,4},{8,10},{10,8},{12,14},{14,12},{16,18},{18,... | collective-permute-start | bytes 786440 | tf_op jit(solution)/shard_map/ppermute | solution.py:410
  6.9 12.2 %collective-permute-start.1 = (f32[8,64,128]{2,1,0:T(8,128)S(1)}, f32[8,64,128]{2,1,0:T(8,128)S(1)}, u32[]{:S(2)}, u32[]{:S(2)}) collective-permute-start(f32[8,64,128]{2,1,0:T(8,128)S(1)} %get-tuple-element.46), channel_id=1, source_target_pairs={{2,4},{4,2},{6,8},{8,6},{10,12},{12,10},{14,16},{16,14},{18,20},{2... | collective-permute-start | bytes 786440 | tf_op jit(solution)/shard_map/ppermute | solution.py:410
  9.0 1.0 %copy-start.2 = (f32[16,64,128]{2,1,0:T(8,128)S(1)}, f32[16,64,128]{2,1,0:T(8,128)}, u32[]{:S(2)}) copy-start(f32[16,64,128]{2,1,0:T(8,128)} %courant.5) | copy-start | bytes 1572868
  10.0 1.0 %copy-start.5 = (f32[1,16,64,128]{3,2,1,0:T(8,128)S(1)}, f32[1,16,64,128]{3,2,1,0:T(8,128)}, u32[]{:S(2)}) copy-start(f32[1,16,64,128]{3,2,1,0:T(8,128)} %param.12) | copy-start | bytes 1572868
  11.1 1.0 %copy-start.7 = (f32[1,16,64,128]{3,2,1,0:T(8,128)S(1)}, f32[1,16,64,128]{3,2,1,0:T(8,128)}, u32[]{:S(2)}) copy-start(f32[1,16,64,128]{3,2,1,0:T(8,128)} %param.14) | copy-start | bytes 1572868
  12.1 1.0 %copy-start.8 = (f32[1,16,64,128]{3,2,1,0:T(8,128)S(1)}, f32[1,16,64,128]{3,2,1,0:T(8,128)}, u32[]{:S(2)}) copy-start(f32[1,16,64,128]{3,2,1,0:T(8,128)} %param.11) | copy-start | bytes 1572868
  13.2 1.0 %copy-start.9 = (f32[1,16,64,128]{3,2,1,0:T(8,128)S(1)}, f32[1,16,64,128]{3,2,1,0:T(8,128)}, u32[]{:S(2)}) copy-start(f32[1,16,64,128]{3,2,1,0:T(8,128)} %param.13) | copy-start | bytes 1572868
  19.4 6.4 %collective-permute-start.2 = (f32[8,64,128]{2,1,0:T(8,128)S(1)}, f32[8,64,128]{2,1,0:T(8,128)S(1)}, u32[]{:S(2)}, u32[]{:S(2)}) collective-permute-start(f32[8,64,128]{2,1,0:T(8,128)S(1)} %get-tuple-element.57), channel_id=1, source_target_pairs={{0,2},{2,0},{4,6},{6,4},{8,10},{10,8},{12,14},{14,12},{16,18},{18,... | collective-permute-start | bytes 786440 | tf_op jit(solution)/shard_map/ppermute | solution.py:410
  22.3 3.5 %collective-permute-start.3 = (f32[8,64,128]{2,1,0:T(8,128)S(1)}, f32[8,64,128]{2,1,0:T(8,128)S(1)}, u32[]{:S(2)}, u32[]{:S(2)}) collective-permute-start(f32[8,64,128]{2,1,0:T(8,128)S(1)} %get-tuple-element.58), channel_id=1, source_target_pairs={{2,4},{4,2},{6,8},{8,6},{10,12},{12,10},{14,16},{16,14},{18,20},{2... | collective-permute-start | bytes 786440 | tf_op jit(solution)/shard_map/ppermute | solution.py:410
  26.2 9.6 %collective-permute-start.4 = (f32[8,64,128]{2,1,0:T(8,128)S(1)}, f32[8,64,128]{2,1,0:T(8,128)S(1)}, u32[]{:S(2)}, u32[]{:S(2)}) collective-permute-start(f32[8,64,128]{2,1,0:T(8,128)S(1)} %get-tuple-element.66), channel_id=1, source_target_pairs={{0,2},{2,0},{4,6},{6,4},{8,10},{10,8},{12,14},{14,12},{16,18},{18,... | collective-permute-start | bytes 786440 | tf_op jit(solution)/shard_map/ppermute | solution.py:410
  32.3 3.5 %collective-permute-start.5 = (f32[8,64,128]{2,1,0:T(8,128)S(1)}, f32[8,64,128]{2,1,0:T(8,128)S(1)}, u32[]{:S(2)}, u32[]{:S(2)}) collective-permute-start(f32[8,64,128]{2,1,0:T(8,128)S(1)} %get-tuple-element.67), channel_id=1, source_target_pairs={{2,4},{4,2},{6,8},{8,6},{10,12},{12,10},{14,16},{16,14},{18,20},{2... | collective-permute-start | bytes 786440 | tf_op jit(solution)/shard_map/ppermute | solution.py:410
  36.1 11.5 %collective-permute-start.6 = (f32[8,64,128]{2,1,0:T(8,128)S(1)}, f32[8,64,128]{2,1,0:T(8,128)S(1)}, u32[]{:S(2)}, u32[]{:S(2)}) collective-permute-start(f32[8,64,128]{2,1,0:T(8,128)S(1)} %get-tuple-element.75), channel_id=1, source_target_pairs={{0,2},{2,0},{4,6},{6,4},{8,10},{10,8},{12,14},{14,12},{16,18},{18,... | collective-permute-start | bytes 786440 | tf_op jit(solution)/shard_map/ppermute | solution.py:410
  43.2 4.4 %collective-permute-start.7 = (f32[8,64,128]{2,1,0:T(8,128)S(1)}, f32[8,64,128]{2,1,0:T(8,128)S(1)}, u32[]{:S(2)}, u32[]{:S(2)}) collective-permute-start(f32[8,64,128]{2,1,0:T(8,128)S(1)} %get-tuple-element.76), channel_id=1, source_target_pairs={{2,4},{4,2},{6,8},{8,6},{10,12},{12,10},{14,16},{16,14},{18,20},{2... | collective-permute-start | bytes 786440 | tf_op jit(solution)/shard_map/ppermute | solution.py:410
  47.0 2.3 %copy-start = (f32[2,5,16,32,128]{4,3,2,1,0:T(8,128)S(1)}, f32[2,5,16,32,128]{4,3,2,1,0:T(8,128)}, u32[]{:S(2)}) copy-start(f32[2,5,16,32,128]{4,3,2,1,0:T(8,128)} %refs_2_.1) | copy-start | bytes 7864324
  47.0 25.9 %collective-permute-start.9 = (f32[8,64,128]{2,1,0:T(8,128)}, f32[8,64,128]{2,1,0:T(8,128)}, u32[]{:S(2)}, u32[]{:S(2)}) collective-permute-start(f32[8,64,128]{2,1,0:T(8,128)} %get-tuple-element.86.grad.inner), channel_id=1, source_target_pairs={{1,0},{0,1},{3,2},{2,3},{5,4},{4,5},{7,6},{6,7},{9,8},{8,9},{11,10... | collective-permute-start | bytes 786440 | tf_op jit(solution)/shard_map/ppermute | solution.py:413
  47.7 25.2 %collective-permute-start.10 = (f32[8,64,128]{2,1,0:T(8,128)S(1)}, f32[8,64,128]{2,1,0:T(8,128)}, u32[]{:S(2)}, u32[]{:S(2)}) collective-permute-start(f32[8,64,128]{2,1,0:T(8,128)S(1)} %last_join.1.grad.outer), channel_id=1, source_target_pairs={{1,0},{0,1},{3,2},{2,3},{5,4},{4,5},{7,6},{6,7},{9,8},{8,9},{11,10... | collective-permute-start | bytes 786440 | tf_op jit(solution)/shard_map/ppermute | solution.py:413
  63.7 16.3 %copy-start.3 = (f32[16,64,128]{2,1,0:T(8,128)S(1)}, f32[16,64,128]{2,1,0:T(8,128)}, u32[]{:S(2)}) copy-start(f32[16,64,128]{2,1,0:T(8,128)} %courant.5) | copy-start | bytes 1572868
  66.5 13.5 %all-to-all-start = ((f32[32,1,128]{2,1,0:T(1,128)}), f32[32,1,128]{2,1,0:T(1,128)S(1)}, u32[]{:S(2)}, u32[]{:S(2)}) async-start(f32[32,1,128]{2,1,0:T(1,128)} %bitcast.6), calls=%async_computation | async-start | bytes 32768 | tf_op jit(solution)/shard_map/all_to_all | solution.py:520

commit v2 on v1

v2 whole, which is shorter than its diff:
```python
import functools

import jax
import jax.numpy as jnp
from jax import lax
from jax.experimental import pallas as pl
from jax.experimental.pallas import tpu as pltpu
from jax.sharding import PartitionSpec as P

STEPS = 4
PAIRS = 5
REACH = 4
PAD = 8
CHUNK = 16
coefficients = (-205.0 / 72.0, 8.0 / 5.0, -1.0 / 5.0, 8.0 / 315.0, -1.0 / 560.0)

F32 = jnp.float32
VM = pl.BlockSpec(memory_space=pltpu.VMEM)
SM = pl.BlockSpec(memory_space=pltpu.SMEM)
HB = pl.BlockSpec(memory_space=pltpu.HBM)
PARAMS = pltpu.CompilerParams(vmem_limit_bytes=16 << 20)


def shape(*dims):
    return jax.ShapeDtypeStruct(dims, F32)


def natural_row(row, rows, odd):
    return jnp.where(odd == 1, rows - 1 - row, row)


def odd_depth():
    return lax.rem(lax.axis_index("depth"), 2)


def lane_ids(width):
    return lax.broadcasted_iota(jnp.int32, (1, width), 1)


def laplace_chunk(ref, row, start, size):
    rows, width = ref.shape[0], ref.shape[2]
    core = ref[row, PAD + start : PAD + start + size, :]
    lane = lax.broadcasted_iota(jnp.int32, (size, width), 1)
    total = (3.0 * coefficients[0]) * core
    for reach in range(1, REACH + 1):
        near = (
            ref[row, PAD + start + reach : PAD + start + reach + size, :]
            + ref[row, PAD + start - reach : PAD + start - reach + size, :]
        )
        if row - reach >= 0:
            near = near + ref[row - reach, PAD + start : PAD + start + size, :]
        if row + reach < rows:
            near = near + ref[row + reach, PAD + start : PAD + start + size, :]
        near = near + jnp.where(lane >= reach, pltpu.roll(core, reach, 1), 0.0)
        near = near + jnp.where(lane < width - reach, pltpu.roll(core, width - reach, 1), 0.0)
        total = total + coefficients[reach] * near
    return total


def zero_pads(ref):
    rows, padded, width = ref.shape
    for row in range(rows):
        ref[row, :PAD, :] = jnp.zeros((PAD, width), F32)
        ref[row, padded - PAD :, :] = jnp.zeros((PAD, width), F32)


def stage_kernel(
    wave,
    wave_old,
    adjoint,
    adjoint_old,
    courant,
    history,
    o_wave,
    o_wave_old,
    o_adj,
    o_adj_old,
    o_cour,
    o_prod,
    to_core,
    to_chip,
    o_history,
    b_wave,
    b_wave_old,
    b_adj,
    b_adj_old,
    b_cour,
    sems,
):
    rows, across, width = courant.shape
    fetched = [(wave, b_wave), (adjoint, b_adj), (courant, b_cour), (wave_old, b_wave_old), (adjoint_old, b_adj_old)]
    copies = [pltpu.make_async_copy(src, dst, sems.at[n]) for n, (src, dst) in enumerate(fetched)]
    for n, (start, at) in enumerate([(0, 0), (rows - REACH, REACH)]):
        src = history.at[:, :, pl.ds(start, REACH)]
        copies.append(pltpu.make_async_copy(src, o_history.at[:, :, pl.ds(at, REACH)], sems.at[len(fetched) + n]))
    for copy in copies:
        copy.start()
    zero_pads(o_wave)
    zero_pads(o_wave_old)
    zero_pads(o_prod)
    odd = odd_depth()
    for copy in copies[:3]:
        copy.wait()
    for row in range(rows):
        src = natural_row(row, rows, odd)
        now, adj, cour = b_wave[src], b_adj[src], b_cour[src]
        prod = cour * adj
        o_wave[row, PAD : PAD + across, :] = now
        o_adj[row] = adj
        o_cour[row] = cour
        o_prod[row, PAD : PAD + across, :] = prod
        if row < REACH:
            to_chip[row] = now
            to_chip[REACH + row] = prod
        if row >= rows - REACH:
            to_core[row - (rows - REACH)] = now
            to_core[row - (rows - REACH) + REACH] = prod
    for copy in copies[3:5]:
        copy.wait()
    for row in range(rows):
        src = natural_row(row, rows, odd)
        o_wave_old[row, PAD : PAD + across, :] = b_wave_old[src]
        o_adj_old[row] = b_adj_old[src]
    for copy in copies[5:]:
        copy.wait()


def split_cell(cell, rows, across, width):
    depth_row = cell // (across * width) - lax.axis_index("depth") * rows
    rest = cell % (across * width)
    inside = (depth_row >= 0) & (depth_row < rows)
    row = jnp.where(odd_depth() == 1, rows - 1 - depth_row, depth_row)
    return inside, row, rest // width, rest % width


def receiver_kernel(across, receivers, residual, out):
    cells = out.shape[1]
    width = out.shape[2]
    count = receivers.shape[1]
    inside, row, place, lane = split_cell(receivers[...], cells // across, across, width)
    keys = jnp.where(inside, row * across + place, -1)
    hot = (lax.broadcasted_iota(jnp.int32, (cells, count), 0) == keys).astype(jnp.bfloat16)
    lanes = lax.broadcasted_iota(jnp.int32, (width, count), 0) == lane
    for moment in range(STEPS):
        value = jnp.where(lanes, residual[moment : moment + 1, :], 0.0)
        high = value.astype(jnp.bfloat16)
        left = value - high.astype(F32)
        middle = left.astype(jnp.bfloat16)
        low = (left - middle.astype(F32)).astype(jnp.bfloat16)
        pieces = [
            lax.dot_general(hot, piece, (((1,), (1,)), ((), ())), preferred_element_type=F32)
            for piece in (low, middle, high)
        ]
        out[moment] = (pieces[0] + pieces[1]) + pieces[2]


def local_kernel(
    moment, cell, wavelet, wave, wave_old, prod, adj, adj_old, courant, injected, o_lap, o_wave, o_adj, o_prod
):
    rows, across, width = adj.shape
    zero_pads(o_wave)
    zero_pads(o_prod)
    for row in range(rows):
        for start in range(0, across, CHUNK):
            part = (row, pl.ds(start, CHUNK), slice(None))
            wide = (row, pl.ds(PAD + start, CHUNK), slice(None))
            lap = laplace_chunk(wave, row, start, CHUNK)
            o_lap[part] = lap
            o_wave[wide] = 2.0 * wave[wide] - wave_old[wide] + courant[part] * lap
            new = 2.0 * adj[part] - adj_old[part] + laplace_chunk(prod, row, start, CHUNK)
            new = new + injected[STEPS - 1 - moment, row * across + start : row * across + start + CHUNK, :]
            o_adj[part] = new
            o_prod[wide] = courant[part] * new
    inside, row, place, lane = split_cell(cell[0], rows, across, width)

    @pl.when(inside)
    def _():
        spot = (row, pl.ds(PAD + place, 1), slice(None))
        o_wave[spot] = o_wave[spot] + jnp.where(lane_ids(width) == lane, wavelet[0, moment], 0.0)


def chip_terms(ref, field):
    for place in range(REACH):
        term = None
        for reach in range(place + 1, REACH + 1):
            one = coefficients[reach] * ref[field * REACH + reach - place - 1]
            term = one if term is None else term + one
        yield place, term


def core_terms(ref, field, rows):
    for place in range(REACH):
        term = None
        for reach in range(place + 1, REACH + 1):
            one = coefficients[reach] * ref[field * REACH + REACH - reach + place]
            term = one if term is None else term + one
        yield rows - 1 - place, term


def join_kernel(chip, halo, courant, lap, wave, adj, prod, o_lap, o_wave, o_adj, o_prod, send):
    rows, across, width = adj.shape
    inner = slice(PAD, PAD + across)
    first = 0 if chip else rows - REACH
    for row, term in chip_terms(halo, 0) if chip else core_terms(halo, 0, rows):
        o_lap[row] = lap[row] + term
        new = wave[row, inner, :] + courant[row] * term
        o_wave[row, inner, :] = new
        send[row - first] = new
    for row, term in chip_terms(halo, 1) if chip else core_terms(halo, 1, rows):
        new = adj[row] + term
        o_adj[row] = new
        new = courant[row] * new
        o_prod[row, inner, :] = new
        send[REACH + row - first] = new


def last_rows(which, wave, prod, adj, adj_old, injected, extra_lap=None, extra_adj=None):
    across = adj.shape[1]
    for place, row in enumerate(which):
        for start in range(0, across, CHUNK):
            part = (row, pl.ds(start, CHUNK), slice(None))
            lap = laplace_chunk(wave, row, start, CHUNK)
            new = 2.0 * adj[part] - adj_old[part] + laplace_chunk(prod, row, start, CHUNK)
            new = new + injected[0, row * across + start : row * across + start + CHUNK, :]
            if extra_lap is not None and row in extra_lap:
                lap = lap + extra_lap[row][start : start + CHUNK]
                new = new + extra_adj[row][start : start + CHUNK]
            yield place, row, start, part, lap, new


def inner_kernel(
    scale, count, wave, prod, adj, adj_old, injected, lap1, lap2, lap3, adj4, adj3, *outs
):
    rows, across, width = adj.shape
    piece = across // count
    which = inner_rows(rows)
    full = outs[count]
    for place, row, start, part, lap, new in last_rows(which, wave, prod, adj, adj_old, injected):
        known = adj[part] * lap2[part] + adj3[part] * lap3[part]
        full[place, start : start + CHUNK, :] = scale * (known + adj4[part] * lap + new * lap1[part])
    for turn in range(count):
        offset = lax.rem(lax.axis_index("shot") + turn, count) * piece
        for place in range(len(which)):
            outs[turn][place] = full[place, pl.ds(pl.multiple_of(offset, 8), piece), :]


def outer_kernel(
    scale, from_core, wave, prod, adj, adj_old, injected, lap1, lap2, lap3, adj4, adj3, o_grad, o_lap, o_adj
):
    rows = adj.shape[0]
    waves = dict(core_terms(from_core, 0, rows))
    adjs = dict(core_terms(from_core, 1, rows))
    which = outer_rows(rows)
    for place, row, start, part, lap, new in last_rows(which, wave, prod, adj, adj_old, injected, waves, adjs):
        put = (place, pl.ds(start, CHUNK), slice(None))
        known = adj[part] * lap2[part] + adj3[part] * lap3[part]
        if row < REACH:
            o_grad[put] = known
            o_lap[put] = lap
            o_adj[put] = new
        else:
            o_grad[put] = scale * (known + adj4[part] * lap + new * lap1[part])


def last_join_kernel(scale, from_chip, grad, lap, adj, lap1, adj4, o_grad):
    waves = dict(chip_terms(from_chip, 0))
    adjs = dict(chip_terms(from_chip, 1))
    for row in range(REACH):
        last_lap = lap[row] + waves[row]
        last_adj = adj[row] + adjs[row]
        o_grad[row] = scale * (grad[row] + adj4[row] * last_lap + last_adj * lap1[row])


def fold(value):
    total = value[:8]
    for start in range(8, value.shape[0], 8):
        total = total + value[start : start + 8]
    return total


PRODUCTS = [(0, a, 1, b) for a in range(PAIRS) for b in range(a, PAIRS)] + [
    (1, a, 1, b) for a in range(PAIRS) for b in range(a, PAIRS)
]
SLOT = {key: PRODUCTS.index(key) for key in PRODUCTS}
FIRST_DOT = len(PRODUCTS)


def gram_kernel(history, out):
    pairs, rows, piece = history.shape[1], history.shape[2], history.shape[3]
    width = history.shape[4]
    for group in range(0, len(PRODUCTS), 10):
        members = PRODUCTS[group : group + 10]

        def body(row, sums, members=members):
            new = list(sums)
            for start in range(0, piece, 8):
                part = {}
                for a, i, b, j in members:
                    for key in ((a, i), (b, j)):
                        if key not in part:
                            part[key] = history[key[0], key[1], row, start : start + 8, :]
                for n, (a, i, b, j) in enumerate(members):
                    new[n] = new[n] + part[a, i] * part[b, j]
            return tuple(new)

        sums = lax.fori_loop(0, rows, body, tuple(jnp.zeros((8, width), F32) for _ in members))
        for n in range(len(members)):
            out[group + n] = sums[n]


def inner_rows(rows):
    return list(range(REACH, rows - REACH))


def outer_rows(rows):
    return list(range(REACH)) + list(range(rows - REACH, rows))


def add_dots(sums, values, history, row):
    for kind in range(2):
        for pair in range(PAIRS):
            n = kind * PAIRS + pair
            sums[n] = sums[n] + fold(history[kind, pair, row] * values)


def outer_dots_kernel(count, grad, *refs):
    pieces, out = refs[:count], refs[count]
    total, piece = grad.shape[0], pieces[0].shape[3]
    odd = odd_depth()
    sums = [jnp.zeros((8, grad.shape[2]), F32) for _ in range(2 * PAIRS)]
    for place in range(total):
        source = natural_row(place, total, odd)
        for turn, ref in enumerate(pieces):
            offset = lax.rem(lax.axis_index("shot") + turn, count) * piece
            values = grad[place, pl.ds(pl.multiple_of(offset, 8), piece), :]
            add_dots(sums, values, ref, source)
    for n in range(2 * PAIRS):
        out[n] = sums[n]


def line_kernel(outer, gram, history, *refs):
    parts, out, o_inner = refs[:-2], refs[-2], refs[-1]
    rows = history.shape[2]
    odd = odd_depth()
    sums = [outer[n] for n in range(2 * PAIRS)]
    for place, row in enumerate(inner_rows(rows)):
        values = parts[0][place]
        for other in parts[1:]:
            values = values + other[place]
        o_inner[place] = values
        add_dots(sums, values, history, natural_row(row, rows, odd))
    lane = lane_ids(out.shape[1])
    line = jnp.zeros((1, out.shape[1]), F32)
    for n in range(FIRST_DOT + 2 * PAIRS):
        value = gram[n] if n < FIRST_DOT else sums[n - FIRST_DOT]
        line = line + jnp.where(lane == n, jnp.sum(value, axis=(0, 1), keepdims=True), 0.0)
    out[...] = jnp.broadcast_to(line, out.shape)


def weights(line):
    lane = lane_ids(line.shape[1])

    def number(n):
        return jnp.sum(jnp.where(lane == n, line, 0.0), axis=(0, 1), keepdims=True)

    values = [number(n) for n in range(FIRST_DOT + 2 * PAIRS)]

    def sy(a, b):
        return values[SLOT[0, a, 1, b]]

    def yy(a, b):
        return values[SLOT[1, min(a, b), 1, max(a, b)]]

    s_grad = values[FIRST_DOT : FIRST_DOT + PAIRS]
    y_grad = values[FIRST_DOT + PAIRS :]
    rho = [1.0 / sy(i, i) for i in range(PAIRS)]
    alpha = [None] * PAIRS
    for i in reversed(range(PAIRS)):
        dot = s_grad[i]
        for j in range(PAIRS - 1, i, -1):
            dot = dot - alpha[j] * sy(i, j)
        alpha[i] = rho[i] * dot
    scale = sy(PAIRS - 1, PAIRS - 1) / yy(PAIRS - 1, PAIRS - 1)
    s_weight = [None] * PAIRS
    for i in range(PAIRS):
        dot = y_grad[i]
        for j in range(PAIRS):
            dot = dot - alpha[j] * yy(i, j)
        dot = scale * dot
        for j in range(i):
            dot = dot + s_weight[j] * sy(j, i)
        s_weight[i] = alpha[i] - rho[i] * dot
    return scale, [-(scale * a) for a in alpha], s_weight


def weights_kernel(lines, inner, history, o_weights, o_move):
    rows = history.shape[2]
    piece, width = inner.shape[1], inner.shape[2]
    odd = odd_depth()
    total = lines[0:8]
    for start in range(8, lines.shape[0], 8):
        total = total + lines[start : start + 8]
    scale, y_weight, s_weight = weights(jnp.sum(total, axis=0, keepdims=True))
    wide = [jnp.broadcast_to(v, (8, width)) for v in [scale] + s_weight + y_weight]
    for n, value in enumerate(wide):
        o_weights[n] = value
    for place, row in enumerate(inner_rows(rows)):
        source = natural_row(row, rows, odd)
        for start in range(0, piece, 8):
            at = slice(start, start + 8)
            o_move[place, at, :] = move_of(wide, inner[place, at, :], history, source, at)


def move_of(wide, grad, history, row, at):
    move = wide[0] * grad
    for pair in range(PAIRS):
        move = move + wide[1 + pair] * history[0, pair, row, at, :]
        move = move + wide[1 + PAIRS + pair] * history[1, pair, row, at, :]
    return -move


def finish_kernel(count, weight, courant, inner, inner_move, outer, *refs):
    others, pieces = refs[: count - 1], refs[count - 1 : 2 * count - 1]
    o_grad, o_direction, o_next = refs[2 * count - 1 :]
    rows, across, width = courant.shape
    piece = across // count
    odd = odd_depth()
    wide = [weight[n] for n in range(1 + 2 * PAIRS)]
    mine = lax.axis_index("shot") * piece
    for place, row in enumerate(inner_rows(rows)):
        source = natural_row(row, rows, odd)
        at = pl.ds(pl.multiple_of(mine, 8), piece)
        o_grad[source] = inner[place]
        o_direction[source] = inner_move[place]
        o_next[source, at, :] = courant[source, at, :] + 0.05 * inner_move[place]
    outer_list = outer_rows(rows)
    for place, row in enumerate(outer_list):
        source = natural_row(row, rows, odd)
        kept = natural_row(place, len(outer_list), odd)
        for turn, ref in enumerate(pieces):
            offset = lax.rem(lax.axis_index("shot") + turn, count) * piece
            for start in range(0, piece, 8):
                at = pl.ds(pl.multiple_of(offset + start, 8), 8)
                grad = outer[place, at, :]
                for other in others:
                    grad = grad + other[place, at, :]
                move = move_of(wide, grad, ref, kept, slice(start, start + 8))
                if turn == 0:
                    o_grad[source, start : start + 8, :] = grad
                    o_direction[source, start : start + 8, :] = move
                o_next[source, at, :] = courant[source, at, :] + 0.05 * move


def last_piece_kernel(count, courant, done, *refs):
    moves, o_next, buffer, sem = refs[: count - 1], refs[-3], refs[-2], refs[-1]
    rows, across, width = courant.shape
    piece = across // count
    odd = odd_depth()
    first = REACH
    copies = []
    for turn in range(1, count):
        offset = pl.multiple_of(lax.rem(lax.axis_index("shot") + turn, count) * piece, 8)
        for place, row in enumerate(inner_rows(rows)):
            source = natural_row(row, rows, odd)
            value = courant[source, pl.ds(offset, piece), :] + 0.05 * moves[turn - 1][place]
            buffer[turn - 1, source - first] = value
        copies.append(
            pltpu.make_async_copy(
                buffer.at[turn - 1],
                o_next.at[pl.ds(first, rows - 2 * REACH), pl.ds(offset, piece)],
                sem.at[turn - 1],
            )
        )
        copies[-1].start()
    for copy in copies:
        copy.wait()


def call(
    kernel, name, outs, *args, specs=None, out_specs=None, aliases=None, scratch=(), cost=1 << 20
):
    return pl.pallas_call(
        kernel,
        name=name,
        out_shape=outs,
        in_specs=specs or [VM] * len(args),
        out_specs=out_specs or jax.tree.map(lambda _: VM, outs),
        input_output_aliases=aliases or {},
        scratch_shapes=list(scratch),
        compiler_params=PARAMS,
        cost_estimate=pl.CostEstimate(flops=cost, bytes_accessed=cost, transcendentals=0),
    )(*args)


def per_device(
    courant,
    wave_before,
    wave_current,
    adjoint_after,
    adjoint_current,
    source_cell,
    wavelet,
    receiver_cell,
    residual,
    history,
):
    rows, across, width = courant.shape
    depths = lax.axis_size("depth")
    shots = lax.axis_size("shot")
    devices = depths * shots
    piece = across // shots
    slab = shape(rows, across, width)
    padded = shape(rows, across + 2 * PAD, width)
    halo = shape(2 * REACH, across, width)
    on_chip = [(i, i ^ 1) for i in range(depths)]
    off_chip = [(i, i + 1 if i % 2 else i - 1) for i in range(1, depths - 1)]

    def swap_core(value):
        return lax.ppermute(value, "depth", on_chip)

    def swap_chip(value):
        return lax.ppermute(value, "depth", off_chip)

    def from_shot(value, turn):
        return lax.ppermute(value, "shot", [((i + turn) % shots, i) for i in range(shots)])

    block = pltpu.VMEM((rows, across, width), F32)
    wave, wave_old, adj, adj_old, cour, prod, to_core, to_chip, kept = call(
        stage_kernel,
        "stage",
        [padded, padded, slab, slab, slab, padded, halo, halo, shape(2, PAIRS, 2 * REACH, piece, width)],
        wave_current[0],
        wave_before[0],
        adjoint_current[0],
        adjoint_after[0],
        courant,
        history,
        specs=[HB] * 6,
        scratch=[block] * 5 + [pltpu.SemaphoreType.DMA((7,))],
    )
    from_chip = swap_chip(to_chip)
    from_core = swap_core(to_core)
    kept = [kept] + [from_shot(kept, turn) for turn in range(1, shots)]
    injected = call(
        functools.partial(receiver_kernel, across),
        "receivers",
        shape(STEPS, rows * across, width),
        receiver_cell,
        residual[0],
    )

    laps, adjs = [], []
    for moment in range(STEPS - 1):
        lap, new_wave, new_adj, new_prod = call(
            functools.partial(local_kernel, moment),
            f"local_{moment}",
            [slab, padded, slab, padded],
            source_cell,
            wavelet,
            wave,
            wave_old,
            prod,
            adj,
            adj_old,
            cour,
            injected,
            specs=[SM, SM] + [VM] * 7,
        )
        sends = []
        for chip, came in ((False, from_core), (True, from_chip)):
            lap, new_wave, new_adj, new_prod, send = call(
                functools.partial(join_kernel, chip),
                f"join_{'chip' if chip else 'core'}_{moment}",
                [slab, padded, slab, padded, halo],
                came,
                cour,
                lap,
                new_wave,
                new_adj,
                new_prod,
                aliases={2: 0, 3: 1, 4: 2, 5: 3},
            )
            sends.append(send)
        from_core = swap_core(sends[0])
        from_chip = swap_chip(sends[1])
        laps.append(lap)
        adjs.append(new_adj)
        wave_old, wave = wave, new_wave
        adj_old, adj = adj, new_adj
        prod = new_prod

    scale = 1.0 / (shots * STEPS)
    inner_count = rows - 2 * REACH
    last = (wave, prod, adj, adj_old, injected, laps[0], laps[1], laps[2], adjs[0], adjs[1])
    mine = shape(inner_count, piece, width)
    inner = call(
        functools.partial(inner_kernel, scale, shots),
        "inner",
        [mine] * shots,
        *last,
        scratch=[pltpu.VMEM((inner_count, across, width), F32)],
    )
    parts = [inner[0]] + [from_shot(inner[shots - turn], turn) for turn in range(1, shots)]
    gram = call(gram_kernel, "gram", shape(len(PRODUCTS), 8, width), history)
    outer_part = shape(2 * REACH, across, width)
    chip_part = shape(REACH, across, width)
    outer, lap, new_adj = call(
        functools.partial(outer_kernel, scale),
        "outer",
        [outer_part, chip_part, chip_part],
        from_core,
        *last,
    )
    outer = call(
        functools.partial(last_join_kernel, scale),
        "last_join",
        outer_part,
        from_chip,
        outer,
        lap,
        new_adj,
        laps[0],
        adjs[0],
        aliases={1: 0},
    )
    others = [from_shot(outer, turn) for turn in range(1, shots)]
    outer_dots = call(
        functools.partial(outer_dots_kernel, shots),
        "outer_dots",
        shape(2 * PAIRS, 8, width),
        outer,
        *kept,
    )
    line, inner_grad = call(
        line_kernel,
        "line",
        [shape(devices, 128), mine],
        outer_dots,
        gram,
        history,
        *parts,
    )
    lines = lax.all_to_all(line, ("depth", "shot"), 0, 0, tiled=True)
    weight, move = call(
        weights_kernel,
        "weights",
        [shape(1 + 2 * PAIRS, 8, width), mine],
        lines,
        inner_grad,
        history,
    )
    moves = [from_shot(move, turn) for turn in range(1, shots)]
    own = shape(rows, piece, width)
    gradient, direction, courant_next = call(
        functools.partial(finish_kernel, shots),
        "finish",
        [own, own, slab],
        weight,
        courant,
        inner_grad,
        move,
        outer,
        *others,
        *kept,
    )
    courant_next = call(
        functools.partial(last_piece_kernel, shots),
        "last_piece",
        slab,
        courant,
        courant_next,
        *moves,
        specs=[VM, HB] + [VM] * (shots - 1),
        out_specs=HB,
        aliases={1: 0},
        scratch=[
            pltpu.VMEM((shots - 1, inner_count, piece, width), F32),
            pltpu.SemaphoreType.DMA((shots - 1,)),
        ],
    )
    return gradient, direction, courant_next


def solution(mesh):
    return jax.shard_map(
        per_device,
        mesh=mesh,
        in_specs=(
            P("depth", None, None),
            P("shot", "depth", None, None),
            P("shot", "depth", None, None),
            P("shot", "depth", None, None),
            P("shot", "depth", None, None),
            P("shot"),
            P("shot", None),
            P("shot", None),
            P("shot", None, None),
            P(None, None, "depth", "shot", None),
        ),
        out_specs=(P("depth", "shot", None), P("depth", "shot", None), P("depth", None, None)),
        check_vma=False,
    )
```

time: 84.3 us -> 70.5 us (0.84)
  blocking collectives: 0 us -> 17.2 us
  waiting for transfers between devices: 18.8 us -> 3.96 us
  starting transfers between devices: 30.6 us -> 22.5 us
  Pallas kernels: 23.6 us -> 17.7 us
  local copies, waits for them, and re-layouts: 8.35 us -> 6.96 us
    all_to_all x0 -> x1, blocking collectives: none -> 17.2 us  [per_device(): lines = lax.all_to_all(line, ('depth', 'shot'), 0, 0, tiled=True)]
    ppermute x11 -> x12, waiting for transfers between devices: 11.7 us -> 3.96 us  [the longest x4 3.94 us: from_shot(): lax.ppermute(value, 'shot', [((i + turn) % shots, i) for i in range(shots)])]
    all_to_all x1 -> x0, waiting for transfers between devices: 7.1 us -> none  [per_device(): lines = lax.all_to_all(line, ('depth', 'shot'), 0, 0, tiled=True)]
    all_to_all x1 -> x0, starting transfers between devices: 6.38 us -> none  [per_device(): lines = lax.all_to_all(line, ('depth', 'shot'), 0, 0, tiled=True)]
    pallas_call x15 -> x20, Pallas kernels: 23.6 us -> 17.7 us  [call(): pl.pallas_call(kernel, name=name, out_shape=outs, in_specs=specs or [VM]...]
    ppermute x11 -> x12, starting transfers between devices: 24.2 us -> 22.5 us  [the longest x4 13.9 us: swap_core(): return lax.ppermute(value, 'depth', on_chip)]
    unnamed x26 -> x22, local copies, waits for them, and re-layouts: 8.35 us -> 6.96 us
  transfers between devices with their start and end apart: 12 -> 12, of which waited for: 2 -> 2; matrix products, arithmetic and copies ran while one was open for 1% -> 0% of each run, Pallas kernels for 24% -> 23%
where the time goes in v2:
time: 70.5 us; the launch traced here: 70 us
  starting transfers between devices  22.5 us (32%)
  Pallas kernels  17.7 us (25%)
  blocking collectives  17.2 us (24%)
  local copies, waits for them, and re-layouts  6.96 us (10%)
  waiting for transfers between devices  3.96 us (6%)
  between operations  1.65 us (2%)
    pallas_call x20, Pallas kernels, call(): pl.pallas_call(kernel, name=name, out_shape=outs, in_specs=specs or [VM]...  17.7 us
    all_to_all x1, blocking collectives, per_device(): lines = lax.all_to_all(line, ('depth', 'shot'), 0, 0, tiled=True)  17.2 us
    ppermute x4, starting transfers between devices, swap_core(): return lax.ppermute(value, 'depth', on_chip)  13.9 us
    unnamed x22, local copies, waits for them, and re-layouts  6.96 us
    ppermute x4, starting transfers between devices, from_shot(): lax.ppermute(value, 'shot', [((i + turn) % shots, i) for i in range(shots)])  5.76 us
    ppermute x4, waiting for transfers between devices, from_shot(): lax.ppermute(value, 'shot', [((i + turn) % shots, i) for i in range(shots)])  3.94 us
    ppermute x4, starting transfers between devices, swap_chip(): return lax.ppermute(value, 'depth', off_chip)  2.88 us
  transfers between devices with their start and end apart: 12, of which 2 were waited for; matrix products, arithmetic and copies ran while one was open for 0% of the time, Pallas kernels for 23%

profile of v2, /device:TPU:0, one launch (start us, length us, event | category | flops | bytes accessed | tf_op | source)
XLA Modules:
  0.0 70.0 jit_solution(271105494274431110)
XLA Ops:
  0.6 0.0 copy-start
  0.6 1.7 %copy-done = f32[2,5,16,32,128]{4,3,2,1,0:T(8,128)S(1)} copy-done((f32[2,5,16,32,128]{4,3,2,1,0:T(8,128)S(1)}, f32[2,5,16,32,128]{4,3,2,1,0:T(8,128)}, u32[]{:S(2)}) %copy-start) | copy-done | bytes 2621464
  2.4 1.0 %copy-done.2 = f32[16,64,128]{2,1,0:T(8,128)S(1)} copy-done((f32[16,64,128]{2,1,0:T(8,128)S(1)}, f32[16,64,128]{2,1,0:T(8,128)}, u32[]{:S(2)}) %copy-start.2) | copy-done | bytes 524312
  3.4 1.0 %copy-done.4 = f32[1,16,64,128]{3,2,1,0:T(8,128)S(1)} copy-done((f32[1,16,64,128]{3,2,1,0:T(8,128)S(1)}, f32[1,16,64,128]{3,2,1,0:T(8,128)}, u32[]{:S(2)}) %copy-start.4) | copy-done | bytes 524312
  4.5 1.0 %copy-done.5 = f32[1,16,64,128]{3,2,1,0:T(8,128)S(1)} copy-done((f32[1,16,64,128]{3,2,1,0:T(8,128)S(1)}, f32[1,16,64,128]{3,2,1,0:T(8,128)}, u32[]{:S(2)}) %copy-start.5) | copy-done | bytes 524312
  5.5 1.0 %copy-done.6 = f32[1,16,64,128]{3,2,1,0:T(8,128)S(1)} copy-done((f32[1,16,64,128]{3,2,1,0:T(8,128)S(1)}, f32[1,16,64,128]{3,2,1,0:T(8,128)}, u32[]{:S(2)}) %copy-start.6) | copy-done | bytes 524312
  6.5 1.0 %copy-done.7 = f32[1,16,64,128]{3,2,1,0:T(8,128)S(1)} copy-done((f32[1,16,64,128]{3,2,1,0:T(8,128)S(1)}, f32[1,16,64,128]{3,2,1,0:T(8,128)}, u32[]{:S(2)}) %copy-start.7) | copy-done | bytes 524312
  7.6 0.6 stage.1
  8.2 0.0 copy-start.8
  8.2 3.0 %collective-permute-start.8 = (f32[2,5,8,32,128]{4,3,2,1,0:T(8,128)S(1)}, f32[2,5,8,32,128]{4,3,2,1,0:T(8,128)S(1)}, u32[]{:S(2)}, u32[]{:S(2)}) collective-permute-start(f32[2,5,8,32,128]{4,3,2,1,0:T(8,128)S(1)} %get-tuple-element.119.refs_0_.refs_1_), channel_id=1, source_target_pairs={{1,0},{0,1},{3,2},{2,3},{5,4},{4,5},{7,6},{6,7},{9,8},{8,9},{11,10... | collective-permute-start | bytes 3932168 | tf_op jit(solution)/shard_map/ppermute | solution.py:525
  11.2 0.0 collective-permute-start.1
  11.2 0.7 collective-permute-start
  12.6 1.8 %receivers.2.injected = f32[4,1024,128]{2,1,0:T(8,128)S(1)} custom-call(s32[1,256]{1,0:T(1,128)S(1)} %copy-done.10, f32[4,256]{1,0:T(4,128)S(1)} %bitcast.15), custom_call_target="tpu_custom_call" | custom-call | flops 1048576 | bytes 1048576 | tf_op jit(solution)/shard_map/receivers/pallas_call | solution.py:482
  14.4 2.8 %local_0.1 = (f32[16,64,128]{2,1,0:T(8,128)S(1)}, f32[16,80,128]{2,1,0:T(8,128)S(1)}, f32[16,64,128]{2,1,0:T(8,128)S(1)}, f32[16,80,128]{2,1,0:T(8,128)S(1)}) custom-call(s32[1]{0:T(128)S(6)} %copy.66.cell, f32[1,4]{1,0:T(1,128)S(1)} %copy-done.8, f32[16,80,128]{2,1,0:T(8,128)S(1)} %get-tuple-element.69.wave.wave_old, ...), custom_call_target="tpu_custom_call" | custom-call | flops 1048576 | bytes 1048576 | tf_op jit(solution)/shard_map/local_0/pallas_call | solution.py:482
  17.2 0.0 collective-permute-done.1.halo
  17.3 0.1 join_core_0.1
  17.4 2.9 %collective-permute-start.3 = (f32[8,64,128]{2,1,0:T(8,128)S(1)}, f32[8,64,128]{2,1,0:T(8,128)S(1)}, u32[]{:S(2)}, u32[]{:S(2)}) collective-permute-start(f32[8,64,128]{2,1,0:T(8,128)S(1)} %get-tuple-element.83), channel_id=1, source_target_pairs={{0,2},{2,0},{4,6},{6,4},{8,10},{10,8},{12,14},{14,12},{16,18},{18,... | collective-permute-start | bytes 786440 | tf_op jit(solution)/shard_map/ppermute | solution.py:519
  20.3 0.0 collective-permute-done.halo
  20.3 0.1 join_chip_0.1
  20.4 0.7 collective-permute-start.2
  21.1 2.8 %local_1.1 = (f32[16,64,128]{2,1,0:T(8,128)S(1)}, f32[16,80,128]{2,1,0:T(8,128)S(1)}, f32[16,64,128]{2,1,0:T(8,128)S(1)}, f32[16,80,128]{2,1,0:T(8,128)S(1)}) custom-call(s32[1]{0:T(128)S(6)} %copy.66.cell, f32[1,4]{1,0:T(1,128)S(1)} %copy-done.8, f32[16,80,128]{2,1,0:T(8,128)S(1)} %get-tuple-element.84.wave.wave_old, ...), custom_call_target="tpu_custom_call" | custom-call | flops 1048576 | bytes 1048576 | tf_op jit(solution)/shard_map/local_1/pallas_call | solution.py:482
  23.9 0.1 join_core_1.1
  24.1 4.3 %collective-permute-start.5 = (f32[8,64,128]{2,1,0:T(8,128)S(1)}, f32[8,64,128]{2,1,0:T(8,128)S(1)}, u32[]{:S(2)}, u32[]{:S(2)}) collective-permute-start(f32[8,64,128]{2,1,0:T(8,128)S(1)} %get-tuple-element.96), channel_id=1, source_target_pairs={{0,2},{2,0},{4,6},{6,4},{8,10},{10,8},{12,14},{14,12},{16,18},{18,... | collective-permute-start | bytes 786440 | tf_op jit(solution)/shard_map/ppermute | solution.py:519
  28.4 0.1 join_chip_1.1
  28.6 0.7 collective-permute-start.4
  29.3 2.8 %local_2.1 = (f32[16,64,128]{2,1,0:T(8,128)S(1)}, f32[16,80,128]{2,1,0:T(8,128)S(1)}, f32[16,64,128]{2,1,0:T(8,128)S(1)}, f32[16,80,128]{2,1,0:T(8,128)S(1)}) custom-call(s32[1]{0:T(128)S(6)} %copy.66.cell, f32[1,4]{1,0:T(1,128)S(1)} %copy-done.8, f32[16,80,128]{2,1,0:T(8,128)S(1)} %get-tuple-element.97.wave, ...), custom_call_target="tpu_custom_call" | custom-call | flops 1048576 | bytes 1048576 | tf_op jit(solution)/shard_map/local_2/pallas_call | solution.py:482
  32.1 0.0 collective-permute-done.5.halo
  32.1 0.1 join_core_2.1
  32.2 6.6 %collective-permute-start.7 = (f32[8,64,128]{2,1,0:T(8,128)S(1)}, f32[8,64,128]{2,1,0:T(8,128)S(1)}, u32[]{:S(2)}, u32[]{:S(2)}) collective-permute-start(f32[8,64,128]{2,1,0:T(8,128)S(1)} %get-tuple-element.109), channel_id=1, source_target_pairs={{0,2},{2,0},{4,6},{6,4},{8,10},{10,8},{12,14},{14,12},{16,18},{18,... | collective-permute-start | bytes 786440 | tf_op jit(solution)/shard_map/ppermute | solution.py:519
  38.8 0.1 join_chip_2.1
  39.0 0.9 %collective-permute-start.6 = (f32[8,64,128]{2,1,0:T(8,128)S(1)}, f32[8,64,128]{2,1,0:T(8,128)S(1)}, u32[]{:S(2)}, u32[]{:S(2)}) collective-permute-start(f32[8,64,128]{2,1,0:T(8,128)S(1)} %get-tuple-element.108), channel_id=1, source_target_pairs={{2,4},{4,2},{6,8},{8,6},{10,12},{12,10},{14,16},{16,14},{18,20},{2... | collective-permute-start | bytes 786440 | tf_op jit(solution)/shard_map/ppermute | solution.py:522
  39.8 1.2 %inner.1 = (f32[8,32,128]{2,1,0:T(8,128)S(1)}, f32[8,32,128]{2,1,0:T(8,128)S(1)}) custom-call(f32[16,80,128]{2,1,0:T(8,128)S(1)} %get-tuple-element.110.wave, f32[16,80,128]{2,1,0:T(8,128)S(1)} %get-tuple-element.111.prod, f32[16,64,128]{2,1,0:T(8,128)S(1)} %get-tuple-element.112.adj, f32[16,64,128]{2,1,0:T(8,128)S(1)} %get-tuple-element.99.adj.adj_old.adj3, ...), custom_call_target="tpu_custom_call" | custom-call | flops 1048576 | bytes 1048576 | tf_op jit(solution)/shard_map/inner/pallas_call | solution.py:482
  41.1 0.6 collective-permute-start.9
  41.7 0.0 collective-permute-done.7.from_core
  41.7 1.2 %outer.1 = (f32[8,64,128]{2,1,0:T(8,128)S(1)}, f32[4,64,128]{2,1,0:T(8,128)S(1)}, f32[4,64,128]{2,1,0:T(8,128)S(1)}) custom-call(f32[8,64,128]{2,1,0:T(8,128)S(1)} %collective-permute-done.7.from_core, f32[16,80,128]{2,1,0:T(8,128)S(1)} %get-tuple-element.110.wave, f32[16,80,128]{2,1,0:T(8,128)S(1)} %get-tuple-element.111.prod, ...), custom_call_target="tpu_custom_call" | custom-call | flops 1048576 | bytes 1048576 | tf_op jit(solution)/shard_map/outer/pallas_call | solution.py:482
  42.9 0.1 last_join.1.grad.outer
  43.0 1.6 %collective-permute-start.10 = (f32[8,64,128]{2,1,0:T(8,128)S(1)}, f32[8,64,128]{2,1,0:T(8,128)S(1)}, u32[]{:S(2)}, u32[]{:S(2)}) collective-permute-start(f32[8,64,128]{2,1,0:T(8,128)S(1)} %last_join.1.grad.outer), channel_id=1, source_target_pairs={{1,0},{0,1},{3,2},{2,3},{5,4},{4,5},{7,6},{6,7},{9,8},{8,9},{11,10... | collective-permute-start | bytes 786440 | tf_op jit(solution)/shard_map/ppermute | solution.py:525
  44.6 0.7 %gram.1 = f32[30,8,128]{2,1,0:T(8,128)S(1)} custom-call(f32[2,5,16,32,128]{4,3,2,1,0:T(8,128)S(1)} %copy-done.1), custom_call_target="tpu_custom_call" | custom-call | flops 1048576 | bytes 1048576 | tf_op jit(solution)/shard_map/gram/pallas_call | solution.py:482
  45.3 0.3 outer_dots.1.outer
  45.6 0.5 collective-permute-done.9.refs_1_
  46.1 0.2 line.1
  46.4 0.0 copy-start.3
  46.4 17.2 %all_to_all.11 = f32[32,1,128]{2,1,0:T(1,128)S(1)} all-to-all(f32[32,1,128]{2,1,0:T(1,128)S(1)} %bitcast.14), channel_id=1, replica_groups=mesh['depth'=16,'shot'=2] {'depth','shot'}, dimensions={0} | all-to-all | bytes 32768 | tf_op jit(solution)/shard_map/all_to_all | solution.py:643
  63.6 0.3 weights.1
  63.9 0.6 collective-permute-start.11
  64.5 1.3 %finish.1 = (f32[16,32,128]{2,1,0:T(8,128)}, f32[16,32,128]{2,1,0:T(8,128)}, f32[16,64,128]{2,1,0:T(8,128)}) custom-call(f32[11,8,128]{2,1,0:T(8,128)S(1)} %get-tuple-element.124.weight, f32[16,64,128]{2,1,0:T(8,128)S(1)} %copy-done.3, f32[8,32,128]{2,1,0:T(8,128)S(1)} %get-tuple-element.123.inner, f32[8,32,128]{2,1,0:T(8,128)S(1)} %get-tuple-element.125.inner_move, ...), custom_call_target="tpu_custom_call" | custom-call | flops 1048576 | bytes 1048576 | tf_op jit(solution)/shard_map/finish/pallas_call | solution.py:482
  65.8 3.4 %collective-permute-done.11.refs_0_ = f32[8,32,128]{2,1,0:T(8,128)S(1)} collective-permute-done((f32[8,32,128]{2,1,0:T(8,128)S(1)}, f32[8,32,128]{2,1,0:T(8,128)S(1)}, u32[]{:S(2)}, u32[]{:S(2)}) %collective-permute-start.11) | collective-permute-done | bytes 131104 | tf_op jit(solution)/shard_map/ppermute | solution.py:525
  69.2 0.7 last_piece.1
  (19 shorter events, 0.0 us)
Async XLA Ops:
  0.6 1.7 %copy-start = (f32[2,5,16,32,128]{4,3,2,1,0:T(8,128)S(1)}, f32[2,5,16,32,128]{4,3,2,1,0:T(8,128)}, u32[]{:S(2)}) copy-start(f32[2,5,16,32,128]{4,3,2,1,0:T(8,128)} %history.7) | copy-start | bytes 7864324
  2.4 1.0 %copy-start.2 = (f32[16,64,128]{2,1,0:T(8,128)S(1)}, f32[16,64,128]{2,1,0:T(8,128)}, u32[]{:S(2)}) copy-start(f32[16,64,128]{2,1,0:T(8,128)} %courant.5) | copy-start | bytes 1572868
  3.4 1.0 %copy-start.4 = (f32[1,16,64,128]{3,2,1,0:T(8,128)S(1)}, f32[1,16,64,128]{3,2,1,0:T(8,128)}, u32[]{:S(2)}) copy-start(f32[1,16,64,128]{3,2,1,0:T(8,128)} %param.12) | copy-start | bytes 1572868
  4.5 1.0 %copy-start.5 = (f32[1,16,64,128]{3,2,1,0:T(8,128)S(1)}, f32[1,16,64,128]{3,2,1,0:T(8,128)}, u32[]{:S(2)}) copy-start(f32[1,16,64,128]{3,2,1,0:T(8,128)} %param.11) | copy-start | bytes 1572868
  5.5 1.0 %copy-start.6 = (f32[1,16,64,128]{3,2,1,0:T(8,128)S(1)}, f32[1,16,64,128]{3,2,1,0:T(8,128)}, u32[]{:S(2)}) copy-start(f32[1,16,64,128]{3,2,1,0:T(8,128)} %param.14) | copy-start | bytes 1572868
  6.5 1.0 %copy-start.7 = (f32[1,16,64,128]{3,2,1,0:T(8,128)S(1)}, f32[1,16,64,128]{3,2,1,0:T(8,128)}, u32[]{:S(2)}) copy-start(f32[1,16,64,128]{3,2,1,0:T(8,128)} %param.13) | copy-start | bytes 1572868
  7.6 5.0 %copy-start.9 = (f32[1,4,256]{2,1,0:T(4,128)S(1)}, f32[1,4,256]{2,1,0:T(4,128)}, u32[]{:S(2)}) copy-start(f32[1,4,256]{2,1,0:T(4,128)} %param.18) | copy-start | bytes 12292
  7.6 5.0 %copy-start.10 = (s32[1,256]{1,0:T(1,128)S(1)}, s32[1,256]{1,0:T(1,128)}, u32[]{:S(2)}) copy-start(s32[1,256]{1,0:T(1,128)} %receivers.3) | copy-start | bytes 3076
  8.2 6.2 %copy-start.8 = (f32[1,4]{1,0:T(1,128)S(1)}, f32[1,4]{1,0:T(1,128)}, u32[]{:S(2)}) copy-start(f32[1,4]{1,0:T(1,128)} %wavelet.5) | copy-start | bytes 52
  8.2 37.1 %collective-permute-start.8 = (f32[2,5,8,32,128]{4,3,2,1,0:T(8,128)S(1)}, f32[2,5,8,32,128]{4,3,2,1,0:T(8,128)S(1)}, u32[]{:S(2)}, u32[]{:S(2)}) collective-permute-start(f32[2,5,8,32,128]{4,3,2,1,0:T(8,128)S(1)} %get-tuple-element.119.refs_0_.refs_1_), channel_id=1, source_target_pairs={{1,0},{0,1},{3,2},{2,3},{5,4},{4,5},{7,6},{6,7},{9,8},{8,9},{11,10... | collective-permute-start | bytes 3932168 | tf_op jit(solution)/shard_map/ppermute | solution.py:525
  11.2 6.0 %collective-permute-start.1 = (f32[8,64,128]{2,1,0:T(8,128)S(1)}, f32[8,64,128]{2,1,0:T(8,128)S(1)}, u32[]{:S(2)}, u32[]{:S(2)}) collective-permute-start(f32[8,64,128]{2,1,0:T(8,128)S(1)} %get-tuple-element.68), channel_id=1, source_target_pairs={{0,2},{2,0},{4,6},{6,4},{8,10},{10,8},{12,14},{14,12},{16,18},{18,... | collective-permute-start | bytes 786440 | tf_op jit(solution)/shard_map/ppermute | solution.py:519
  11.2 9.1 %collective-permute-start = (f32[8,64,128]{2,1,0:T(8,128)S(1)}, f32[8,64,128]{2,1,0:T(8,128)S(1)}, u32[]{:S(2)}, u32[]{:S(2)}) collective-permute-start(f32[8,64,128]{2,1,0:T(8,128)S(1)} %get-tuple-element.66), channel_id=1, source_target_pairs={{2,4},{4,2},{6,8},{8,6},{10,12},{12,10},{14,16},{16,14},{18,20},{2... | collective-permute-start | bytes 786440 | tf_op jit(solution)/shard_map/ppermute | solution.py:522
  17.4 6.5 %collective-permute-start.3 = (f32[8,64,128]{2,1,0:T(8,128)S(1)}, f32[8,64,128]{2,1,0:T(8,128)S(1)}, u32[]{:S(2)}, u32[]{:S(2)}) collective-permute-start(f32[8,64,128]{2,1,0:T(8,128)S(1)} %get-tuple-element.83), channel_id=1, source_target_pairs={{0,2},{2,0},{4,6},{6,4},{8,10},{10,8},{12,14},{14,12},{16,18},{18,... | collective-permute-start | bytes 786440 | tf_op jit(solution)/shard_map/ppermute | solution.py:519
  20.4 8.0 %collective-permute-start.2 = (f32[8,64,128]{2,1,0:T(8,128)S(1)}, f32[8,64,128]{2,1,0:T(8,128)S(1)}, u32[]{:S(2)}, u32[]{:S(2)}) collective-permute-start(f32[8,64,128]{2,1,0:T(8,128)S(1)} %get-tuple-element.82), channel_id=1, source_target_pairs={{2,4},{4,2},{6,8},{8,6},{10,12},{12,10},{14,16},{16,14},{18,20},{2... | collective-permute-start | bytes 786440 | tf_op jit(solution)/shard_map/ppermute | solution.py:522
  24.1 8.0 %collective-permute-start.5 = (f32[8,64,128]{2,1,0:T(8,128)S(1)}, f32[8,64,128]{2,1,0:T(8,128)S(1)}, u32[]{:S(2)}, u32[]{:S(2)}) collective-permute-start(f32[8,64,128]{2,1,0:T(8,128)S(1)} %get-tuple-element.96), channel_id=1, source_target_pairs={{0,2},{2,0},{4,6},{6,4},{8,10},{10,8},{12,14},{14,12},{16,18},{18,... | collective-permute-start | bytes 786440 | tf_op jit(solution)/shard_map/ppermute | solution.py:519
  28.6 10.3 %collective-permute-start.4 = (f32[8,64,128]{2,1,0:T(8,128)S(1)}, f32[8,64,128]{2,1,0:T(8,128)S(1)}, u32[]{:S(2)}, u32[]{:S(2)}) collective-permute-start(f32[8,64,128]{2,1,0:T(8,128)S(1)} %get-tuple-element.95), channel_id=1, source_target_pairs={{2,4},{4,2},{6,8},{8,6},{10,12},{12,10},{14,16},{16,14},{18,20},{2... | collective-permute-start | bytes 786440 | tf_op jit(solution)/shard_map/ppermute | solution.py:522
  32.2 9.5 %collective-permute-start.7 = (f32[8,64,128]{2,1,0:T(8,128)S(1)}, f32[8,64,128]{2,1,0:T(8,128)S(1)}, u32[]{:S(2)}, u32[]{:S(2)}) collective-permute-start(f32[8,64,128]{2,1,0:T(8,128)S(1)} %get-tuple-element.109), channel_id=1, source_target_pairs={{0,2},{2,0},{4,6},{6,4},{8,10},{10,8},{12,14},{14,12},{16,18},{18,... | collective-permute-start | bytes 786440 | tf_op jit(solution)/shard_map/ppermute | solution.py:519
  39.0 3.9 %collective-permute-start.6 = (f32[8,64,128]{2,1,0:T(8,128)S(1)}, f32[8,64,128]{2,1,0:T(8,128)S(1)}, u32[]{:S(2)}, u32[]{:S(2)}) collective-permute-start(f32[8,64,128]{2,1,0:T(8,128)S(1)} %get-tuple-element.108), channel_id=1, source_target_pairs={{2,4},{4,2},{6,8},{8,6},{10,12},{12,10},{14,16},{16,14},{18,20},{2... | collective-permute-start | bytes 786440 | tf_op jit(solution)/shard_map/ppermute | solution.py:522
  41.1 5.0 %collective-permute-start.9 = (f32[8,32,128]{2,1,0:T(8,128)S(1)}, f32[8,32,128]{2,1,0:T(8,128)S(1)}, u32[]{:S(2)}, u32[]{:S(2)}) collective-permute-start(f32[8,32,128]{2,1,0:T(8,128)S(1)} %get-tuple-element.121), channel_id=1, source_target_pairs={{1,0},{0,1},{3,2},{2,3},{5,4},{4,5},{7,6},{6,7},{9,8},{8,9},{11,10... | collective-permute-start | bytes 393224 | tf_op jit(solution)/shard_map/ppermute | solution.py:525
  41.7 2.9 %copy-start.1 = (f32[2,5,16,32,128]{4,3,2,1,0:T(8,128)S(1)}, f32[2,5,16,32,128]{4,3,2,1,0:T(8,128)}, u32[]{:S(2)}) copy-start(f32[2,5,16,32,128]{4,3,2,1,0:T(8,128)} %history.7) | copy-start | bytes 7864324
  43.0 21.5 %collective-permute-start.10 = (f32[8,64,128]{2,1,0:T(8,128)S(1)}, f32[8,64,128]{2,1,0:T(8,128)S(1)}, u32[]{:S(2)}, u32[]{:S(2)}) collective-permute-start(f32[8,64,128]{2,1,0:T(8,128)S(1)} %last_join.1.grad.outer), channel_id=1, source_target_pairs={{1,0},{0,1},{3,2},{2,3},{5,4},{4,5},{7,6},{6,7},{9,8},{8,9},{11,10... | collective-permute-start | bytes 786440 | tf_op jit(solution)/shard_map/ppermute | solution.py:525
  46.4 18.1 %copy-start.3 = (f32[16,64,128]{2,1,0:T(8,128)S(1)}, f32[16,64,128]{2,1,0:T(8,128)}, u32[]{:S(2)}) copy-start(f32[16,64,128]{2,1,0:T(8,128)} %courant.5) | copy-start | bytes 1572868
  63.9 5.3 %collective-permute-start.11 = (f32[8,32,128]{2,1,0:T(8,128)S(1)}, f32[8,32,128]{2,1,0:T(8,128)S(1)}, u32[]{:S(2)}, u32[]{:S(2)}) collective-permute-start(f32[8,32,128]{2,1,0:T(8,128)S(1)} %get-tuple-element.125.inner_move), channel_id=1, source_target_pairs={{1,0},{0,1},{3,2},{2,3},{5,4},{4,5},{7,6},{6,7},{9,8},{8,9},{11,10... | collective-permute-start | bytes 393224 | tf_op jit(solution)/shard_map/ppermute | solution.py:525

commit v3 on v2

--- a/solution.py
+++ b/solution.py
@@ -19,6 +19,10 @@
 SM = pl.BlockSpec(memory_space=pltpu.SMEM)
 HB = pl.BlockSpec(memory_space=pltpu.HBM)
 PARAMS = pltpu.CompilerParams(vmem_limit_bytes=16 << 20)
+
+
+def in_hbm(value):
+    return pltpu.with_memory_space_constraint(value, pltpu.HBM)
 
 
 def shape(*dims):
@@ -70,7 +74,6 @@
     adjoint,
     adjoint_old,
     courant,
-    history,
     o_wave,
     o_wave_old,
     o_adj,
@@ -79,7 +82,6 @@
     o_prod,
     to_core,
     to_chip,
-    o_history,
     b_wave,
     b_wave_old,
     b_adj,
@@ -90,9 +92,6 @@
     rows, across, width = courant.shape
     fetched = [(wave, b_wave), (adjoint, b_adj), (courant, b_cour), (wave_old, b_wave_old), (adjoint_old, b_adj_old)]
     copies = [pltpu.make_async_copy(src, dst, sems.at[n]) for n, (src, dst) in enumerate(fetched)]
-    for n, (start, at) in enumerate([(0, 0), (rows - REACH, REACH)]):
-        src = history.at[:, :, pl.ds(start, REACH)]
-        copies.append(pltpu.make_async_copy(src, o_history.at[:, :, pl.ds(at, REACH)], sems.at[len(fetched) + n]))
     for copy in copies:
         copy.start()
     zero_pads(o_wave)
@@ -115,14 +114,19 @@
         if row >= rows - REACH:
             to_core[row - (rows - REACH)] = now
             to_core[row - (rows - REACH) + REACH] = prod
-    for copy in copies[3:5]:
+    for copy in copies[3:]:
         copy.wait()
     for row in range(rows):
         src = natural_row(row, rows, odd)
         o_wave_old[row, PAD : PAD + across, :] = b_wave_old[src]
         o_adj_old[row] = b_adj_old[src]
-    for copy in copies[5:]:
-        copy.wait()
+
+
+def keep_kernel(history, _, out, sem):
+    start = odd_depth() * (history.shape[2] - REACH)
+    copy = pltpu.make_async_copy(history.at[:, :, pl.ds(start, REACH)], out, sem)
+    copy.start()
+    copy.wait()
 
 
 def split_cell(cell, rows, across, width):
@@ -155,8 +159,9 @@
 
 
 def local_kernel(
-    moment, cell, wavelet, wave, wave_old, prod, adj, adj_old, courant, injected, o_lap, o_wave, o_adj, o_prod
+    moment, cell, wavelet, wave, wave_old, prod, adj, adj_old, courant, injected, *outs
 ):
+    o_lap, o_wave, o_adj, o_prod = outs[-4:]
     rows, across, width = adj.shape
     zero_pads(o_wave)
     zero_pads(o_prod)
@@ -228,47 +233,50 @@
             yield place, row, start, part, lap, new
 
 
-def inner_kernel(
-    scale, count, wave, prod, adj, adj_old, injected, lap1, lap2, lap3, adj4, adj3, *outs
-):
-    rows, across, width = adj.shape
-    piece = across // count
-    which = inner_rows(rows)
-    full = outs[count]
+def lay_pieces(full, outs):
+    count = len(outs)
+    piece = full.shape[1] // count
+    for turn, out in enumerate(outs):
+        offset = lax.rem(lax.axis_index("shot") + turn, count) * piece
+        for place in range(full.shape[0]):
+            out[place] = full[place, pl.ds(pl.multiple_of(offset, 8), piece), :]
+
+
+def inner_kernel(scale, wave, prod, adj, adj_old, injected, lap1, lap2, lap3, adj4, adj3, *outs):
+    full = outs[-1]
+    which = inner_rows(adj.shape[0])
     for place, row, start, part, lap, new in last_rows(which, wave, prod, adj, adj_old, injected):
         known = adj[part] * lap2[part] + adj3[part] * lap3[part]
         full[place, start : start + CHUNK, :] = scale * (known + adj4[part] * lap + new * lap1[part])
-    for turn in range(count):
-        offset = lax.rem(lax.axis_index("shot") + turn, count) * piece
-        for place in range(len(which)):
-            outs[turn][place] = full[place, pl.ds(pl.multiple_of(offset, 8), piece), :]
+    lay_pieces(full, outs[:-1])
 
 
 def outer_kernel(
-    scale, from_core, wave, prod, adj, adj_old, injected, lap1, lap2, lap3, adj4, adj3, o_grad, o_lap, o_adj
+    scale, from_core, wave, prod, adj, adj_old, injected, lap1, lap2, lap3, adj4, adj3, o_known, o_lap, o_adj, *outs
 ):
     rows = adj.shape[0]
+    full = outs[-1]
     waves = dict(core_terms(from_core, 0, rows))
     adjs = dict(core_terms(from_core, 1, rows))
-    which = outer_rows(rows)
+    which = list(range(rows - REACH, rows)) + list(range(REACH))
     for place, row, start, part, lap, new in last_rows(which, wave, prod, adj, adj_old, injected, waves, adjs):
-        put = (place, pl.ds(start, CHUNK), slice(None))
         known = adj[part] * lap2[part] + adj3[part] * lap3[part]
         if row < REACH:
-            o_grad[put] = known
-            o_lap[put] = lap
-            o_adj[put] = new
+            o_known[part] = known
+            o_lap[part] = lap
+            o_adj[part] = new
         else:
-            o_grad[put] = scale * (known + adj4[part] * lap + new * lap1[part])
-
-
-def last_join_kernel(scale, from_chip, grad, lap, adj, lap1, adj4, o_grad):
+            full[place, start : start + CHUNK, :] = scale * (known + adj4[part] * lap + new * lap1[part])
+    lay_pieces(full, outs[:-1])
+
+
+def last_join_kernel(scale, from_chip, known, lap, adj, lap1, adj4, o_grad):
     waves = dict(chip_terms(from_chip, 0))
     adjs = dict(chip_terms(from_chip, 1))
     for row in range(REACH):
         last_lap = lap[row] + waves[row]
         last_adj = adj[row] + adjs[row]
-        o_grad[row] = scale * (grad[row] + adj4[row] * last_lap + last_adj * lap1[row])
+        o_grad[row] = scale * (known[row] + adj4[row] * last_lap + last_adj * lap1[row])
 
 
 def fold(value):
@@ -312,8 +320,8 @@
     return list(range(REACH, rows - REACH))
 
 
-def outer_rows(rows):
-    return list(range(REACH)) + list(range(rows - REACH, rows))
+def near_rows(rows):
+    return list(range(REACH, rows))
 
 
 def add_dots(sums, values, history, row):
@@ -323,7 +331,7 @@
             sums[n] = sums[n] + fold(history[kind, pair, row] * values)
 
 
-def outer_dots_kernel(count, grad, *refs):
+def chip_dots_kernel(count, grad, *refs):
     pieces, out = refs[:count], refs[count]
     total, piece = grad.shape[0], pieces[0].shape[3]
     odd = odd_depth()
@@ -338,16 +346,17 @@
         out[n] = sums[n]
 
 
-def line_kernel(outer, gram, history, *refs):
-    parts, out, o_inner = refs[:-2], refs[-2], refs[-1]
+def line_kernel(count, chip, gram, history, *refs):
+    inner, core, out, o_near = refs[:count], refs[count : 2 * count], refs[-2], refs[-1]
     rows = history.shape[2]
     odd = odd_depth()
-    sums = [outer[n] for n in range(2 * PAIRS)]
-    for place, row in enumerate(inner_rows(rows)):
-        values = parts[0][place]
+    sums = [chip[n] for n in range(2 * PAIRS)]
+    for place, row in enumerate(near_rows(rows)):
+        parts, at = (inner, place) if place < inner[0].shape[0] else (core, place - inner[0].shape[0])
+        values = parts[0][at]
         for other in parts[1:]:
-            values = values + other[place]
-        o_inner[place] = values
+            values = values + other[at]
+        o_near[place] = values
         add_dots(sums, values, history, natural_row(row, rows, odd))
     lane = lane_ids(out.shape[1])
     line = jnp.zeros((1, out.shape[1]), F32)
@@ -393,9 +402,9 @@
     return scale, [-(scale * a) for a in alpha], s_weight
 
 
-def weights_kernel(lines, inner, history, o_weights, o_move):
+def weights_kernel(lines, near, history, o_weights, o_move):
     rows = history.shape[2]
-    piece, width = inner.shape[1], inner.shape[2]
+    piece, width = near.shape[1], near.shape[2]
     odd = odd_depth()
     total = lines[0:8]
     for start in range(8, lines.shape[0], 8):
@@ -404,11 +413,11 @@
     wide = [jnp.broadcast_to(v, (8, width)) for v in [scale] + s_weight + y_weight]
     for n, value in enumerate(wide):
         o_weights[n] = value
-    for place, row in enumerate(inner_rows(rows)):
+    for place, row in enumerate(near_rows(rows)):
         source = natural_row(row, rows, odd)
         for start in range(0, piece, 8):
             at = slice(start, start + 8)
-            o_move[place, at, :] = move_of(wide, inner[place, at, :], history, source, at)
+            o_move[place, at, :] = move_of(wide, near[place, at, :], history, source, at)
 
 
 def move_of(wide, grad, history, row, at):
@@ -419,31 +428,29 @@
     return -move
 
 
-def finish_kernel(count, weight, courant, inner, inner_move, outer, *refs):
+def finish_kernel(count, weight, courant, near, near_move, chip, *refs):
     others, pieces = refs[: count - 1], refs[count - 1 : 2 * count - 1]
     o_grad, o_direction, o_next = refs[2 * count - 1 :]
     rows, across, width = courant.shape
     piece = across // count
     odd = odd_depth()
     wide = [weight[n] for n in range(1 + 2 * PAIRS)]
-    mine = lax.axis_index("shot") * piece
-    for place, row in enumerate(inner_rows(rows)):
+    mine = pl.ds(pl.multiple_of(lax.axis_index("shot") * piece, 8), piece)
+    for place, row in enumerate(near_rows(rows)):
         source = natural_row(row, rows, odd)
-        at = pl.ds(pl.multiple_of(mine, 8), piece)
-        o_grad[source] = inner[place]
-        o_direction[source] = inner_move[place]
-        o_next[source, at, :] = courant[source, at, :] + 0.05 * inner_move[place]
-    outer_list = outer_rows(rows)
-    for place, row in enumerate(outer_list):
+        o_grad[source] = near[place]
+        o_direction[source] = near_move[place]
+        o_next[source, mine, :] = courant[source, mine, :] + 0.05 * near_move[place]
+    for row in range(REACH):
         source = natural_row(row, rows, odd)
-        kept = natural_row(place, len(outer_list), odd)
+        kept = natural_row(row, REACH, odd)
         for turn, ref in enumerate(pieces):
             offset = lax.rem(lax.axis_index("shot") + turn, count) * piece
             for start in range(0, piece, 8):
                 at = pl.ds(pl.multiple_of(offset + start, 8), 8)
-                grad = outer[place, at, :]
+                grad = chip[row, at, :]
                 for other in others:
-                    grad = grad + other[place, at, :]
+                    grad = grad + other[row, at, :]
                 move = move_of(wide, grad, ref, kept, slice(start, start + 8))
                 if turn == 0:
                     o_grad[source, start : start + 8, :] = grad
@@ -456,18 +463,18 @@
     rows, across, width = courant.shape
     piece = across // count
     odd = odd_depth()
-    first = REACH
+    first = (1 - odd) * REACH
     copies = []
     for turn in range(1, count):
         offset = pl.multiple_of(lax.rem(lax.axis_index("shot") + turn, count) * piece, 8)
-        for place, row in enumerate(inner_rows(rows)):
+        for place, row in enumerate(near_rows(rows)):
             source = natural_row(row, rows, odd)
             value = courant[source, pl.ds(offset, piece), :] + 0.05 * moves[turn - 1][place]
             buffer[turn - 1, source - first] = value
         copies.append(
             pltpu.make_async_copy(
                 buffer.at[turn - 1],
-                o_next.at[pl.ds(first, rows - 2 * REACH), pl.ds(offset, piece)],
+                o_next.at[pl.ds(first, rows - REACH), pl.ds(offset, piece)],
                 sem.at[turn - 1],
             )
         )
@@ -525,21 +532,29 @@
         return lax.ppermute(value, "shot", [((i + turn) % shots, i) for i in range(shots)])
 
     block = pltpu.VMEM((rows, across, width), F32)
-    wave, wave_old, adj, adj_old, cour, prod, to_core, to_chip, kept = call(
+    held = [
+        in_hbm(value)
+        for value in (wave_current[0], wave_before[0], adjoint_current[0], adjoint_after[0], courant, history)
+    ]
+    wave, wave_old, adj, adj_old, cour, prod, to_core, to_chip = call(
         stage_kernel,
         "stage",
-        [padded, padded, slab, slab, slab, padded, halo, halo, shape(2, PAIRS, 2 * REACH, piece, width)],
-        wave_current[0],
-        wave_before[0],
-        adjoint_current[0],
-        adjoint_after[0],
-        courant,
-        history,
-        specs=[HB] * 6,
-        scratch=[block] * 5 + [pltpu.SemaphoreType.DMA((7,))],
+        [padded, padded, slab, slab, slab, padded, halo, halo],
+        *held[:5],
+        specs=[HB] * 5,
+        scratch=[block] * 5 + [pltpu.SemaphoreType.DMA((5,))],
     )
     from_chip = swap_chip(to_chip)
     from_core = swap_core(to_core)
+    kept = call(
+        keep_kernel,
+        "keep",
+        shape(2, PAIRS, REACH, piece, width),
+        held[5],
+        from_core,
+        specs=[HB, VM],
+        scratch=[pltpu.SemaphoreType.DMA],
+    )
     kept = [kept] + [from_shot(kept, turn) for turn in range(1, shots)]
     injected = call(
         functools.partial(receiver_kernel, across),
@@ -548,6 +563,8 @@
         receiver_cell,
         residual[0],
     )
+
+    gram = call(gram_kernel, "gram", shape(len(PRODUCTS), 8, width), history)
 
     laps, adjs = [], []
     for moment in range(STEPS - 1):
@@ -564,7 +581,8 @@
             adj_old,
             cour,
             injected,
-            specs=[SM, SM] + [VM] * 7,
+            *([gram] if moment == STEPS - 2 else []),
+            specs=[SM, SM] + [VM] * (8 if moment == STEPS - 2 else 7),
         )
         sends = []
         for chip, came in ((False, from_core), (True, from_chip)):
@@ -590,63 +608,67 @@
         prod = new_prod
 
     scale = 1.0 / (shots * STEPS)
-    inner_count = rows - 2 * REACH
+    inner_count, near_count = rows - 2 * REACH, rows - REACH
     last = (wave, prod, adj, adj_old, injected, laps[0], laps[1], laps[2], adjs[0], adjs[1])
-    mine = shape(inner_count, piece, width)
+
+    def sum_parts(values):
+        return [values[0]] + [from_shot(values[shots - turn], turn) for turn in range(1, shots)]
+
     inner = call(
-        functools.partial(inner_kernel, scale, shots),
+        functools.partial(inner_kernel, scale),
         "inner",
-        [mine] * shots,
+        [shape(inner_count, piece, width)] * shots,
         *last,
         scratch=[pltpu.VMEM((inner_count, across, width), F32)],
     )
-    parts = [inner[0]] + [from_shot(inner[shots - turn], turn) for turn in range(1, shots)]
-    gram = call(gram_kernel, "gram", shape(len(PRODUCTS), 8, width), history)
-    outer_part = shape(2 * REACH, across, width)
+    inner = sum_parts(inner)
     chip_part = shape(REACH, across, width)
-    outer, lap, new_adj = call(
+    known, lap, new_adj, *core = call(
         functools.partial(outer_kernel, scale),
         "outer",
-        [outer_part, chip_part, chip_part],
+        [chip_part] * 3 + [shape(REACH, piece, width)] * shots,
         from_core,
         *last,
-    )
-    outer = call(
+        scratch=[pltpu.VMEM((REACH, across, width), F32)],
+    )
+    core = sum_parts(core)
+    chip = call(
         functools.partial(last_join_kernel, scale),
         "last_join",
-        outer_part,
+        chip_part,
         from_chip,
-        outer,
+        known,
         lap,
         new_adj,
         laps[0],
         adjs[0],
-        aliases={1: 0},
-    )
-    others = [from_shot(outer, turn) for turn in range(1, shots)]
-    outer_dots = call(
-        functools.partial(outer_dots_kernel, shots),
-        "outer_dots",
+    )
+    others = [from_shot(chip, turn) for turn in range(1, shots)]
+    chip_dots = call(
+        functools.partial(chip_dots_kernel, shots),
+        "chip_dots",
         shape(2 * PAIRS, 8, width),
-        outer,
+        chip,
         *kept,
     )
-    line, inner_grad = call(
-        line_kernel,
+    near = shape(near_count, piece, width)
+    line, near_grad = call(
+        functools.partial(line_kernel, shots),
         "line",
-        [shape(devices, 128), mine],
-        outer_dots,
+        [shape(devices, 128), near],
+        chip_dots,
         gram,
         history,
-        *parts,
+        *inner,
+        *core,
     )
     lines = lax.all_to_all(line, ("depth", "shot"), 0, 0, tiled=True)
     weight, move = call(
         weights_kernel,
         "weights",
-        [shape(1 + 2 * PAIRS, 8, width), mine],
+        [shape(1 + 2 * PAIRS, 8, width), near],
         lines,
-        inner_grad,
+        near_grad,
         history,
     )
     moves = [from_shot(move, turn) for turn in range(1, shots)]
@@ -657,9 +679,9 @@
         [own, own, slab],
         weight,
         courant,
-        inner_grad,
+        near_grad,
         move,
-        outer,
+        chip,
         *others,
         *kept,
     )
@@ -674,7 +696,7 @@
         out_specs=HB,
         aliases={1: 0},
         scratch=[
-            pltpu.VMEM((shots - 1, inner_count, piece, width), F32),
+            pltpu.VMEM((shots - 1, near_count, piece, width), F32),
             pltpu.SemaphoreType.DMA((shots - 1,)),
         ],
     )

time: 70.5 us -> 69.3 us (0.983)
  waiting for transfers between devices: 3.96 us -> 11 us
  local copies, waits for them, and re-layouts: 6.96 us -> 0.02 us
  Pallas kernels: 17.7 us -> 20 us
  blocking collectives: 17.2 us -> 15 us
  starting transfers between devices: 22.5 us -> 21.4 us
    ppermute x4 -> x5, waiting for transfers between devices: 3.94 us -> 10.9 us  [from_shot(): lax.ppermute(value, 'shot', [((i + turn) % shots, i) for i in range(shots)])]
    unnamed x22 -> x10, local copies, waits for them, and re-layouts: 6.96 us -> 0.02 us
    all_to_all x1, blocking collectives: 17.2 us -> 15 us  [per_device(): lines = lax.all_to_all(line, ('depth', 'shot'), 0, 0, tiled=True)]
    pallas_call x20 -> x21, Pallas kernels: 17.7 us -> 20 us  [call(): pl.pallas_call(kernel, name=name, out_shape=outs, in_specs=specs or [VM]...]
    ppermute x4, starting transfers between devices: 13.9 us -> 12.6 us  [swap_core(): return lax.ppermute(value, 'depth', on_chip)]
    ppermute x4 -> x5, starting transfers between devices: 5.76 us -> 5.85 us  [from_shot(): lax.ppermute(value, 'shot', [((i + turn) % shots, i) for i in range(shots)])]
  transfers between devices with their start and end apart: 12 -> 13, of which waited for: 2 -> 3; matrix products, arithmetic and copies ran while one was open for 0% -> 0% of each run, Pallas kernels for 23% -> 24%
where the time goes in v3:
time: 69.3 us; the launch traced here: 69 us
  starting transfers between devices  21.4 us (31%)
  Pallas kernels  20 us (29%)
  blocking collectives  15 us (22%)
  waiting for transfers between devices  11 us (16%)
  between operations  1.67 us (2%)
    pallas_call x21, Pallas kernels, call(): pl.pallas_call(kernel, name=name, out_shape=outs, in_specs=specs or [VM]...  20 us
    all_to_all x1, blocking collectives, per_device(): lines = lax.all_to_all(line, ('depth', 'shot'), 0, 0, tiled=True)  15 us
    ppermute x4, starting transfers between devices, swap_core(): return lax.ppermute(value, 'depth', on_chip)  12.6 us
    ppermute x5, waiting for transfers between devices, from_shot(): lax.ppermute(value, 'shot', [((i + turn) % shots, i) for i in range(shots)])  10.9 us
    ppermute x5, starting transfers between devices, from_shot(): lax.ppermute(value, 'shot', [((i + turn) % shots, i) for i in range(shots)])  5.85 us
    ppermute x4, starting transfers between devices, swap_chip(): return lax.ppermute(value, 'depth', off_chip)  2.88 us
  transfers between devices with their start and end apart: 13, of which 3 were waited for; matrix products, arithmetic and copies ran while one was open for 0% of the time, Pallas kernels for 24%

profile of v3, /device:TPU:0, one launch (start us, length us, event | category | flops | bytes accessed | tf_op | source)
XLA Modules:
  0.0 69.0 jit_solution(4604077416213273758)
XLA Ops:
  0.7 1.8 %stage.1 = (f32[16,80,128]{2,1,0:T(8,128)S(1)}, f32[16,80,128]{2,1,0:T(8,128)S(1)}, f32[16,64,128]{2,1,0:T(8,128)S(1)}, f32[16,64,128]{2,1,0:T(8,128)S(1)}, f32[...) custom-call(f32[16,64,128]{2,1,0:T(8,128)} %bitcast.12, ...), custom_call_target="tpu_custom_call" | custom-call | flops 1048576 | bytes 1048576 | tf_op jit(solution)/shard_map/stage/pallas_call | solution.py:489
  2.5 0.5 collective-permute-start.1
  3.0 0.7 collective-permute-start
  4.3 1.8 %receivers.2.injected = f32[4,1024,128]{2,1,0:T(8,128)S(1)} custom-call(s32[1,256]{1,0:T(1,128)S(1)} %copy-done.4, f32[4,256]{1,0:T(4,128)S(1)} %bitcast.11), custom_call_target="tpu_custom_call" | custom-call | flops 1048576 | bytes 1048576 | tf_op jit(solution)/shard_map/receivers/pallas_call | solution.py:489
  6.2 2.8 %local_0.1 = (f32[16,64,128]{2,1,0:T(8,128)S(1)}, f32[16,80,128]{2,1,0:T(8,128)S(1)}, f32[16,64,128]{2,1,0:T(8,128)S(1)}, f32[16,80,128]{2,1,0:T(8,128)S(1)}) custom-call(s32[1]{0:T(128)S(6)} %copy.64.cell, f32[1,4]{1,0:T(1,128)S(1)} %copy-done.2, f32[16,80,128]{2,1,0:T(8,128)S(1)} %get-tuple-element.70.wave.wave_old, ...), custom_call_target="tpu_custom_call" | custom-call | flops 1048576 | bytes 1048576 | tf_op jit(solution)/shard_map/local_0/pallas_call | solution.py:489
  9.0 0.0 collective-permute-done.1.halo._
  9.0 0.1 join_core_0.1
  9.2 3.9 %collective-permute-start.3 = (f32[8,64,128]{2,1,0:T(8,128)S(1)}, f32[8,64,128]{2,1,0:T(8,128)S(1)}, u32[]{:S(2)}, u32[]{:S(2)}) collective-permute-start(f32[8,64,128]{2,1,0:T(8,128)S(1)} %get-tuple-element.84), channel_id=1, source_target_pairs={{0,2},{2,0},{4,6},{6,4},{8,10},{10,8},{12,14},{14,12},{16,18},{18,... | collective-permute-start | bytes 786440 | tf_op jit(solution)/shard_map/ppermute | solution.py:526
  13.1 0.0 collective-permute-done.halo
  13.1 0.1 join_chip_0.1
  13.2 0.7 collective-permute-start.2
  13.9 1.1 %keep.1.refs_0_.refs_1_ = f32[2,5,4,32,128]{4,3,2,1,0:T(8,128)S(1)} custom-call(f32[2,5,16,32,128]{4,3,2,1,0:T(8,128)} %history.7, f32[8,64,128]{2,1,0:T(8,128)S(1)} %collective-permute-done.1.halo._), custom_call_target="tpu_custom_call" | custom-call | flops 1048576 | bytes 1048576 | tf_op jit(solution)/shard_map/keep/pallas_call | solution.py:489
  15.0 1.6 %collective-permute-start.8 = (f32[2,5,4,32,128]{4,3,2,1,0:T(8,128)S(1)}, f32[2,5,4,32,128]{4,3,2,1,0:T(8,128)S(1)}, u32[]{:S(2)}, u32[]{:S(2)}) collective-permute-start(f32[2,5,4,32,128]{4,3,2,1,0:T(8,128)S(1)} %keep.1.refs_0_.refs_1_), channel_id=1, source_target_pairs={{1,0},{0,1},{3,2},{2,3},{5,4},{4,5},{7,6},{6,7},{9,8},{8,9},{11,10... | collective-permute-start | bytes 1966088 | tf_op jit(solution)/shard_map/ppermute | solution.py:532
  16.6 2.8 %local_1.1 = (f32[16,64,128]{2,1,0:T(8,128)S(1)}, f32[16,80,128]{2,1,0:T(8,128)S(1)}, f32[16,64,128]{2,1,0:T(8,128)S(1)}, f32[16,80,128]{2,1,0:T(8,128)S(1)}) custom-call(s32[1]{0:T(128)S(6)} %copy.64.cell, f32[1,4]{1,0:T(1,128)S(1)} %copy-done.2, f32[16,80,128]{2,1,0:T(8,128)S(1)} %get-tuple-element.85.wave.wave_old, ...), custom_call_target="tpu_custom_call" | custom-call | flops 1048576 | bytes 1048576 | tf_op jit(solution)/shard_map/local_1/pallas_call | solution.py:489
  19.4 0.0 collective-permute-done.3.halo
  19.4 0.0 copy-start
  19.5 0.1 join_core_1.1
  19.6 4.0 %collective-permute-start.5 = (f32[8,64,128]{2,1,0:T(8,128)S(1)}, f32[8,64,128]{2,1,0:T(8,128)S(1)}, u32[]{:S(2)}, u32[]{:S(2)}) collective-permute-start(f32[8,64,128]{2,1,0:T(8,128)S(1)} %get-tuple-element.97), channel_id=1, source_target_pairs={{0,2},{2,0},{4,6},{6,4},{8,10},{10,8},{12,14},{14,12},{16,18},{18,... | collective-permute-start | bytes 786440 | tf_op jit(solution)/shard_map/ppermute | solution.py:526
  23.6 0.0 collective-permute-done.2.halo
  23.6 0.1 join_chip_1.1
  23.7 0.7 collective-permute-start.4
  24.4 0.7 %gram.1.outs_0_ = f32[30,8,128]{2,1,0:T(8,128)S(1)} custom-call(f32[2,5,16,32,128]{4,3,2,1,0:T(8,128)S(1)} %copy-done), custom_call_target="tpu_custom_call" | custom-call | flops 1048576 | bytes 1048576 | tf_op jit(solution)/shard_map/gram/pallas_call | solution.py:489
  25.2 2.9 %local_2.1 = (f32[16,64,128]{2,1,0:T(8,128)S(1)}, f32[16,80,128]{2,1,0:T(8,128)S(1)}, f32[16,64,128]{2,1,0:T(8,128)S(1)}, f32[16,80,128]{2,1,0:T(8,128)S(1)}) custom-call(s32[1]{0:T(128)S(6)} %copy.64.cell, f32[1,4]{1,0:T(1,128)S(1)} %copy-done.2, f32[16,80,128]{2,1,0:T(8,128)S(1)} %get-tuple-element.98.wave, ...), custom_call_target="tpu_custom_call" | custom-call | flops 1048576 | bytes 1048576 | tf_op jit(solution)/shard_map/local_2/pallas_call | solution.py:489
  28.0 0.0 collective-permute-done.5.halo
  28.1 0.1 join_core_2.1
  28.2 4.2 %collective-permute-start.7 = (f32[8,64,128]{2,1,0:T(8,128)S(1)}, f32[8,64,128]{2,1,0:T(8,128)S(1)}, u32[]{:S(2)}, u32[]{:S(2)}) collective-permute-start(f32[8,64,128]{2,1,0:T(8,128)S(1)} %get-tuple-element.110), channel_id=1, source_target_pairs={{0,2},{2,0},{4,6},{6,4},{8,10},{10,8},{12,14},{14,12},{16,18},{18,... | collective-permute-start | bytes 786440 | tf_op jit(solution)/shard_map/ppermute | solution.py:526
  32.4 0.0 collective-permute-done.4.halo
  32.4 0.1 join_chip_2.1
  32.5 0.9 %collective-permute-start.6 = (f32[8,64,128]{2,1,0:T(8,128)S(1)}, f32[8,64,128]{2,1,0:T(8,128)S(1)}, u32[]{:S(2)}, u32[]{:S(2)}) collective-permute-start(f32[8,64,128]{2,1,0:T(8,128)S(1)} %get-tuple-element.109), channel_id=1, source_target_pairs={{2,4},{4,2},{6,8},{8,6},{10,12},{12,10},{14,16},{16,14},{18,20},{2... | collective-permute-start | bytes 786440 | tf_op jit(solution)/shard_map/ppermute | solution.py:529
  33.4 1.3 %inner.1 = (f32[8,32,128]{2,1,0:T(8,128)S(1)}, f32[8,32,128]{2,1,0:T(8,128)S(1)}) custom-call(f32[16,80,128]{2,1,0:T(8,128)S(1)} %get-tuple-element.111.wave, f32[16,80,128]{2,1,0:T(8,128)S(1)} %get-tuple-element.112.prod, f32[16,64,128]{2,1,0:T(8,128)S(1)} %get-tuple-element.113.adj, f32[16,64,128]{2,1,0:T(8,128)S(1)} %get-tuple-element.100.adj.adj_old.adj3, ...), custom_call_target="tpu_custom_call" | custom-call | flops 1048576 | bytes 1048576 | tf_op jit(solution)/shard_map/inner/pallas_call | solution.py:489
  34.7 1.6 %collective-permute-start.9 = (f32[8,32,128]{2,1,0:T(8,128)S(1)}, f32[8,32,128]{2,1,0:T(8,128)S(1)}, u32[]{:S(2)}, u32[]{:S(2)}) collective-permute-start(f32[8,32,128]{2,1,0:T(8,128)S(1)} %get-tuple-element.121), channel_id=1, source_target_pairs={{1,0},{0,1},{3,2},{2,3},{5,4},{4,5},{7,6},{6,7},{9,8},{8,9},{11,10... | collective-permute-start | bytes 393224 | tf_op jit(solution)/shard_map/ppermute | solution.py:532
  36.3 0.0 collective-permute-done.7.from_core
  36.3 1.2 %outer.1 = (f32[4,64,128]{2,1,0:T(8,128)S(1)}, f32[4,64,128]{2,1,0:T(8,128)S(1)}, f32[4,64,128]{2,1,0:T(8,128)S(1)}, f32[4,32,128]{2,1,0:T(8,128)S(1)}, f32[4,32,128]{2,1,0:T(8,128)S(1)}) custom-call(f32[8,64,128]{2,1,0:T(8,128)S(1)} %collective-permute-done.7.from_core, f32[16,80,128]{2,1,0:T(8,128)S(1)} %get-tuple-element.111.wave, ...), custom_call_target="tpu_custom_call" | custom-call | flops 1048576 | bytes 1048576 | tf_op jit(solution)/shard_map/outer/pallas_call | solution.py:489
  37.5 0.6 collective-permute-start.10
  38.0 0.0 collective-permute-done.6.from_chip
  38.0 0.1 last_join.1.grad.chip
  38.1 0.1 chip_dots.1.chip
  38.3 1.4 %collective-permute-done.9.refs_1_ = f32[8,32,128]{2,1,0:T(8,128)S(1)} collective-permute-done((f32[8,32,128]{2,1,0:T(8,128)S(1)}, f32[8,32,128]{2,1,0:T(8,128)S(1)}, u32[]{:S(2)}, u32[]{:S(2)}) %collective-permute-start.9) | collective-permute-done | bytes 131104 | tf_op jit(solution)/shard_map/ppermute | solution.py:532
  39.7 2.1 %collective-permute-done.10.refs_3_ = f32[4,32,128]{2,1,0:T(8,128)S(1)} collective-permute-done((f32[4,32,128]{2,1,0:T(8,128)S(1)}, f32[4,32,128]{2,1,0:T(8,128)S(1)}, u32[]{:S(2)}, u32[]{:S(2)}) %collective-permute-start.10) | collective-permute-done | bytes 65568 | tf_op jit(solution)/shard_map/ppermute | solution.py:532
  41.8 0.3 line.1
  42.2 15.0 %all_to_all.11 = f32[32,1,128]{2,1,0:T(1,128)S(1)} all-to-all(f32[32,1,128]{2,1,0:T(1,128)S(1)} %bitcast.10), channel_id=1, replica_groups=mesh['depth'=16,'shot'=2] {'depth','shot'}, dimensions={0} | all-to-all | bytes 32768 | tf_op jit(solution)/shard_map/all_to_all | solution.py:665
  57.1 0.4 weights.1
  57.5 0.6 collective-permute-start.12
  58.0 1.5 %collective-permute-start.11 = (f32[4,64,128]{2,1,0:T(8,128)S(1)}, f32[4,64,128]{2,1,0:T(8,128)S(1)}, u32[]{:S(2)}, u32[]{:S(2)}) collective-permute-start(f32[4,64,128]{2,1,0:T(8,128)S(1)} %last_join.1.grad.chip), channel_id=1, source_target_pairs={{1,0},{0,1},{3,2},{2,3},{5,4},{4,5},{7,6},{6,7},{9,8},{8,9},{11,10... | collective-permute-start | bytes 393224 | tf_op jit(solution)/shard_map/ppermute | solution.py:532
  59.6 7.4 %collective-permute-done.11.refs_0_ = f32[4,64,128]{2,1,0:T(8,128)S(1)} collective-permute-done((f32[4,64,128]{2,1,0:T(8,128)S(1)}, f32[4,64,128]{2,1,0:T(8,128)S(1)}, u32[]{:S(2)}, u32[]{:S(2)}) %collective-permute-start.11) | collective-permute-done | bytes 131104 | tf_op jit(solution)/shard_map/ppermute | solution.py:532
  66.9 1.1 %finish.1 = (f32[16,32,128]{2,1,0:T(8,128)}, f32[16,32,128]{2,1,0:T(8,128)}, f32[16,64,128]{2,1,0:T(8,128)}) custom-call(f32[11,8,128]{2,1,0:T(8,128)S(1)} %get-tuple-element.126.weight, f32[16,64,128]{2,1,0:T(8,128)S(1)} %copy-done.1, f32[12,32,128]{2,1,0:T(8,128)S(1)} %get-tuple-element.125.near, f32[12,32,128]{2,1,0:T(8,128)S(1)} %get-tuple-element.127.near_move, ...), custom_call_target="tpu_custom_call" | custom-call | flops 1048576 | bytes 1048576 | tf_op jit(solution)/shard_map/finish/pallas_call | solution.py:489
  68.1 0.0 collective-permute-done.12.refs_0_
  68.1 0.7 %last_piece.1 = f32[16,64,128]{2,1,0:T(8,128)} custom-call(f32[16,64,128]{2,1,0:T(8,128)S(1)} %copy-done.1, f32[16,64,128]{2,1,0:T(8,128)} %get-tuple-element.130.done, f32[12,32,128]{2,1,0:T(8,128)S(1)} %collective-permute-done.12.refs_0_), custom_call_target="tpu_custom_call", output_to_operand_aliasing={{}: (1, {})} | custom-call | flops 1048576 | bytes 1048576 | tf_op jit(solution)/shard_map/last_piece/pallas_call | solution.py:489
  (10 shorter events, 0.0 us)
Async XLA Ops:
  0.6 3.7 %copy-start.3 = (f32[1,4,256]{2,1,0:T(4,128)S(1)}, f32[1,4,256]{2,1,0:T(4,128)}, u32[]{:S(2)}) copy-start(f32[1,4,256]{2,1,0:T(4,128)} %param.18) | copy-start | bytes 12292
  0.6 3.7 %copy-start.4 = (s32[1,256]{1,0:T(1,128)S(1)}, s32[1,256]{1,0:T(1,128)}, u32[]{:S(2)}) copy-start(s32[1,256]{1,0:T(1,128)} %receivers.3) | copy-start | bytes 3076
  0.7 5.5 %copy-start.2 = (f32[1,4]{1,0:T(1,128)S(1)}, f32[1,4]{1,0:T(1,128)}, u32[]{:S(2)}) copy-start(f32[1,4]{1,0:T(1,128)} %wavelet.5) | copy-start | bytes 52
  2.5 6.6 %collective-permute-start.1 = (f32[8,64,128]{2,1,0:T(8,128)S(1)}, f32[8,64,128]{2,1,0:T(8,128)S(1)}, u32[]{:S(2)}, u32[]{:S(2)}) collective-permute-start(f32[8,64,128]{2,1,0:T(8,128)S(1)} %get-tuple-element.69), channel_id=1, source_target_pairs={{0,2},{2,0},{4,6},{6,4},{8,10},{10,8},{12,14},{14,12},{16,18},{18,... | collective-permute-start | bytes 786440 | tf_op jit(solution)/shard_map/ppermute | solution.py:526
  3.0 10.1 %collective-permute-start = (f32[8,64,128]{2,1,0:T(8,128)S(1)}, f32[8,64,128]{2,1,0:T(8,128)S(1)}, u32[]{:S(2)}, u32[]{:S(2)}) collective-permute-start(f32[8,64,128]{2,1,0:T(8,128)S(1)} %get-tuple-element.67), channel_id=1, source_target_pairs={{2,4},{4,2},{6,8},{8,6},{10,12},{12,10},{14,16},{16,14},{18,20},{2... | collective-permute-start | bytes 786440 | tf_op jit(solution)/shard_map/ppermute | solution.py:529
  9.2 10.3 %collective-permute-start.3 = (f32[8,64,128]{2,1,0:T(8,128)S(1)}, f32[8,64,128]{2,1,0:T(8,128)S(1)}, u32[]{:S(2)}, u32[]{:S(2)}) collective-permute-start(f32[8,64,128]{2,1,0:T(8,128)S(1)} %get-tuple-element.84), channel_id=1, source_target_pairs={{0,2},{2,0},{4,6},{6,4},{8,10},{10,8},{12,14},{14,12},{16,18},{18,... | collective-permute-start | bytes 786440 | tf_op jit(solution)/shard_map/ppermute | solution.py:526
  13.2 10.4 %collective-permute-start.2 = (f32[8,64,128]{2,1,0:T(8,128)S(1)}, f32[8,64,128]{2,1,0:T(8,128)S(1)}, u32[]{:S(2)}, u32[]{:S(2)}) collective-permute-start(f32[8,64,128]{2,1,0:T(8,128)S(1)} %get-tuple-element.83), channel_id=1, source_target_pairs={{2,4},{4,2},{6,8},{8,6},{10,12},{12,10},{14,16},{16,14},{18,20},{2... | collective-permute-start | bytes 786440 | tf_op jit(solution)/shard_map/ppermute | solution.py:529
  15.0 23.1 %collective-permute-start.8 = (f32[2,5,4,32,128]{4,3,2,1,0:T(8,128)S(1)}, f32[2,5,4,32,128]{4,3,2,1,0:T(8,128)S(1)}, u32[]{:S(2)}, u32[]{:S(2)}) collective-permute-start(f32[2,5,4,32,128]{4,3,2,1,0:T(8,128)S(1)} %keep.1.refs_0_.refs_1_), channel_id=1, source_target_pairs={{1,0},{0,1},{3,2},{2,3},{5,4},{4,5},{7,6},{6,7},{9,8},{8,9},{11,10... | collective-permute-start | bytes 1966088 | tf_op jit(solution)/shard_map/ppermute | solution.py:532
  19.4 5.0 %copy-start = (f32[2,5,16,32,128]{4,3,2,1,0:T(8,128)S(1)}, f32[2,5,16,32,128]{4,3,2,1,0:T(8,128)}, u32[]{:S(2)}) copy-start(f32[2,5,16,32,128]{4,3,2,1,0:T(8,128)} %history.7) | copy-start | bytes 7864324
  19.6 8.5 %collective-permute-start.5 = (f32[8,64,128]{2,1,0:T(8,128)S(1)}, f32[8,64,128]{2,1,0:T(8,128)S(1)}, u32[]{:S(2)}, u32[]{:S(2)}) collective-permute-start(f32[8,64,128]{2,1,0:T(8,128)S(1)} %get-tuple-element.97), channel_id=1, source_target_pairs={{0,2},{2,0},{4,6},{6,4},{8,10},{10,8},{12,14},{14,12},{16,18},{18,... | collective-permute-start | bytes 786440 | tf_op jit(solution)/shard_map/ppermute | solution.py:526
  23.7 8.6 %collective-permute-start.4 = (f32[8,64,128]{2,1,0:T(8,128)S(1)}, f32[8,64,128]{2,1,0:T(8,128)S(1)}, u32[]{:S(2)}, u32[]{:S(2)}) collective-permute-start(f32[8,64,128]{2,1,0:T(8,128)S(1)} %get-tuple-element.96), channel_id=1, source_target_pairs={{2,4},{4,2},{6,8},{8,6},{10,12},{12,10},{14,16},{16,14},{18,20},{2... | collective-permute-start | bytes 786440 | tf_op jit(solution)/shard_map/ppermute | solution.py:529
  28.2 8.1 %collective-permute-start.7 = (f32[8,64,128]{2,1,0:T(8,128)S(1)}, f32[8,64,128]{2,1,0:T(8,128)S(1)}, u32[]{:S(2)}, u32[]{:S(2)}) collective-permute-start(f32[8,64,128]{2,1,0:T(8,128)S(1)} %get-tuple-element.110), channel_id=1, source_target_pairs={{0,2},{2,0},{4,6},{6,4},{8,10},{10,8},{12,14},{14,12},{16,18},{18,... | collective-permute-start | bytes 786440 | tf_op jit(solution)/shard_map/ppermute | solution.py:526
  32.5 5.5 %collective-permute-start.6 = (f32[8,64,128]{2,1,0:T(8,128)S(1)}, f32[8,64,128]{2,1,0:T(8,128)S(1)}, u32[]{:S(2)}, u32[]{:S(2)}) collective-permute-start(f32[8,64,128]{2,1,0:T(8,128)S(1)} %get-tuple-element.109), channel_id=1, source_target_pairs={{2,4},{4,2},{6,8},{8,6},{10,12},{12,10},{14,16},{16,14},{18,20},{2... | collective-permute-start | bytes 786440 | tf_op jit(solution)/shard_map/ppermute | solution.py:529
  34.7 5.0 %collective-permute-start.9 = (f32[8,32,128]{2,1,0:T(8,128)S(1)}, f32[8,32,128]{2,1,0:T(8,128)S(1)}, u32[]{:S(2)}, u32[]{:S(2)}) collective-permute-start(f32[8,32,128]{2,1,0:T(8,128)S(1)} %get-tuple-element.121), channel_id=1, source_target_pairs={{1,0},{0,1},{3,2},{2,3},{5,4},{4,5},{7,6},{6,7},{9,8},{8,9},{11,10... | collective-permute-start | bytes 393224 | tf_op jit(solution)/shard_map/ppermute | solution.py:532
  37.5 4.3 %collective-permute-start.10 = (f32[4,32,128]{2,1,0:T(8,128)S(1)}, f32[4,32,128]{2,1,0:T(8,128)S(1)}, u32[]{:S(2)}, u32[]{:S(2)}) collective-permute-start(f32[4,32,128]{2,1,0:T(8,128)S(1)} %get-tuple-element.123), channel_id=1, source_target_pairs={{1,0},{0,1},{3,2},{2,3},{5,4},{4,5},{7,6},{6,7},{9,8},{8,9},{11,10... | collective-permute-start | bytes 196616 | tf_op jit(solution)/shard_map/ppermute | solution.py:532
  41.8 25.1 %copy-start.1 = (f32[16,64,128]{2,1,0:T(8,128)S(1)}, f32[16,64,128]{2,1,0:T(8,128)}, u32[]{:S(2)}) copy-start(f32[16,64,128]{2,1,0:T(8,128)} %courant.5) | copy-start | bytes 1572868
  57.5 10.6 %collective-permute-start.12 = (f32[12,32,128]{2,1,0:T(8,128)S(1)}, f32[12,32,128]{2,1,0:T(8,128)S(1)}, u32[]{:S(2)}, u32[]{:S(2)}) collective-permute-start(f32[12,32,128]{2,1,0:T(8,128)S(1)} %get-tuple-element.127.near_move), channel_id=1, source_target_pairs={{1,0},{0,1},{3,2},{2,3},{5,4},{4,5},{7,6},{6,7},{9,8},{8,9},{11,10... | collective-permute-start | bytes 589832 | tf_op jit(solution)/shard_map/ppermute | solution.py:532
  58.0 8.9 %collective-permute-start.11 = (f32[4,64,128]{2,1,0:T(8,128)S(1)}, f32[4,64,128]{2,1,0:T(8,128)S(1)}, u32[]{:S(2)}, u32[]{:S(2)}) collective-permute-start(f32[4,64,128]{2,1,0:T(8,128)S(1)} %last_join.1.grad.chip), channel_id=1, source_target_pairs={{1,0},{0,1},{3,2},{2,3},{5,4},{4,5},{7,6},{6,7},{9,8},{8,9},{11,10... | collective-permute-start | bytes 393224 | tf_op jit(solution)/shard_map/ppermute | solution.py:532

commit v4 on v3

--- a/solution.py
+++ b/solution.py
@@ -11,6 +11,7 @@
 PAIRS = 5
 REACH = 4
 PAD = 8
+GROUP = 8
 CHUNK = 16
 coefficients = (-205.0 / 72.0, 8.0 / 5.0, -1.0 / 5.0, 8.0 / 315.0, -1.0 / 560.0)
 
@@ -41,11 +42,42 @@
     return lax.broadcasted_iota(jnp.int32, (1, width), 1)
 
 
-def laplace_chunk(ref, row, start, size):
-    rows, width = ref.shape[0], ref.shape[2]
-    core = ref[row, PAD + start : PAD + start + size, :]
-    lane = lax.broadcasted_iota(jnp.int32, (size, width), 1)
-    total = (3.0 * coefficients[0]) * core
+def split3(value):
+    high = value.astype(jnp.bfloat16)
+    left = value - high.astype(F32)
+    middle = left.astype(jnp.bfloat16)
+    return high, middle, (left - middle.astype(F32)).astype(jnp.bfloat16)
+
+
+def band_parts(width):
+    apart = jnp.abs(
+        lax.broadcasted_iota(jnp.int32, (width, width), 0) - lax.broadcasted_iota(jnp.int32, (width, width), 1)
+    )
+    band = jnp.zeros((width, width), F32)
+    for reach in range(1, REACH + 1):
+        band = band + jnp.where(apart == reach, coefficients[reach], 0.0)
+    high, middle, low = split3(band)
+    pair = jnp.concatenate([high, middle], axis=1)
+    return jnp.concatenate([pair, pair], axis=0), jnp.concatenate([high, low], axis=0)
+
+
+def along_last(ref, which, wide_band, tall_band, out):
+    width = ref.shape[2]
+    across = ref.shape[1] - 2 * PAD
+    for first in range(0, len(which), GROUP):
+        group = which[first : first + GROUP]
+        cells = jnp.concatenate([ref[row, PAD : PAD + across, :] for row in group], axis=0)
+        high, middle, low = split3(cells)
+        large = jnp.dot(jnp.concatenate([high, middle], axis=1), wide_band, preferred_element_type=F32)
+        small = jnp.dot(jnp.concatenate([low, high], axis=1), tall_band, preferred_element_type=F32)
+        total = large[:, :width] + (large[:, width:] + small)
+        for n in range(len(group)):
+            out[first + n] = total[n * across : (n + 1) * across]
+
+
+def laplace_chunk(ref, row, start, size, along):
+    rows = ref.shape[0]
+    total = along + (3.0 * coefficients[0]) * ref[row, PAD + start : PAD + start + size, :]
     for reach in range(1, REACH + 1):
         near = (
             ref[row, PAD + start + reach : PAD + start + reach + size, :]
@@ -55,8 +87,6 @@
             near = near + ref[row - reach, PAD + start : PAD + start + size, :]
         if row + reach < rows:
             near = near + ref[row + reach, PAD + start : PAD + start + size, :]
-        near = near + jnp.where(lane >= reach, pltpu.roll(core, reach, 1), 0.0)
-        near = near + jnp.where(lane < width - reach, pltpu.roll(core, width - reach, 1), 0.0)
         total = total + coefficients[reach] * near
     return total
 
@@ -82,6 +112,8 @@
     o_prod,
     to_core,
     to_chip,
+    o_wide,
+    o_tall,
     b_wave,
     b_wave_old,
     b_adj,
@@ -97,6 +129,7 @@
     zero_pads(o_wave)
     zero_pads(o_wave_old)
     zero_pads(o_prod)
+    o_wide[...], o_tall[...] = band_parts(width)
     odd = odd_depth()
     for copy in copies[:3]:
         copy.wait()
@@ -159,20 +192,22 @@
 
 
 def local_kernel(
-    moment, cell, wavelet, wave, wave_old, prod, adj, adj_old, courant, injected, *outs
+    moment, cell, wavelet, wave, wave_old, prod, adj, adj_old, courant, injected, wide_band, tall_band, *outs
 ):
-    o_lap, o_wave, o_adj, o_prod = outs[-4:]
+    o_lap, o_wave, o_adj, o_prod, along_wave, along_prod = outs[-6:]
     rows, across, width = adj.shape
+    along_last(wave, list(range(rows)), wide_band[...], tall_band[...], along_wave)
+    along_last(prod, list(range(rows)), wide_band[...], tall_band[...], along_prod)
     zero_pads(o_wave)
     zero_pads(o_prod)
     for row in range(rows):
         for start in range(0, across, CHUNK):
             part = (row, pl.ds(start, CHUNK), slice(None))
             wide = (row, pl.ds(PAD + start, CHUNK), slice(None))
-            lap = laplace_chunk(wave, row, start, CHUNK)
+            lap = laplace_chunk(wave, row, start, CHUNK, along_wave[part])
             o_lap[part] = lap
             o_wave[wide] = 2.0 * wave[wide] - wave_old[wide] + courant[part] * lap
-            new = 2.0 * adj[part] - adj_old[part] + laplace_chunk(prod, row, start, CHUNK)
+            new = 2.0 * adj[part] - adj_old[part] + laplace_chunk(prod, row, start, CHUNK, along_prod[part])
             new = new + injected[STEPS - 1 - moment, row * across + start : row * across + start + CHUNK, :]
             o_adj[part] = new
             o_prod[wide] = courant[part] * new
@@ -219,17 +254,17 @@
         send[REACH + row - first] = new
 
 
-def last_rows(which, wave, prod, adj, adj_old, injected, extra_lap=None, extra_adj=None):
+def last_rows(which, wave, prod, adj, adj_old, injected, wide_band, tall_band, along_wave, along_prod):
     across = adj.shape[1]
+    along_last(wave, which, wide_band[...], tall_band[...], along_wave)
+    along_last(prod, which, wide_band[...], tall_band[...], along_prod)
     for place, row in enumerate(which):
         for start in range(0, across, CHUNK):
             part = (row, pl.ds(start, CHUNK), slice(None))
-            lap = laplace_chunk(wave, row, start, CHUNK)
-            new = 2.0 * adj[part] - adj_old[part] + laplace_chunk(prod, row, start, CHUNK)
+            put = (place, pl.ds(start, CHUNK), slice(None))
+            lap = laplace_chunk(wave, row, start, CHUNK, along_wave[put])
+            new = 2.0 * adj[part] - adj_old[part] + laplace_chunk(prod, row, start, CHUNK, along_prod[put])
             new = new + injected[0, row * across + start : row * across + start + CHUNK, :]
-            if extra_lap is not None and row in extra_lap:
-                lap = lap + extra_lap[row][start : start + CHUNK]
-                new = new + extra_adj[row][start : start + CHUNK]
             yield place, row, start, part, lap, new
 
 
@@ -242,35 +277,47 @@
             out[place] = full[place, pl.ds(pl.multiple_of(offset, 8), piece), :]
 
 
-def inner_kernel(scale, wave, prod, adj, adj_old, injected, lap1, lap2, lap3, adj4, adj3, *outs):
-    full = outs[-1]
+def known_terms(part, adj, lap2, lap3, adj3):
+    return adj[part] * lap2[part] + adj3[part] * lap3[part]
+
+
+def inner_kernel(scale, _, wave, prod, adj, adj_old, injected, wide, tall, lap1, lap2, lap3, adj4, adj3, *outs):
+    full, along = outs[-3], outs[-2:]
     which = inner_rows(adj.shape[0])
-    for place, row, start, part, lap, new in last_rows(which, wave, prod, adj, adj_old, injected):
-        known = adj[part] * lap2[part] + adj3[part] * lap3[part]
+    for place, row, start, part, lap, new in last_rows(which, wave, prod, adj, adj_old, injected, wide, tall, *along):
+        known = known_terms(part, adj, lap2, lap3, adj3)
         full[place, start : start + CHUNK, :] = scale * (known + adj4[part] * lap + new * lap1[part])
-    lay_pieces(full, outs[:-1])
-
-
-def outer_kernel(
-    scale, from_core, wave, prod, adj, adj_old, injected, lap1, lap2, lap3, adj4, adj3, o_known, o_lap, o_adj, *outs
+    lay_pieces(full, outs[:-3])
+
+
+def core_kernel(
+    scale, from_core, wave, prod, adj, adj_old, injected, wide, tall, lap1, lap2, lap3, adj4, adj3, *outs
 ):
+    full, along = outs[-3], outs[-2:]
     rows = adj.shape[0]
-    full = outs[-1]
     waves = dict(core_terms(from_core, 0, rows))
     adjs = dict(core_terms(from_core, 1, rows))
-    which = list(range(rows - REACH, rows)) + list(range(REACH))
-    for place, row, start, part, lap, new in last_rows(which, wave, prod, adj, adj_old, injected, waves, adjs):
-        known = adj[part] * lap2[part] + adj3[part] * lap3[part]
-        if row < REACH:
-            o_known[part] = known
-            o_lap[part] = lap
-            o_adj[part] = new
-        else:
-            full[place, start : start + CHUNK, :] = scale * (known + adj4[part] * lap + new * lap1[part])
-    lay_pieces(full, outs[:-1])
-
-
-def last_join_kernel(scale, from_chip, known, lap, adj, lap1, adj4, o_grad):
+    which = list(range(rows - REACH, rows))
+    for place, row, start, part, lap, new in last_rows(which, wave, prod, adj, adj_old, injected, wide, tall, *along):
+        known = known_terms(part, adj, lap2, lap3, adj3)
+        lap = lap + waves[row][start : start + CHUNK]
+        new = new + adjs[row][start : start + CHUNK]
+        full[place, start : start + CHUNK, :] = scale * (known + adj4[part] * lap + new * lap1[part])
+    lay_pieces(full, outs[:-3])
+
+
+def chip_kernel(
+    wave, prod, adj, adj_old, injected, wide, tall, lap1, lap2, lap3, adj4, adj3, o_known, o_lap, o_adj, *along
+):
+    which = list(range(REACH))
+    for place, row, start, part, lap, new in last_rows(which, wave, prod, adj, adj_old, injected, wide, tall, *along):
+        o_known[part] = known_terms(part, adj, lap2, lap3, adj3)
+        o_lap[part] = lap
+        o_adj[part] = new
+
+
+def last_join_kernel(scale, from_chip, known, lap, adj, lap1, adj4, *refs):
+    o_grad = refs[-1]
     waves = dict(chip_terms(from_chip, 0))
     adjs = dict(chip_terms(from_chip, 1))
     for row in range(REACH):
@@ -402,7 +449,8 @@
     return scale, [-(scale * a) for a in alpha], s_weight
 
 
-def weights_kernel(lines, near, history, o_weights, o_move):
+def weights_kernel(lines, near, history, *refs):
+    o_weights, o_move = refs[-2:]
     rows = history.shape[2]
     piece, width = near.shape[1], near.shape[2]
     odd = odd_depth()
@@ -536,10 +584,11 @@
         in_hbm(value)
         for value in (wave_current[0], wave_before[0], adjoint_current[0], adjoint_after[0], courant, history)
     ]
-    wave, wave_old, adj, adj_old, cour, prod, to_core, to_chip = call(
+    bands = [jax.ShapeDtypeStruct((2 * width, n * width), jnp.bfloat16) for n in (2, 1)]
+    wave, wave_old, adj, adj_old, cour, prod, to_core, to_chip, *bands = call(
         stage_kernel,
         "stage",
-        [padded, padded, slab, slab, slab, padded, halo, halo],
+        [padded, padded, slab, slab, slab, padded, halo, halo] + bands,
         *held[:5],
         specs=[HB] * 5,
         scratch=[block] * 5 + [pltpu.SemaphoreType.DMA((5,))],
@@ -581,8 +630,10 @@
             adj_old,
             cour,
             injected,
+            *bands,
             *([gram] if moment == STEPS - 2 else []),
-            specs=[SM, SM] + [VM] * (8 if moment == STEPS - 2 else 7),
+            specs=[SM, SM] + [VM] * (10 if moment == STEPS - 2 else 9),
+            scratch=[block] * 2,
         )
         sends = []
         for chip, came in ((False, from_core), (True, from_chip)):
@@ -609,29 +660,33 @@
 
     scale = 1.0 / (shots * STEPS)
     inner_count, near_count = rows - 2 * REACH, rows - REACH
-    last = (wave, prod, adj, adj_old, injected, laps[0], laps[1], laps[2], adjs[0], adjs[1])
+    last = (wave, prod, adj, adj_old, injected, *bands, laps[0], laps[1], laps[2], adjs[0], adjs[1])
 
     def sum_parts(values):
         return [values[0]] + [from_shot(values[shots - turn], turn) for turn in range(1, shots)]
 
+    def some_rows(count, copies):
+        return [pltpu.VMEM((count, across, width), F32)] * copies
+
+    core = call(
+        functools.partial(core_kernel, scale),
+        "core",
+        [shape(REACH, piece, width)] * shots,
+        from_core,
+        *last,
+        scratch=some_rows(REACH, 3),
+    )
     inner = call(
         functools.partial(inner_kernel, scale),
         "inner",
         [shape(inner_count, piece, width)] * shots,
+        core[0],
         *last,
-        scratch=[pltpu.VMEM((inner_count, across, width), F32)],
-    )
-    inner = sum_parts(inner)
+        scratch=some_rows(inner_count, 3),
+    )
+    core, inner = sum_parts(core), sum_parts(inner)
     chip_part = shape(REACH, across, width)
-    known, lap, new_adj, *core = call(
-        functools.partial(outer_kernel, scale),
-        "outer",
-        [chip_part] * 3 + [shape(REACH, piece, width)] * shots,
-        from_core,
-        *last,
-        scratch=[pltpu.VMEM((REACH, across, width), F32)],
-    )
-    core = sum_parts(core)
+    known, lap, new_adj = call(chip_kernel, "chip", [chip_part] * 3, *last, scratch=some_rows(REACH, 2))
     chip = call(
         functools.partial(last_join_kernel, scale),
         "last_join",
@@ -642,6 +697,8 @@
         new_adj,
         laps[0],
         adjs[0],
+        *core[1:],
+        *inner[1:],
     )
     others = [from_shot(chip, turn) for turn in range(1, shots)]
     chip_dots = call(
@@ -670,6 +727,7 @@
         lines,
         near_grad,
         history,
+        *others,
     )
     moves = [from_shot(move, turn) for turn in range(1, shots)]
     own = shape(rows, piece, width)

time: 69.3 us -> 66 us (0.952)
  waiting for transfers between devices: 11 us -> 8.8 us
  Pallas kernels: 20 us -> 17.9 us
  starting transfers between devices: 21.4 us -> 22.3 us
    ppermute x5, waiting for transfers between devices: 10.9 us -> 8.44 us  [from_shot(): lax.ppermute(value, 'shot', [((i + turn) % shots, i) for i in range(shots)])]
    pallas_call x21 -> x22, Pallas kernels: 20 us -> 17.9 us  [call(): pl.pallas_call(kernel, name=name, out_shape=outs, in_specs=specs or [VM]...]
    ppermute x4, starting transfers between devices: 12.6 us -> 13.8 us  [swap_core(): return lax.ppermute(value, 'depth', on_chip)]
  transfers between devices with their start and end apart: 13 -> 13, of which waited for: 3 -> 3; matrix products, arithmetic and copies ran while one was open for 0% -> 0% of each run, Pallas kernels for 24% -> 23%
where the time goes in v4:
time: 66 us; the launch traced here: 65.7 us
  starting transfers between devices  22.3 us (34%)
  Pallas kernels  17.9 us (27%)
  blocking collectives  15.1 us (23%)
  waiting for transfers between devices  8.8 us (13%)
  between operations  1.52 us (2%)
    pallas_call x22, Pallas kernels, call(): pl.pallas_call(kernel, name=name, out_shape=outs, in_specs=specs or [VM]...  17.9 us
    all_to_all x1, blocking collectives, per_device(): lines = lax.all_to_all(line, ('depth', 'shot'), 0, 0, tiled=True)  15.1 us
    ppermute x4, starting transfers between devices, swap_core(): return lax.ppermute(value, 'depth', on_chip)  13.8 us
    ppermute x5, waiting for transfers between devices, from_shot(): lax.ppermute(value, 'shot', [((i + turn) % shots, i) for i in range(shots)])  8.44 us
    ppermute x5, starting transfers between devices, from_shot(): lax.ppermute(value, 'shot', [((i + turn) % shots, i) for i in range(shots)])  5.83 us
    ppermute x4, starting transfers between devices, swap_chip(): return lax.ppermute(value, 'depth', off_chip)  2.7 us
  transfers between devices with their start and end apart: 13, of which 3 were waited for; matrix products, arithmetic and copies ran while one was open for 0% of the time, Pallas kernels for 23%

profile of v4, /device:TPU:0, one launch (start us, length us, event | category | flops | bytes accessed | tf_op | source)
XLA Modules:
  0.0 65.7 jit_solution(10742645482912727907)
XLA Ops:
  0.7 1.8 %stage.1 = (f32[16,80,128]{2,1,0:T(8,128)S(1)}, f32[16,80,128]{2,1,0:T(8,128)S(1)}, f32[16,64,128]{2,1,0:T(8,128)S(1)}, f32[16,64,128]{2,1,0:T(8,128)S(1)}, f32[...) custom-call(f32[16,64,128]{2,1,0:T(8,128)} %bitcast.12, ...), custom_call_target="tpu_custom_call" | custom-call | flops 1048576 | bytes 1048576 | tf_op jit(solution)/shard_map/stage/pallas_call | solution.py:537
  2.5 0.5 collective-permute-start.1
  3.0 0.7 %collective-permute-start = (f32[8,64,128]{2,1,0:T(8,128)S(1)}, f32[8,64,128]{2,1,0:T(8,128)S(1)}, u32[]{:S(2)}, u32[]{:S(2)}) collective-permute-start(f32[8,64,128]{2,1,0:T(8,128)S(1)} %get-tuple-element.69), channel_id=1, source_target_pairs={{2,4},{4,2},{6,8},{8,6},{10,12},{12,10},{14,16},{16,14},{18,20},{2... | collective-permute-start | bytes 786440 | tf_op jit(solution)/shard_map/ppermute | solution.py:577
  4.3 1.8 %receivers.2.injected = f32[4,1024,128]{2,1,0:T(8,128)S(1)} custom-call(s32[1,256]{1,0:T(1,128)S(1)} %copy-done.4, f32[4,256]{1,0:T(4,128)S(1)} %bitcast.11), custom_call_target="tpu_custom_call" | custom-call | flops 1048576 | bytes 1048576 | tf_op jit(solution)/shard_map/receivers/pallas_call | solution.py:537
  6.2 2.2 %local_0.1 = (f32[16,64,128]{2,1,0:T(8,128)S(1)}, f32[16,80,128]{2,1,0:T(8,128)S(1)}, f32[16,64,128]{2,1,0:T(8,128)S(1)}, f32[16,80,128]{2,1,0:T(8,128)S(1)}) custom-call(s32[1]{0:T(128)S(6)} %copy.64.cell, f32[1,4]{1,0:T(1,128)S(1)} %copy-done.2, f32[16,80,128]{2,1,0:T(8,128)S(1)} %get-tuple-element.72.wave.wave_old, ...), custom_call_target="tpu_custom_call" | custom-call | flops 1048576 | bytes 1048576 | tf_op jit(solution)/shard_map/local_0/pallas_call | solution.py:537
  8.4 0.0 collective-permute-done.1.halo._
  8.4 0.1 join_core_0.1
  8.5 3.9 %collective-permute-start.3 = (f32[8,64,128]{2,1,0:T(8,128)S(1)}, f32[8,64,128]{2,1,0:T(8,128)S(1)}, u32[]{:S(2)}, u32[]{:S(2)}) collective-permute-start(f32[8,64,128]{2,1,0:T(8,128)S(1)} %get-tuple-element.88), channel_id=1, source_target_pairs={{0,2},{2,0},{4,6},{6,4},{8,10},{10,8},{12,14},{14,12},{16,18},{18,... | collective-permute-start | bytes 786440 | tf_op jit(solution)/shard_map/ppermute | solution.py:574
  12.5 0.0 collective-permute-done.halo
  12.5 0.1 join_chip_0.1
  12.6 0.7 %collective-permute-start.2 = (f32[8,64,128]{2,1,0:T(8,128)S(1)}, f32[8,64,128]{2,1,0:T(8,128)S(1)}, u32[]{:S(2)}, u32[]{:S(2)}) collective-permute-start(f32[8,64,128]{2,1,0:T(8,128)S(1)} %get-tuple-element.87), channel_id=1, source_target_pairs={{2,4},{4,2},{6,8},{8,6},{10,12},{12,10},{14,16},{16,14},{18,20},{2... | collective-permute-start | bytes 786440 | tf_op jit(solution)/shard_map/ppermute | solution.py:577
  13.3 2.3 %local_1.1 = (f32[16,64,128]{2,1,0:T(8,128)S(1)}, f32[16,80,128]{2,1,0:T(8,128)S(1)}, f32[16,64,128]{2,1,0:T(8,128)S(1)}, f32[16,80,128]{2,1,0:T(8,128)S(1)}) custom-call(s32[1]{0:T(128)S(6)} %copy.64.cell, f32[1,4]{1,0:T(1,128)S(1)} %copy-done.2, f32[16,80,128]{2,1,0:T(8,128)S(1)} %get-tuple-element.89.wave.wave_old, ...), custom_call_target="tpu_custom_call" | custom-call | flops 1048576 | bytes 1048576 | tf_op jit(solution)/shard_map/local_1/pallas_call | solution.py:537
  15.6 0.1 join_core_1.1
  15.7 0.0 copy-start
  15.7 4.9 %collective-permute-start.5 = (f32[8,64,128]{2,1,0:T(8,128)S(1)}, f32[8,64,128]{2,1,0:T(8,128)S(1)}, u32[]{:S(2)}, u32[]{:S(2)}) collective-permute-start(f32[8,64,128]{2,1,0:T(8,128)S(1)} %get-tuple-element.101), channel_id=1, source_target_pairs={{0,2},{2,0},{4,6},{6,4},{8,10},{10,8},{12,14},{14,12},{16,18},{18,... | collective-permute-start | bytes 786440 | tf_op jit(solution)/shard_map/ppermute | solution.py:574
  20.6 1.1 %keep.1.refs_0_.refs_1_ = f32[2,5,4,32,128]{4,3,2,1,0:T(8,128)S(1)} custom-call(f32[2,5,16,32,128]{4,3,2,1,0:T(8,128)} %history.7, f32[8,64,128]{2,1,0:T(8,128)S(1)} %collective-permute-done.1.halo._), custom_call_target="tpu_custom_call" | custom-call | flops 1048576 | bytes 1048576 | tf_op jit(solution)/shard_map/keep/pallas_call | solution.py:537
  21.8 1.6 %collective-permute-start.10 = (f32[2,5,4,32,128]{4,3,2,1,0:T(8,128)S(1)}, f32[2,5,4,32,128]{4,3,2,1,0:T(8,128)S(1)}, u32[]{:S(2)}, u32[]{:S(2)}) collective-permute-start(f32[2,5,4,32,128]{4,3,2,1,0:T(8,128)S(1)} %keep.1.refs_0_.refs_1_), channel_id=1, source_target_pairs={{1,0},{0,1},{3,2},{2,3},{5,4},{4,5},{7,6},{6,7},{9,8},{8,9},{11,10... | collective-permute-start | bytes 1966088 | tf_op jit(solution)/shard_map/ppermute | solution.py:580
  23.3 0.0 collective-permute-done.2.halo
  23.3 0.1 join_chip_1.1
  23.5 0.7 %collective-permute-start.4 = (f32[8,64,128]{2,1,0:T(8,128)S(1)}, f32[8,64,128]{2,1,0:T(8,128)S(1)}, u32[]{:S(2)}, u32[]{:S(2)}) collective-permute-start(f32[8,64,128]{2,1,0:T(8,128)S(1)} %get-tuple-element.100), channel_id=1, source_target_pairs={{2,4},{4,2},{6,8},{8,6},{10,12},{12,10},{14,16},{16,14},{18,20},{2... | collective-permute-start | bytes 786440 | tf_op jit(solution)/shard_map/ppermute | solution.py:577
  24.2 0.7 %gram.1.outs_0_ = f32[30,8,128]{2,1,0:T(8,128)S(1)} custom-call(f32[2,5,16,32,128]{4,3,2,1,0:T(8,128)S(1)} %copy-done), custom_call_target="tpu_custom_call" | custom-call | flops 1048576 | bytes 1048576 | tf_op jit(solution)/shard_map/gram/pallas_call | solution.py:537
  24.9 2.4 %local_2.1 = (f32[16,64,128]{2,1,0:T(8,128)S(1)}, f32[16,80,128]{2,1,0:T(8,128)S(1)}, f32[16,64,128]{2,1,0:T(8,128)S(1)}, f32[16,80,128]{2,1,0:T(8,128)S(1)}) custom-call(s32[1]{0:T(128)S(6)} %copy.64.cell, f32[1,4]{1,0:T(1,128)S(1)} %copy-done.2, f32[16,80,128]{2,1,0:T(8,128)S(1)} %get-tuple-element.102.wave, ...), custom_call_target="tpu_custom_call" | custom-call | flops 1048576 | bytes 1048576 | tf_op jit(solution)/shard_map/local_2/pallas_call | solution.py:537
  27.3 0.0 collective-permute-done.5.halo
  27.3 0.1 join_core_2.1
  27.4 4.5 %collective-permute-start.7 = (f32[8,64,128]{2,1,0:T(8,128)S(1)}, f32[8,64,128]{2,1,0:T(8,128)S(1)}, u32[]{:S(2)}, u32[]{:S(2)}) collective-permute-start(f32[8,64,128]{2,1,0:T(8,128)S(1)} %get-tuple-element.123), channel_id=1, source_target_pairs={{0,2},{2,0},{4,6},{6,4},{8,10},{10,8},{12,14},{14,12},{16,18},{18,... | collective-permute-start | bytes 786440 | tf_op jit(solution)/shard_map/ppermute | solution.py:574
  31.9 0.0 collective-permute-done.4.halo
  31.9 0.1 join_chip_2.1
  32.0 0.7 %collective-permute-start.6 = (f32[8,64,128]{2,1,0:T(8,128)S(1)}, f32[8,64,128]{2,1,0:T(8,128)S(1)}, u32[]{:S(2)}, u32[]{:S(2)}) collective-permute-start(f32[8,64,128]{2,1,0:T(8,128)S(1)} %get-tuple-element.113), channel_id=1, source_target_pairs={{2,4},{4,2},{6,8},{8,6},{10,12},{12,10},{14,16},{16,14},{18,20},{2... | collective-permute-start | bytes 786440 | tf_op jit(solution)/shard_map/ppermute | solution.py:577
  32.7 0.3 collective-permute-done.7.from_core
  33.0 0.6 core.1
  33.6 1.0 %inner.1 = (f32[8,32,128]{2,1,0:T(8,128)S(1)}, f32[8,32,128]{2,1,0:T(8,128)S(1)}) custom-call(f32[4,32,128]{2,1,0:T(8,128)S(1)} %get-tuple-element.125._.refs_2_, f32[16,80,128]{2,1,0:T(8,128)S(1)} %get-tuple-element.114.wave, f32[16,80,128]{2,1,0:T(8,128)S(1)} %get-tuple-element.115.prod, f32[16,64,128]{2,1,0:T(8,128)S(1)} %get-tuple-element.116.adj, ...), custom_call_target="tpu_custom_call" | custom-call | flops 1048576 | bytes 1048576 | tf_op jit(solution)/shard_map/inner/pallas_call | solution.py:537
  34.6 1.6 %collective-permute-start.9 = (f32[8,32,128]{2,1,0:T(8,128)S(1)}, f32[8,32,128]{2,1,0:T(8,128)S(1)}, u32[]{:S(2)}, u32[]{:S(2)}) collective-permute-start(f32[8,32,128]{2,1,0:T(8,128)S(1)} %get-tuple-element.126), channel_id=1, source_target_pairs={{1,0},{0,1},{3,2},{2,3},{5,4},{4,5},{7,6},{6,7},{9,8},{8,9},{11,10... | collective-permute-start | bytes 393224 | tf_op jit(solution)/shard_map/ppermute | solution.py:580
  36.2 0.5 collective-permute-start.8
  36.7 0.5 chip.1
  37.3 3.5 %collective-permute-done.8.refs_0_.refs_3_ = f32[4,32,128]{2,1,0:T(8,128)S(1)} collective-permute-done((f32[4,32,128]{2,1,0:T(8,128)S(1)}, f32[4,32,128]{2,1,0:T(8,128)S(1)}, u32[]{:S(2)}, u32[]{:S(2)}) %collective-permute-start.8) | collective-permute-done | bytes 65568 | tf_op jit(solution)/shard_map/ppermute | solution.py:580
  40.7 0.1 last_join.1.grad.chip
  40.8 1.6 %collective-permute-start.11 = (f32[4,64,128]{2,1,0:T(8,128)S(1)}, f32[4,64,128]{2,1,0:T(8,128)S(1)}, u32[]{:S(2)}, u32[]{:S(2)}) collective-permute-start(f32[4,64,128]{2,1,0:T(8,128)S(1)} %last_join.1.grad.chip), channel_id=1, source_target_pairs={{1,0},{0,1},{3,2},{2,3},{5,4},{4,5},{7,6},{6,7},{9,8},{8,9},{11,10... | collective-permute-start | bytes 393224 | tf_op jit(solution)/shard_map/ppermute | solution.py:580
  42.4 0.0 collective-permute-done.10.refs_1_.refs_2_
  42.4 0.1 chip_dots.1.chip
  42.5 0.0 copy-start.1
  42.5 0.3 line.1
  42.9 15.1 %all_to_all.11 = f32[32,1,128]{2,1,0:T(1,128)S(1)} all-to-all(f32[32,1,128]{2,1,0:T(1,128)S(1)} %bitcast.10), channel_id=1, replica_groups=mesh['depth'=16,'shot'=2] {'depth','shot'}, dimensions={0} | all-to-all | bytes 32768 | tf_op jit(solution)/shard_map/all_to_all | solution.py:722
  58.0 0.0 collective-permute-done.11.refs_0_
  58.0 0.4 weights.1
  58.3 0.6 collective-permute-start.12
  58.9 1.1 %finish.1 = (f32[16,32,128]{2,1,0:T(8,128)}, f32[16,32,128]{2,1,0:T(8,128)}, f32[16,64,128]{2,1,0:T(8,128)}) custom-call(f32[11,8,128]{2,1,0:T(8,128)S(1)} %get-tuple-element.130.weight, f32[16,64,128]{2,1,0:T(8,128)S(1)} %copy-done.1, f32[12,32,128]{2,1,0:T(8,128)S(1)} %get-tuple-element.129.near, f32[12,32,128]{2,1,0:T(8,128)S(1)} %get-tuple-element.131.near_move, ...), custom_call_target="tpu_custom_call" | custom-call | flops 1048576 | bytes 1048576 | tf_op jit(solution)/shard_map/finish/pallas_call | solution.py:537
  60.0 5.0 %collective-permute-done.12.refs_0_ = f32[12,32,128]{2,1,0:T(8,128)S(1)} collective-permute-done((f32[12,32,128]{2,1,0:T(8,128)S(1)}, f32[12,32,128]{2,1,0:T(8,128)S(1)}, u32[]{:S(2)}, u32[]{:S(2)}) %collective-permute-start.12) | collective-permute-done | bytes 196640 | tf_op jit(solution)/shard_map/ppermute | solution.py:580
  65.0 0.7 %last_piece.1 = f32[16,64,128]{2,1,0:T(8,128)} custom-call(f32[16,64,128]{2,1,0:T(8,128)S(1)} %copy-done.1, f32[16,64,128]{2,1,0:T(8,128)} %get-tuple-element.134.done, f32[12,32,128]{2,1,0:T(8,128)S(1)} %collective-permute-done.12.refs_0_), custom_call_target="tpu_custom_call", output_to_operand_aliasing={{}: (1, {})} | custom-call | flops 1048576 | bytes 1048576 | tf_op jit(solution)/shard_map/last_piece/pallas_call | solution.py:537
  (11 shorter events, 0.0 us)
Async XLA Ops:
  0.6 3.7 %copy-start.3 = (f32[1,4,256]{2,1,0:T(4,128)S(1)}, f32[1,4,256]{2,1,0:T(4,128)}, u32[]{:S(2)}) copy-start(f32[1,4,256]{2,1,0:T(4,128)} %param.18) | copy-start | bytes 12292
  0.6 3.7 %copy-start.4 = (s32[1,256]{1,0:T(1,128)S(1)}, s32[1,256]{1,0:T(1,128)}, u32[]{:S(2)}) copy-start(s32[1,256]{1,0:T(1,128)} %receivers.3) | copy-start | bytes 3076
  0.7 5.5 %copy-start.2 = (f32[1,4]{1,0:T(1,128)S(1)}, f32[1,4]{1,0:T(1,128)}, u32[]{:S(2)}) copy-start(f32[1,4]{1,0:T(1,128)} %wavelet.5) | copy-start | bytes 52
  2.5 5.9 %collective-permute-start.1 = (f32[8,64,128]{2,1,0:T(8,128)S(1)}, f32[8,64,128]{2,1,0:T(8,128)S(1)}, u32[]{:S(2)}, u32[]{:S(2)}) collective-permute-start(f32[8,64,128]{2,1,0:T(8,128)S(1)} %get-tuple-element.71), channel_id=1, source_target_pairs={{0,2},{2,0},{4,6},{6,4},{8,10},{10,8},{12,14},{14,12},{16,18},{18,... | collective-permute-start | bytes 786440 | tf_op jit(solution)/shard_map/ppermute | solution.py:574
  3.0 9.5 %collective-permute-start = (f32[8,64,128]{2,1,0:T(8,128)S(1)}, f32[8,64,128]{2,1,0:T(8,128)S(1)}, u32[]{:S(2)}, u32[]{:S(2)}) collective-permute-start(f32[8,64,128]{2,1,0:T(8,128)S(1)} %get-tuple-element.69), channel_id=1, source_target_pairs={{2,4},{4,2},{6,8},{8,6},{10,12},{12,10},{14,16},{16,14},{18,20},{2... | collective-permute-start | bytes 786440 | tf_op jit(solution)/shard_map/ppermute | solution.py:577
  8.5 7.0 %collective-permute-start.3 = (f32[8,64,128]{2,1,0:T(8,128)S(1)}, f32[8,64,128]{2,1,0:T(8,128)S(1)}, u32[]{:S(2)}, u32[]{:S(2)}) collective-permute-start(f32[8,64,128]{2,1,0:T(8,128)S(1)} %get-tuple-element.88), channel_id=1, source_target_pairs={{0,2},{2,0},{4,6},{6,4},{8,10},{10,8},{12,14},{14,12},{16,18},{18,... | collective-permute-start | bytes 786440 | tf_op jit(solution)/shard_map/ppermute | solution.py:574
  12.6 10.7 %collective-permute-start.2 = (f32[8,64,128]{2,1,0:T(8,128)S(1)}, f32[8,64,128]{2,1,0:T(8,128)S(1)}, u32[]{:S(2)}, u32[]{:S(2)}) collective-permute-start(f32[8,64,128]{2,1,0:T(8,128)S(1)} %get-tuple-element.87), channel_id=1, source_target_pairs={{2,4},{4,2},{6,8},{8,6},{10,12},{12,10},{14,16},{16,14},{18,20},{2... | collective-permute-start | bytes 786440 | tf_op jit(solution)/shard_map/ppermute | solution.py:577
  15.7 8.5 %copy-start = (f32[2,5,16,32,128]{4,3,2,1,0:T(8,128)S(1)}, f32[2,5,16,32,128]{4,3,2,1,0:T(8,128)}, u32[]{:S(2)}) copy-start(f32[2,5,16,32,128]{4,3,2,1,0:T(8,128)} %history.7) | copy-start | bytes 7864324
  15.7 11.5 %collective-permute-start.5 = (f32[8,64,128]{2,1,0:T(8,128)S(1)}, f32[8,64,128]{2,1,0:T(8,128)S(1)}, u32[]{:S(2)}, u32[]{:S(2)}) collective-permute-start(f32[8,64,128]{2,1,0:T(8,128)S(1)} %get-tuple-element.101), channel_id=1, source_target_pairs={{0,2},{2,0},{4,6},{6,4},{8,10},{10,8},{12,14},{14,12},{16,18},{18,... | collective-permute-start | bytes 786440 | tf_op jit(solution)/shard_map/ppermute | solution.py:574
  21.8 20.7 %collective-permute-start.10 = (f32[2,5,4,32,128]{4,3,2,1,0:T(8,128)S(1)}, f32[2,5,4,32,128]{4,3,2,1,0:T(8,128)S(1)}, u32[]{:S(2)}, u32[]{:S(2)}) collective-permute-start(f32[2,5,4,32,128]{4,3,2,1,0:T(8,128)S(1)} %keep.1.refs_0_.refs_1_), channel_id=1, source_target_pairs={{1,0},{0,1},{3,2},{2,3},{5,4},{4,5},{7,6},{6,7},{9,8},{8,9},{11,10... | collective-permute-start | bytes 1966088 | tf_op jit(solution)/shard_map/ppermute | solution.py:580
  23.5 8.4 %collective-permute-start.4 = (f32[8,64,128]{2,1,0:T(8,128)S(1)}, f32[8,64,128]{2,1,0:T(8,128)S(1)}, u32[]{:S(2)}, u32[]{:S(2)}) collective-permute-start(f32[8,64,128]{2,1,0:T(8,128)S(1)} %get-tuple-element.100), channel_id=1, source_target_pairs={{2,4},{4,2},{6,8},{8,6},{10,12},{12,10},{14,16},{16,14},{18,20},{2... | collective-permute-start | bytes 786440 | tf_op jit(solution)/shard_map/ppermute | solution.py:577
  27.4 5.6 %collective-permute-start.7 = (f32[8,64,128]{2,1,0:T(8,128)S(1)}, f32[8,64,128]{2,1,0:T(8,128)S(1)}, u32[]{:S(2)}, u32[]{:S(2)}) collective-permute-start(f32[8,64,128]{2,1,0:T(8,128)S(1)} %get-tuple-element.123), channel_id=1, source_target_pairs={{0,2},{2,0},{4,6},{6,4},{8,10},{10,8},{12,14},{14,12},{16,18},{18,... | collective-permute-start | bytes 786440 | tf_op jit(solution)/shard_map/ppermute | solution.py:574
  32.0 5.2 %collective-permute-start.6 = (f32[8,64,128]{2,1,0:T(8,128)S(1)}, f32[8,64,128]{2,1,0:T(8,128)S(1)}, u32[]{:S(2)}, u32[]{:S(2)}) collective-permute-start(f32[8,64,128]{2,1,0:T(8,128)S(1)} %get-tuple-element.113), channel_id=1, source_target_pairs={{2,4},{4,2},{6,8},{8,6},{10,12},{12,10},{14,16},{16,14},{18,20},{2... | collective-permute-start | bytes 786440 | tf_op jit(solution)/shard_map/ppermute | solution.py:577
  34.6 6.1 %collective-permute-start.9 = (f32[8,32,128]{2,1,0:T(8,128)S(1)}, f32[8,32,128]{2,1,0:T(8,128)S(1)}, u32[]{:S(2)}, u32[]{:S(2)}) collective-permute-start(f32[8,32,128]{2,1,0:T(8,128)S(1)} %get-tuple-element.126), channel_id=1, source_target_pairs={{1,0},{0,1},{3,2},{2,3},{5,4},{4,5},{7,6},{6,7},{9,8},{8,9},{11,10... | collective-permute-start | bytes 393224 | tf_op jit(solution)/shard_map/ppermute | solution.py:580
  36.2 4.5 %collective-permute-start.8 = (f32[4,32,128]{2,1,0:T(8,128)S(1)}, f32[4,32,128]{2,1,0:T(8,128)S(1)}, u32[]{:S(2)}, u32[]{:S(2)}) collective-permute-start(f32[4,32,128]{2,1,0:T(8,128)S(1)} %get-tuple-element.124), channel_id=1, source_target_pairs={{1,0},{0,1},{3,2},{2,3},{5,4},{4,5},{7,6},{6,7},{9,8},{8,9},{11,10... | collective-permute-start | bytes 196616 | tf_op jit(solution)/shard_map/ppermute | solution.py:580
  40.8 17.1 %collective-permute-start.11 = (f32[4,64,128]{2,1,0:T(8,128)S(1)}, f32[4,64,128]{2,1,0:T(8,128)S(1)}, u32[]{:S(2)}, u32[]{:S(2)}) collective-permute-start(f32[4,64,128]{2,1,0:T(8,128)S(1)} %last_join.1.grad.chip), channel_id=1, source_target_pairs={{1,0},{0,1},{3,2},{2,3},{5,4},{4,5},{7,6},{6,7},{9,8},{8,9},{11,10... | collective-permute-start | bytes 393224 | tf_op jit(solution)/shard_map/ppermute | solution.py:580
  42.5 16.4 %copy-start.1 = (f32[16,64,128]{2,1,0:T(8,128)S(1)}, f32[16,64,128]{2,1,0:T(8,128)}, u32[]{:S(2)}) copy-start(f32[16,64,128]{2,1,0:T(8,128)} %courant.5) | copy-start | bytes 1572868
  58.3 6.7 %collective-permute-start.12 = (f32[12,32,128]{2,1,0:T(8,128)S(1)}, f32[12,32,128]{2,1,0:T(8,128)S(1)}, u32[]{:S(2)}, u32[]{:S(2)}) collective-permute-start(f32[12,32,128]{2,1,0:T(8,128)S(1)} %get-tuple-element.131.near_move), channel_id=1, source_target_pairs={{1,0},{0,1},{3,2},{2,3},{5,4},{4,5},{7,6},{6,7},{9,8},{8,9},{11,10... | collective-permute-start | bytes 589832 | tf_op jit(solution)/shard_map/ppermute | solution.py:580

commit v5 on v4

--- a/solution.py
+++ b/solution.py
@@ -98,6 +98,24 @@
         ref[row, padded - PAD :, :] = jnp.zeros((PAD, width), F32)
 
 
+def first_send_kernel(wave, adjoint, courant, to_chip, to_core, b_wave, b_adj, b_cour, sems):
+    rows = courant.shape[0]
+    odd = odd_depth()
+    copies = []
+    for which, start in enumerate((odd * (rows - REACH), (1 - odd) * (rows - REACH))):
+        for n, (src, dst) in enumerate([(wave, b_wave), (adjoint, b_adj), (courant, b_cour)]):
+            copies.append(pltpu.make_async_copy(src.at[pl.ds(start, REACH)], dst.at[which], sems.at[3 * which + n]))
+    for copy in copies:
+        copy.start()
+    for copy in copies:
+        copy.wait()
+    for which, send in enumerate((to_chip, to_core)):
+        for row in range(REACH):
+            src = natural_row(row, REACH, odd)
+            send[row] = b_wave[which, src]
+            send[REACH + row] = b_cour[which, src] * b_adj[which, src]
+
+
 def stage_kernel(
     wave,
     wave_old,
@@ -110,8 +128,6 @@
     o_adj_old,
     o_cour,
     o_prod,
-    to_core,
-    to_chip,
     o_wide,
     o_tall,
     b_wave,
@@ -141,12 +157,6 @@
         o_adj[row] = adj
         o_cour[row] = cour
         o_prod[row, PAD : PAD + across, :] = prod
-        if row < REACH:
-            to_chip[row] = now
-            to_chip[REACH + row] = prod
-        if row >= rows - REACH:
-            to_core[row - (rows - REACH)] = now
-            to_core[row - (rows - REACH) + REACH] = prod
     for copy in copies[3:]:
         copy.wait()
     for row in range(rows):
@@ -306,9 +316,8 @@
     lay_pieces(full, outs[:-3])
 
 
-def chip_kernel(
-    wave, prod, adj, adj_old, injected, wide, tall, lap1, lap2, lap3, adj4, adj3, o_known, o_lap, o_adj, *along
-):
+def chip_kernel(wave, prod, adj, adj_old, injected, wide, tall, lap1, lap2, lap3, adj4, adj3, *refs):
+    o_known, o_lap, o_adj, *along = refs[-5:]
     which = list(range(REACH))
     for place, row, start, part, lap, new in last_rows(which, wave, prod, adj, adj_old, injected, wide, tall, *along):
         o_known[part] = known_terms(part, adj, lap2, lap3, adj3)
@@ -379,7 +388,7 @@
 
 
 def chip_dots_kernel(count, grad, *refs):
-    pieces, out = refs[:count], refs[count]
+    pieces, out = refs[:count], refs[-1]
     total, piece = grad.shape[0], pieces[0].shape[3]
     odd = odd_depth()
     sums = [jnp.zeros((8, grad.shape[2]), F32) for _ in range(2 * PAIRS)]
@@ -585,16 +594,27 @@
         for value in (wave_current[0], wave_before[0], adjoint_current[0], adjoint_after[0], courant, history)
     ]
     bands = [jax.ShapeDtypeStruct((2 * width, n * width), jnp.bfloat16) for n in (2, 1)]
-    wave, wave_old, adj, adj_old, cour, prod, to_core, to_chip, *bands = call(
+    outer_rows = pltpu.VMEM((2, REACH, across, width), F32)
+    to_chip, to_core = call(
+        first_send_kernel,
+        "first_send",
+        [halo, halo],
+        held[0],
+        held[2],
+        held[4],
+        specs=[HB] * 3,
+        scratch=[outer_rows] * 3 + [pltpu.SemaphoreType.DMA((6,))],
+    )
+    from_chip = swap_chip(to_chip)
+    from_core = swap_core(to_core)
+    wave, wave_old, adj, adj_old, cour, prod, *bands = call(
         stage_kernel,
         "stage",
-        [padded, padded, slab, slab, slab, padded, halo, halo] + bands,
+        [padded, padded, slab, slab, slab, padded] + bands,
         *held[:5],
         specs=[HB] * 5,
         scratch=[block] * 5 + [pltpu.SemaphoreType.DMA((5,))],
     )
-    from_chip = swap_chip(to_chip)
-    from_core = swap_core(to_core)
     kept = call(
         keep_kernel,
         "keep",
@@ -686,7 +706,7 @@
     )
     core, inner = sum_parts(core), sum_parts(inner)
     chip_part = shape(REACH, across, width)
-    known, lap, new_adj = call(chip_kernel, "chip", [chip_part] * 3, *last, scratch=some_rows(REACH, 2))
+    known, lap, new_adj = call(chip_kernel, "chip", [chip_part] * 3, *last, *kept[1:], scratch=some_rows(REACH, 2))
     chip = call(
         functools.partial(last_join_kernel, scale),
         "last_join",
@@ -698,7 +718,6 @@
         laps[0],
         adjs[0],
         *core[1:],
-        *inner[1:],
     )
     others = [from_shot(chip, turn) for turn in range(1, shots)]
     chip_dots = call(
@@ -707,6 +726,7 @@
         shape(2 * PAIRS, 8, width),
         chip,
         *kept,
+        *inner[1:],
     )
     near = shape(near_count, piece, width)
     line, near_grad = call(

time: 66 us -> 65.5 us (level)
  starting transfers between devices: 22.3 us -> 20.9 us
  Pallas kernels: 17.9 us -> 19.2 us
  waiting for transfers between devices: 8.8 us -> 7.57 us
  blocking collectives: 15.1 us -> 15.9 us
    ppermute x4, starting transfers between devices: 13.8 us -> 12.3 us  [swap_core(): return lax.ppermute(value, 'depth', on_chip)]
    pallas_call x22 -> x23, Pallas kernels: 17.9 us -> 19.2 us  [call(): pl.pallas_call(kernel, name=name, out_shape=outs, in_specs=specs or [VM]...]
    ppermute x5, waiting for transfers between devices: 8.44 us -> 7.22 us  [from_shot(): lax.ppermute(value, 'shot', [((i + turn) % shots, i) for i in range(shots)])]
    all_to_all x1, blocking collectives: 15.1 us -> 15.9 us  [per_device(): lines = lax.all_to_all(line, ('depth', 'shot'), 0, 0, tiled=True)]
  transfers between devices with their start and end apart: 13 -> 13, of which waited for: 3 -> 4; matrix products, arithmetic and copies ran while one was open for 0% -> 0% of each run, Pallas kernels for 23% -> 26%
where the time goes in v5:
time: 65.5 us; the launch traced here: 65.2 us
  starting transfers between devices  20.9 us (32%)
  Pallas kernels  19.2 us (29%)
  blocking collectives  15.9 us (24%)
  waiting for transfers between devices  7.57 us (12%)
  between operations  1.52 us (2%)
    pallas_call x23, Pallas kernels, call(): pl.pallas_call(kernel, name=name, out_shape=outs, in_specs=specs or [VM]...  19.2 us
    all_to_all x1, blocking collectives, per_device(): lines = lax.all_to_all(line, ('depth', 'shot'), 0, 0, tiled=True)  15.9 us
    ppermute x4, starting transfers between devices, swap_core(): return lax.ppermute(value, 'depth', on_chip)  12.3 us
    ppermute x5, waiting for transfers between devices, from_shot(): lax.ppermute(value, 'shot', [((i + turn) % shots, i) for i in range(shots)])  7.22 us
    ppermute x5, starting transfers between devices, from_shot(): lax.ppermute(value, 'shot', [((i + turn) % shots, i) for i in range(shots)])  5.91 us
    ppermute x4, starting transfers between devices, swap_chip(): return lax.ppermute(value, 'depth', off_chip)  2.7 us
  transfers between devices with their start and end apart: 13, of which 4 were waited for; matrix products, arithmetic and copies ran while one was open for 0% of the time, Pallas kernels for 26%

profile of v5, /device:TPU:0, one launch (start us, length us, event | category | flops | bytes accessed | tf_op | source)
XLA Modules:
  0.0 65.2 jit_solution(1800863315663753013)
XLA Ops:
  0.7 1.3 %first_send.1 = (f32[8,64,128]{2,1,0:T(8,128)S(1)}, f32[8,64,128]{2,1,0:T(8,128)S(1)}) custom-call(f32[16,64,128]{2,1,0:T(8,128)} %bitcast.12, f32[16,64,128]{2,1,0:T(8,128)} %bitcast.14, f32[16,64,128]{2,1,0:T(8,128)} %courant.7), custom_call_target="tpu_custom_call" | custom-call | flops 1048576 | bytes 1048576 | tf_op jit(solution)/shard_map/first_send/pallas_call | solution.py:546
  2.0 0.0 copy-start.2
  2.0 0.5 collective-permute-start.1
  2.5 0.7 %collective-permute-start = (f32[8,64,128]{2,1,0:T(8,128)S(1)}, f32[8,64,128]{2,1,0:T(8,128)S(1)}, u32[]{:S(2)}, u32[]{:S(2)}) collective-permute-start(f32[8,64,128]{2,1,0:T(8,128)S(1)} %get-tuple-element.69), channel_id=1, source_target_pairs={{2,4},{4,2},{6,8},{8,6},{10,12},{12,10},{14,16},{16,14},{18,20},{2... | collective-permute-start | bytes 786440 | tf_op jit(solution)/shard_map/ppermute | solution.py:586
  3.8 1.8 %stage.1 = (f32[16,80,128]{2,1,0:T(8,128)S(1)}, f32[16,80,128]{2,1,0:T(8,128)S(1)}, f32[16,64,128]{2,1,0:T(8,128)S(1)}, f32[16,64,128]{2,1,0:T(8,128)S(1)}, f32[...) custom-call(f32[16,64,128]{2,1,0:T(8,128)} %bitcast.13, ...), custom_call_target="tpu_custom_call" | custom-call | flops 1048576 | bytes 1048576 | tf_op jit(solution)/shard_map/stage/pallas_call | solution.py:546
  5.6 1.8 %receivers.2.injected = f32[4,1024,128]{2,1,0:T(8,128)S(1)} custom-call(s32[1,256]{1,0:T(1,128)S(1)} %copy-done.4, f32[4,256]{1,0:T(4,128)S(1)} %bitcast.11), custom_call_target="tpu_custom_call" | custom-call | flops 1048576 | bytes 1048576 | tf_op jit(solution)/shard_map/receivers/pallas_call | solution.py:546
  7.5 2.2 %local_0.1 = (f32[16,64,128]{2,1,0:T(8,128)S(1)}, f32[16,80,128]{2,1,0:T(8,128)S(1)}, f32[16,64,128]{2,1,0:T(8,128)S(1)}, f32[16,80,128]{2,1,0:T(8,128)S(1)}) custom-call(s32[1]{0:T(128)S(6)} %copy.64.cell, f32[1,4]{1,0:T(1,128)S(1)} %copy-done.2, f32[16,80,128]{2,1,0:T(8,128)S(1)} %get-tuple-element.72.wave.wave_old, ...), custom_call_target="tpu_custom_call" | custom-call | flops 1048576 | bytes 1048576 | tf_op jit(solution)/shard_map/local_0/pallas_call | solution.py:546
  9.7 0.0 collective-permute-done.1.halo._
  9.7 0.1 join_core_0.1
  9.9 3.9 %collective-permute-start.3 = (f32[8,64,128]{2,1,0:T(8,128)S(1)}, f32[8,64,128]{2,1,0:T(8,128)S(1)}, u32[]{:S(2)}, u32[]{:S(2)}) collective-permute-start(f32[8,64,128]{2,1,0:T(8,128)S(1)} %get-tuple-element.88), channel_id=1, source_target_pairs={{0,2},{2,0},{4,6},{6,4},{8,10},{10,8},{12,14},{14,12},{16,18},{18,... | collective-permute-start | bytes 786440 | tf_op jit(solution)/shard_map/ppermute | solution.py:583
  13.8 0.0 collective-permute-done.halo
  13.8 0.1 join_chip_0.1
  13.9 0.7 %collective-permute-start.2 = (f32[8,64,128]{2,1,0:T(8,128)S(1)}, f32[8,64,128]{2,1,0:T(8,128)S(1)}, u32[]{:S(2)}, u32[]{:S(2)}) collective-permute-start(f32[8,64,128]{2,1,0:T(8,128)S(1)} %get-tuple-element.87), channel_id=1, source_target_pairs={{2,4},{4,2},{6,8},{8,6},{10,12},{12,10},{14,16},{16,14},{18,20},{2... | collective-permute-start | bytes 786440 | tf_op jit(solution)/shard_map/ppermute | solution.py:586
  14.6 1.1 %keep.1.refs_0_.refs_1_ = f32[2,5,4,32,128]{4,3,2,1,0:T(8,128)S(1)} custom-call(f32[2,5,16,32,128]{4,3,2,1,0:T(8,128)} %history.7, f32[8,64,128]{2,1,0:T(8,128)S(1)} %collective-permute-done.1.halo._), custom_call_target="tpu_custom_call" | custom-call | flops 1048576 | bytes 1048576 | tf_op jit(solution)/shard_map/keep/pallas_call | solution.py:546
  15.7 1.6 %collective-permute-start.7 = (f32[2,5,4,32,128]{4,3,2,1,0:T(8,128)S(1)}, f32[2,5,4,32,128]{4,3,2,1,0:T(8,128)S(1)}, u32[]{:S(2)}, u32[]{:S(2)}) collective-permute-start(f32[2,5,4,32,128]{4,3,2,1,0:T(8,128)S(1)} %keep.1.refs_0_.refs_1_), channel_id=1, source_target_pairs={{1,0},{0,1},{3,2},{2,3},{5,4},{4,5},{7,6},{6,7},{9,8},{8,9},{11,10... | collective-permute-start | bytes 1966088 | tf_op jit(solution)/shard_map/ppermute | solution.py:589
  17.3 2.2 %local_1.1 = (f32[16,64,128]{2,1,0:T(8,128)S(1)}, f32[16,80,128]{2,1,0:T(8,128)S(1)}, f32[16,64,128]{2,1,0:T(8,128)S(1)}, f32[16,80,128]{2,1,0:T(8,128)S(1)}) custom-call(s32[1]{0:T(128)S(6)} %copy.64.cell, f32[1,4]{1,0:T(1,128)S(1)} %copy-done.2, f32[16,80,128]{2,1,0:T(8,128)S(1)} %get-tuple-element.89.wave.wave_old, ...), custom_call_target="tpu_custom_call" | custom-call | flops 1048576 | bytes 1048576 | tf_op jit(solution)/shard_map/local_1/pallas_call | solution.py:546
  19.5 0.0 copy-start
  19.5 0.1 join_core_1.1
  19.7 2.8 %collective-permute-start.5 = (f32[8,64,128]{2,1,0:T(8,128)S(1)}, f32[8,64,128]{2,1,0:T(8,128)S(1)}, u32[]{:S(2)}, u32[]{:S(2)}) collective-permute-start(f32[8,64,128]{2,1,0:T(8,128)S(1)} %get-tuple-element.101), channel_id=1, source_target_pairs={{0,2},{2,0},{4,6},{6,4},{8,10},{10,8},{12,14},{14,12},{16,18},{18,... | collective-permute-start | bytes 786440 | tf_op jit(solution)/shard_map/ppermute | solution.py:583
  22.5 0.0 collective-permute-done.2.halo
  22.5 0.1 join_chip_1.1
  22.7 0.7 %collective-permute-start.4 = (f32[8,64,128]{2,1,0:T(8,128)S(1)}, f32[8,64,128]{2,1,0:T(8,128)S(1)}, u32[]{:S(2)}, u32[]{:S(2)}) collective-permute-start(f32[8,64,128]{2,1,0:T(8,128)S(1)} %get-tuple-element.100), channel_id=1, source_target_pairs={{2,4},{4,2},{6,8},{8,6},{10,12},{12,10},{14,16},{16,14},{18,20},{2... | collective-permute-start | bytes 786440 | tf_op jit(solution)/shard_map/ppermute | solution.py:586
  23.4 0.7 %gram.1.outs_0_ = f32[30,8,128]{2,1,0:T(8,128)S(1)} custom-call(f32[2,5,16,32,128]{4,3,2,1,0:T(8,128)S(1)} %copy-done), custom_call_target="tpu_custom_call" | custom-call | flops 1048576 | bytes 1048576 | tf_op jit(solution)/shard_map/gram/pallas_call | solution.py:546
  24.1 2.4 %local_2.1 = (f32[16,64,128]{2,1,0:T(8,128)S(1)}, f32[16,80,128]{2,1,0:T(8,128)S(1)}, f32[16,64,128]{2,1,0:T(8,128)S(1)}, f32[16,80,128]{2,1,0:T(8,128)S(1)}) custom-call(s32[1]{0:T(128)S(6)} %copy.64.cell, f32[1,4]{1,0:T(1,128)S(1)} %copy-done.2, f32[16,80,128]{2,1,0:T(8,128)S(1)} %get-tuple-element.102.wave, ...), custom_call_target="tpu_custom_call" | custom-call | flops 1048576 | bytes 1048576 | tf_op jit(solution)/shard_map/local_2/pallas_call | solution.py:546
  26.4 0.1 join_core_2.1
  26.6 5.0 %collective-permute-start.8 = (f32[8,64,128]{2,1,0:T(8,128)S(1)}, f32[8,64,128]{2,1,0:T(8,128)S(1)}, u32[]{:S(2)}, u32[]{:S(2)}) collective-permute-start(f32[8,64,128]{2,1,0:T(8,128)S(1)} %get-tuple-element.123), channel_id=1, source_target_pairs={{0,2},{2,0},{4,6},{6,4},{8,10},{10,8},{12,14},{14,12},{16,18},{18,... | collective-permute-start | bytes 786440 | tf_op jit(solution)/shard_map/ppermute | solution.py:583
  31.6 0.1 join_chip_2.1
  31.8 0.7 %collective-permute-start.6 = (f32[8,64,128]{2,1,0:T(8,128)S(1)}, f32[8,64,128]{2,1,0:T(8,128)S(1)}, u32[]{:S(2)}, u32[]{:S(2)}) collective-permute-start(f32[8,64,128]{2,1,0:T(8,128)S(1)} %get-tuple-element.113), channel_id=1, source_target_pairs={{2,4},{4,2},{6,8},{8,6},{10,12},{12,10},{14,16},{16,14},{18,20},{2... | collective-permute-start | bytes 786440 | tf_op jit(solution)/shard_map/ppermute | solution.py:586
  32.4 0.3 collective-permute-done.8.from_core
  32.8 0.6 core.1
  33.4 1.6 %collective-permute-start.9 = (f32[4,32,128]{2,1,0:T(8,128)S(1)}, f32[4,32,128]{2,1,0:T(8,128)S(1)}, u32[]{:S(2)}, u32[]{:S(2)}) collective-permute-start(f32[4,32,128]{2,1,0:T(8,128)S(1)} %get-tuple-element.124), channel_id=1, source_target_pairs={{1,0},{0,1},{3,2},{2,3},{5,4},{4,5},{7,6},{6,7},{9,8},{8,9},{11,10... | collective-permute-start | bytes 196616 | tf_op jit(solution)/shard_map/ppermute | solution.py:589
  35.0 1.0 %inner.1 = (f32[8,32,128]{2,1,0:T(8,128)S(1)}, f32[8,32,128]{2,1,0:T(8,128)S(1)}) custom-call(f32[4,32,128]{2,1,0:T(8,128)S(1)} %get-tuple-element.125._.refs_2_, f32[16,80,128]{2,1,0:T(8,128)S(1)} %get-tuple-element.114.wave, f32[16,80,128]{2,1,0:T(8,128)S(1)} %get-tuple-element.115.prod, f32[16,64,128]{2,1,0:T(8,128)S(1)} %get-tuple-element.116.adj, ...), custom_call_target="tpu_custom_call" | custom-call | flops 1048576 | bytes 1048576 | tf_op jit(solution)/shard_map/inner/pallas_call | solution.py:546
  36.0 0.6 collective-permute-start.10
  36.5 0.5 chip.1
  37.0 0.0 collective-permute-done.6.from_chip
  37.1 0.6 collective-permute-done.9.refs_0_.refs_3_
  37.7 0.1 last_join.1.grad.chip
  37.8 1.6 %collective-permute-start.11 = (f32[4,64,128]{2,1,0:T(8,128)S(1)}, f32[4,64,128]{2,1,0:T(8,128)S(1)}, u32[]{:S(2)}, u32[]{:S(2)}) collective-permute-start(f32[4,64,128]{2,1,0:T(8,128)S(1)} %last_join.1.grad.chip), channel_id=1, source_target_pairs={{1,0},{0,1},{3,2},{2,3},{5,4},{4,5},{7,6},{6,7},{9,8},{8,9},{11,10... | collective-permute-start | bytes 393224 | tf_op jit(solution)/shard_map/ppermute | solution.py:589
  39.4 1.6 %collective-permute-done.10.refs_2_.refs_1_ = f32[8,32,128]{2,1,0:T(8,128)S(1)} collective-permute-done((f32[8,32,128]{2,1,0:T(8,128)S(1)}, f32[8,32,128]{2,1,0:T(8,128)S(1)}, u32[]{:S(2)}, u32[]{:S(2)}) %collective-permute-start.10) | collective-permute-done | bytes 131104 | tf_op jit(solution)/shard_map/ppermute | solution.py:589
  41.0 0.1 chip_dots.1.chip
  41.1 0.0 copy-start.1
  41.1 0.3 line.1
  41.5 15.9 %all_to_all.11 = f32[32,1,128]{2,1,0:T(1,128)S(1)} all-to-all(f32[32,1,128]{2,1,0:T(1,128)S(1)} %bitcast.10), channel_id=1, replica_groups=mesh['depth'=16,'shot'=2] {'depth','shot'}, dimensions={0} | all-to-all | bytes 32768 | tf_op jit(solution)/shard_map/all_to_all | solution.py:742
  57.4 0.3 weights.1
  57.8 0.6 collective-permute-start.12
  58.3 1.1 %finish.1 = (f32[16,32,128]{2,1,0:T(8,128)}, f32[16,32,128]{2,1,0:T(8,128)}, f32[16,64,128]{2,1,0:T(8,128)}) custom-call(f32[11,8,128]{2,1,0:T(8,128)S(1)} %get-tuple-element.130.weight, f32[16,64,128]{2,1,0:T(8,128)S(1)} %copy-done.1, f32[12,32,128]{2,1,0:T(8,128)S(1)} %get-tuple-element.129.near, f32[12,32,128]{2,1,0:T(8,128)S(1)} %get-tuple-element.131.near_move, ...), custom_call_target="tpu_custom_call" | custom-call | flops 1048576 | bytes 1048576 | tf_op jit(solution)/shard_map/finish/pallas_call | solution.py:546
  59.5 4.9 %collective-permute-done.12.refs_0_ = f32[12,32,128]{2,1,0:T(8,128)S(1)} collective-permute-done((f32[12,32,128]{2,1,0:T(8,128)S(1)}, f32[12,32,128]{2,1,0:T(8,128)S(1)}, u32[]{:S(2)}, u32[]{:S(2)}) %collective-permute-start.12) | collective-permute-done | bytes 196640 | tf_op jit(solution)/shard_map/ppermute | solution.py:589
  64.4 0.7 %last_piece.1 = f32[16,64,128]{2,1,0:T(8,128)} custom-call(f32[16,64,128]{2,1,0:T(8,128)S(1)} %copy-done.1, f32[16,64,128]{2,1,0:T(8,128)} %get-tuple-element.134.done, f32[12,32,128]{2,1,0:T(8,128)S(1)} %collective-permute-done.12.refs_0_), custom_call_target="tpu_custom_call", output_to_operand_aliasing={{}: (1, {})} | custom-call | flops 1048576 | bytes 1048576 | tf_op jit(solution)/shard_map/last_piece/pallas_call | solution.py:546
  (12 shorter events, 0.0 us)
Async XLA Ops:
  0.6 5.0 %copy-start.3 = (f32[1,4,256]{2,1,0:T(4,128)S(1)}, f32[1,4,256]{2,1,0:T(4,128)}, u32[]{:S(2)}) copy-start(f32[1,4,256]{2,1,0:T(4,128)} %param.18) | copy-start | bytes 12292
  0.6 5.0 %copy-start.4 = (s32[1,256]{1,0:T(1,128)S(1)}, s32[1,256]{1,0:T(1,128)}, u32[]{:S(2)}) copy-start(s32[1,256]{1,0:T(1,128)} %receivers.3) | copy-start | bytes 3076
  2.0 5.5 %copy-start.2 = (f32[1,4]{1,0:T(1,128)S(1)}, f32[1,4]{1,0:T(1,128)}, u32[]{:S(2)}) copy-start(f32[1,4]{1,0:T(1,128)} %wavelet.5) | copy-start | bytes 52
  2.0 7.7 %collective-permute-start.1 = (f32[8,64,128]{2,1,0:T(8,128)S(1)}, f32[8,64,128]{2,1,0:T(8,128)S(1)}, u32[]{:S(2)}, u32[]{:S(2)}) collective-permute-start(f32[8,64,128]{2,1,0:T(8,128)S(1)} %get-tuple-element.71), channel_id=1, source_target_pairs={{0,2},{2,0},{4,6},{6,4},{8,10},{10,8},{12,14},{14,12},{16,18},{18,... | collective-permute-start | bytes 786440 | tf_op jit(solution)/shard_map/ppermute | solution.py:583
  2.5 11.3 %collective-permute-start = (f32[8,64,128]{2,1,0:T(8,128)S(1)}, f32[8,64,128]{2,1,0:T(8,128)S(1)}, u32[]{:S(2)}, u32[]{:S(2)}) collective-permute-start(f32[8,64,128]{2,1,0:T(8,128)S(1)} %get-tuple-element.69), channel_id=1, source_target_pairs={{2,4},{4,2},{6,8},{8,6},{10,12},{12,10},{14,16},{16,14},{18,20},{2... | collective-permute-start | bytes 786440 | tf_op jit(solution)/shard_map/ppermute | solution.py:586
  9.9 9.6 %collective-permute-start.3 = (f32[8,64,128]{2,1,0:T(8,128)S(1)}, f32[8,64,128]{2,1,0:T(8,128)S(1)}, u32[]{:S(2)}, u32[]{:S(2)}) collective-permute-start(f32[8,64,128]{2,1,0:T(8,128)S(1)} %get-tuple-element.88), channel_id=1, source_target_pairs={{0,2},{2,0},{4,6},{6,4},{8,10},{10,8},{12,14},{14,12},{16,18},{18,... | collective-permute-start | bytes 786440 | tf_op jit(solution)/shard_map/ppermute | solution.py:583
  13.9 8.6 %collective-permute-start.2 = (f32[8,64,128]{2,1,0:T(8,128)S(1)}, f32[8,64,128]{2,1,0:T(8,128)S(1)}, u32[]{:S(2)}, u32[]{:S(2)}) collective-permute-start(f32[8,64,128]{2,1,0:T(8,128)S(1)} %get-tuple-element.87), channel_id=1, source_target_pairs={{2,4},{4,2},{6,8},{8,6},{10,12},{12,10},{14,16},{16,14},{18,20},{2... | collective-permute-start | bytes 786440 | tf_op jit(solution)/shard_map/ppermute | solution.py:586
  15.7 20.8 %collective-permute-start.7 = (f32[2,5,4,32,128]{4,3,2,1,0:T(8,128)S(1)}, f32[2,5,4,32,128]{4,3,2,1,0:T(8,128)S(1)}, u32[]{:S(2)}, u32[]{:S(2)}) collective-permute-start(f32[2,5,4,32,128]{4,3,2,1,0:T(8,128)S(1)} %keep.1.refs_0_.refs_1_), channel_id=1, source_target_pairs={{1,0},{0,1},{3,2},{2,3},{5,4},{4,5},{7,6},{6,7},{9,8},{8,9},{11,10... | collective-permute-start | bytes 1966088 | tf_op jit(solution)/shard_map/ppermute | solution.py:589
  19.5 3.8 %copy-start = (f32[2,5,16,32,128]{4,3,2,1,0:T(8,128)S(1)}, f32[2,5,16,32,128]{4,3,2,1,0:T(8,128)}, u32[]{:S(2)}) copy-start(f32[2,5,16,32,128]{4,3,2,1,0:T(8,128)} %history.7) | copy-start | bytes 7864324
  19.7 6.8 %collective-permute-start.5 = (f32[8,64,128]{2,1,0:T(8,128)S(1)}, f32[8,64,128]{2,1,0:T(8,128)S(1)}, u32[]{:S(2)}, u32[]{:S(2)}) collective-permute-start(f32[8,64,128]{2,1,0:T(8,128)S(1)} %get-tuple-element.101), channel_id=1, source_target_pairs={{0,2},{2,0},{4,6},{6,4},{8,10},{10,8},{12,14},{14,12},{16,18},{18,... | collective-permute-start | bytes 786440 | tf_op jit(solution)/shard_map/ppermute | solution.py:583
  22.7 9.0 %collective-permute-start.4 = (f32[8,64,128]{2,1,0:T(8,128)S(1)}, f32[8,64,128]{2,1,0:T(8,128)S(1)}, u32[]{:S(2)}, u32[]{:S(2)}) collective-permute-start(f32[8,64,128]{2,1,0:T(8,128)S(1)} %get-tuple-element.100), channel_id=1, source_target_pairs={{2,4},{4,2},{6,8},{8,6},{10,12},{12,10},{14,16},{16,14},{18,20},{2... | collective-permute-start | bytes 786440 | tf_op jit(solution)/shard_map/ppermute | solution.py:586
  26.6 6.2 %collective-permute-start.8 = (f32[8,64,128]{2,1,0:T(8,128)S(1)}, f32[8,64,128]{2,1,0:T(8,128)S(1)}, u32[]{:S(2)}, u32[]{:S(2)}) collective-permute-start(f32[8,64,128]{2,1,0:T(8,128)S(1)} %get-tuple-element.123), channel_id=1, source_target_pairs={{0,2},{2,0},{4,6},{6,4},{8,10},{10,8},{12,14},{14,12},{16,18},{18,... | collective-permute-start | bytes 786440 | tf_op jit(solution)/shard_map/ppermute | solution.py:583
  31.8 5.3 %collective-permute-start.6 = (f32[8,64,128]{2,1,0:T(8,128)S(1)}, f32[8,64,128]{2,1,0:T(8,128)S(1)}, u32[]{:S(2)}, u32[]{:S(2)}) collective-permute-start(f32[8,64,128]{2,1,0:T(8,128)S(1)} %get-tuple-element.113), channel_id=1, source_target_pairs={{2,4},{4,2},{6,8},{8,6},{10,12},{12,10},{14,16},{16,14},{18,20},{2... | collective-permute-start | bytes 786440 | tf_op jit(solution)/shard_map/ppermute | solution.py:586
  33.4 4.3 %collective-permute-start.9 = (f32[4,32,128]{2,1,0:T(8,128)S(1)}, f32[4,32,128]{2,1,0:T(8,128)S(1)}, u32[]{:S(2)}, u32[]{:S(2)}) collective-permute-start(f32[4,32,128]{2,1,0:T(8,128)S(1)} %get-tuple-element.124), channel_id=1, source_target_pairs={{1,0},{0,1},{3,2},{2,3},{5,4},{4,5},{7,6},{6,7},{9,8},{8,9},{11,10... | collective-permute-start | bytes 196616 | tf_op jit(solution)/shard_map/ppermute | solution.py:589
  36.0 5.0 %collective-permute-start.10 = (f32[8,32,128]{2,1,0:T(8,128)S(1)}, f32[8,32,128]{2,1,0:T(8,128)S(1)}, u32[]{:S(2)}, u32[]{:S(2)}) collective-permute-start(f32[8,32,128]{2,1,0:T(8,128)S(1)} %get-tuple-element.126), channel_id=1, source_target_pairs={{1,0},{0,1},{3,2},{2,3},{5,4},{4,5},{7,6},{6,7},{9,8},{8,9},{11,10... | collective-permute-start | bytes 393224 | tf_op jit(solution)/shard_map/ppermute | solution.py:589
  37.8 19.7 %collective-permute-start.11 = (f32[4,64,128]{2,1,0:T(8,128)S(1)}, f32[4,64,128]{2,1,0:T(8,128)S(1)}, u32[]{:S(2)}, u32[]{:S(2)}) collective-permute-start(f32[4,64,128]{2,1,0:T(8,128)S(1)} %last_join.1.grad.chip), channel_id=1, source_target_pairs={{1,0},{0,1},{3,2},{2,3},{5,4},{4,5},{7,6},{6,7},{9,8},{8,9},{11,10... | collective-permute-start | bytes 393224 | tf_op jit(solution)/shard_map/ppermute | solution.py:589
  41.1 17.2 %copy-start.1 = (f32[16,64,128]{2,1,0:T(8,128)S(1)}, f32[16,64,128]{2,1,0:T(8,128)}, u32[]{:S(2)}) copy-start(f32[16,64,128]{2,1,0:T(8,128)} %courant.7) | copy-start | bytes 1572868
  57.8 6.7 %collective-permute-start.12 = (f32[12,32,128]{2,1,0:T(8,128)S(1)}, f32[12,32,128]{2,1,0:T(8,128)S(1)}, u32[]{:S(2)}, u32[]{:S(2)}) collective-permute-start(f32[12,32,128]{2,1,0:T(8,128)S(1)} %get-tuple-element.131.near_move), channel_id=1, source_target_pairs={{1,0},{0,1},{3,2},{2,3},{5,4},{4,5},{7,6},{6,7},{9,8},{8,9},{11,10... | collective-permute-start | bytes 589832 | tf_op jit(solution)/shard_map/ppermute | solution.py:589

commit v6 on v5

--- a/solution.py
+++ b/solution.py
@@ -291,12 +291,32 @@
     return adj[part] * lap2[part] + adj3[part] * lap3[part]
 
 
-def inner_kernel(scale, _, wave, prod, adj, adj_old, injected, wide, tall, lap1, lap2, lap3, adj4, adj3, *outs):
-    full, along = outs[-3], outs[-2:]
-    which = inner_rows(adj.shape[0])
+def gradient_rows(scale, which, first, full, wave, prod, adj, adj_old, injected, wide, tall, lap1, lap2, lap3, adj4, adj3, along):
     for place, row, start, part, lap, new in last_rows(which, wave, prod, adj, adj_old, injected, wide, tall, *along):
         known = known_terms(part, adj, lap2, lap3, adj3)
-        full[place, start : start + CHUNK, :] = scale * (known + adj4[part] * lap + new * lap1[part])
+        full[first + place, start : start + CHUNK, :] = scale * (known + adj4[part] * lap + new * lap1[part])
+
+
+def join_far_kernel(
+    scale, halo, courant, lap, wave, adj, prod, adj_old, injected, wide, tall, lap1, lap2, adj4, *refs
+):
+    joined, full, along = refs[:5], refs[5], refs[6:]
+    join_kernel(False, halo, courant, lap, wave, adj, prod, *joined)
+    o_lap, o_wave, o_adj, o_prod = joined[:4]
+    which = list(range(2 * REACH, courant.shape[0] - REACH))
+    gradient_rows(
+        scale, which, 0, full, o_wave, o_prod, o_adj, adj_old, injected, wide, tall, lap1, lap2, o_lap, adj4, adj_old, along
+    )
+
+
+def inner_kernel(scale, _, far, wave, prod, adj, adj_old, injected, wide, tall, lap1, lap2, lap3, adj4, adj3, *outs):
+    full, along = outs[-3], outs[-2:]
+    which = list(range(REACH, 2 * REACH))
+    for place in range(far.shape[0]):
+        full[REACH + place] = far[place]
+    gradient_rows(
+        scale, which, 0, full, wave, prod, adj, adj_old, injected, wide, tall, lap1, lap2, lap3, adj4, adj3, along
+    )
     lay_pieces(full, outs[:-3])
 
 
@@ -635,6 +655,11 @@
 
     gram = call(gram_kernel, "gram", shape(len(PRODUCTS), 8, width), history)
 
+    scale = 1.0 / (shots * STEPS)
+
+    def some_rows(count, copies):
+        return [pltpu.VMEM((count, across, width), F32)] * copies
+
     laps, adjs = [], []
     for moment in range(STEPS - 1):
         lap, new_wave, new_adj, new_prod = call(
@@ -657,18 +682,29 @@
         )
         sends = []
         for chip, came in ((False, from_core), (True, from_chip)):
-            lap, new_wave, new_adj, new_prod, send = call(
-                functools.partial(join_kernel, chip),
-                f"join_{'chip' if chip else 'core'}_{moment}",
-                [slab, padded, slab, padded, halo],
-                came,
-                cour,
-                lap,
-                new_wave,
-                new_adj,
-                new_prod,
-                aliases={2: 0, 3: 1, 4: 2, 5: 3},
-            )
+            arrays = (came, cour, lap, new_wave, new_adj, new_prod)
+            if moment == STEPS - 2 and not chip:
+                lap, new_wave, new_adj, new_prod, send, far = call(
+                    functools.partial(join_far_kernel, scale),
+                    "join_far",
+                    [slab, padded, slab, padded, halo, shape(rows - 3 * REACH, across, width)],
+                    *arrays,
+                    adj,
+                    injected,
+                    *bands,
+                    *laps,
+                    adjs[0],
+                    aliases={2: 0, 3: 1, 4: 2, 5: 3},
+                    scratch=some_rows(rows - 3 * REACH, 2),
+                )
+            else:
+                lap, new_wave, new_adj, new_prod, send = call(
+                    functools.partial(join_kernel, chip),
+                    f"join_{'chip' if chip else 'core'}_{moment}",
+                    [slab, padded, slab, padded, halo],
+                    *arrays,
+                    aliases={2: 0, 3: 1, 4: 2, 5: 3},
+                )
             sends.append(send)
         from_core = swap_core(sends[0])
         from_chip = swap_chip(sends[1])
@@ -678,15 +714,11 @@
         adj_old, adj = adj, new_adj
         prod = new_prod
 
-    scale = 1.0 / (shots * STEPS)
     inner_count, near_count = rows - 2 * REACH, rows - REACH
     last = (wave, prod, adj, adj_old, injected, *bands, laps[0], laps[1], laps[2], adjs[0], adjs[1])
 
     def sum_parts(values):
         return [values[0]] + [from_shot(values[shots - turn], turn) for turn in range(1, shots)]
-
-    def some_rows(count, copies):
-        return [pltpu.VMEM((count, across, width), F32)] * copies
 
     core = call(
         functools.partial(core_kernel, scale),
@@ -701,8 +733,9 @@
         "inner",
         [shape(inner_count, piece, width)] * shots,
         core[0],
+        far,
         *last,
-        scratch=some_rows(inner_count, 3),
+        scratch=some_rows(inner_count, 1) + some_rows(REACH, 2),
     )
     core, inner = sum_parts(core), sum_parts(inner)
     chip_part = shape(REACH, across, width)

time: 65.5 us -> 64.9 us (level)
  blocking collectives: 15.9 us -> 15.2 us
    all_to_all x1, blocking collectives: 15.9 us -> 15.2 us  [per_device(): lines = lax.all_to_all(line, ('depth', 'shot'), 0, 0, tiled=True)]
where the time goes in v6:
time: 64.9 us; the launch traced here: 64.5 us
  starting transfers between devices  20.8 us (32%)
  Pallas kernels  19.5 us (30%)
  blocking collectives  15.2 us (23%)
  waiting for transfers between devices  7.55 us (12%)
  between operations  1.53 us (2%)
    pallas_call x23, Pallas kernels, call(): pl.pallas_call(kernel, name=name, out_shape=outs, in_specs=specs or [VM]...  19.5 us
    all_to_all x1, blocking collectives, per_device(): lines = lax.all_to_all(line, ('depth', 'shot'), 0, 0, tiled=True)  15.2 us
    ppermute x4, starting transfers between devices, swap_core(): return lax.ppermute(value, 'depth', on_chip)  12.2 us
    ppermute x5, waiting for transfers between devices, from_shot(): lax.ppermute(value, 'shot', [((i + turn) % shots, i) for i in range(shots)])  7.2 us
    ppermute x5, starting transfers between devices, from_shot(): lax.ppermute(value, 'shot', [((i + turn) % shots, i) for i in range(shots)])  5.91 us
    ppermute x4, starting transfers between devices, swap_chip(): return lax.ppermute(value, 'depth', off_chip)  2.7 us
  transfers between devices with their start and end apart: 13, of which 4 were waited for; matrix products, arithmetic and copies ran while one was open for 0% of the time, Pallas kernels for 26%

profile of v6, /device:TPU:0, one launch (start us, length us, event | category | flops | bytes accessed | tf_op | source)
XLA Modules:
  0.0 64.5 jit_solution(2598114655369720194)
XLA Ops:
  0.7 1.3 %first_send.1 = (f32[8,64,128]{2,1,0:T(8,128)S(1)}, f32[8,64,128]{2,1,0:T(8,128)S(1)}) custom-call(f32[16,64,128]{2,1,0:T(8,128)} %bitcast.12, f32[16,64,128]{2,1,0:T(8,128)} %bitcast.14, f32[16,64,128]{2,1,0:T(8,128)} %courant.7), custom_call_target="tpu_custom_call" | custom-call | flops 1048576 | bytes 1048576 | tf_op jit(solution)/shard_map/first_send/pallas_call | solution.py:566
  2.0 0.0 copy-start.2
  2.0 0.5 collective-permute-start.1
  2.5 0.7 %collective-permute-start = (f32[8,64,128]{2,1,0:T(8,128)S(1)}, f32[8,64,128]{2,1,0:T(8,128)S(1)}, u32[]{:S(2)}, u32[]{:S(2)}) collective-permute-start(f32[8,64,128]{2,1,0:T(8,128)S(1)} %get-tuple-element.70), channel_id=1, source_target_pairs={{2,4},{4,2},{6,8},{8,6},{10,12},{12,10},{14,16},{16,14},{18,20},{2... | collective-permute-start | bytes 786440 | tf_op jit(solution)/shard_map/ppermute | solution.py:606
  3.8 1.8 %stage.1 = (f32[16,80,128]{2,1,0:T(8,128)S(1)}, f32[16,80,128]{2,1,0:T(8,128)S(1)}, f32[16,64,128]{2,1,0:T(8,128)S(1)}, f32[16,64,128]{2,1,0:T(8,128)S(1)}, f32[...) custom-call(f32[16,64,128]{2,1,0:T(8,128)} %bitcast.13, ...), custom_call_target="tpu_custom_call" | custom-call | flops 1048576 | bytes 1048576 | tf_op jit(solution)/shard_map/stage/pallas_call | solution.py:566
  5.6 1.8 %receivers.2.injected = f32[4,1024,128]{2,1,0:T(8,128)S(1)} custom-call(s32[1,256]{1,0:T(1,128)S(1)} %copy-done.4, f32[4,256]{1,0:T(4,128)S(1)} %bitcast.11), custom_call_target="tpu_custom_call" | custom-call | flops 1048576 | bytes 1048576 | tf_op jit(solution)/shard_map/receivers/pallas_call | solution.py:566
  7.5 2.3 %local_0.1 = (f32[16,64,128]{2,1,0:T(8,128)S(1)}, f32[16,80,128]{2,1,0:T(8,128)S(1)}, f32[16,64,128]{2,1,0:T(8,128)S(1)}, f32[16,80,128]{2,1,0:T(8,128)S(1)}) custom-call(s32[1]{0:T(128)S(6)} %copy.64.cell, f32[1,4]{1,0:T(1,128)S(1)} %copy-done.2, f32[16,80,128]{2,1,0:T(8,128)S(1)} %get-tuple-element.73.wave.wave_old, ...), custom_call_target="tpu_custom_call" | custom-call | flops 1048576 | bytes 1048576 | tf_op jit(solution)/shard_map/local_0/pallas_call | solution.py:566
  9.8 0.1 join_core_0.1
  10.0 3.9 %collective-permute-start.3 = (f32[8,64,128]{2,1,0:T(8,128)S(1)}, f32[8,64,128]{2,1,0:T(8,128)S(1)}, u32[]{:S(2)}, u32[]{:S(2)}) collective-permute-start(f32[8,64,128]{2,1,0:T(8,128)S(1)} %get-tuple-element.89), channel_id=1, source_target_pairs={{0,2},{2,0},{4,6},{6,4},{8,10},{10,8},{12,14},{14,12},{16,18},{18,... | collective-permute-start | bytes 786440 | tf_op jit(solution)/shard_map/ppermute | solution.py:603
  13.9 0.1 join_chip_0.1
  14.0 0.7 %collective-permute-start.2 = (f32[8,64,128]{2,1,0:T(8,128)S(1)}, f32[8,64,128]{2,1,0:T(8,128)S(1)}, u32[]{:S(2)}, u32[]{:S(2)}) collective-permute-start(f32[8,64,128]{2,1,0:T(8,128)S(1)} %get-tuple-element.88), channel_id=1, source_target_pairs={{2,4},{4,2},{6,8},{8,6},{10,12},{12,10},{14,16},{16,14},{18,20},{2... | collective-permute-start | bytes 786440 | tf_op jit(solution)/shard_map/ppermute | solution.py:606
  14.7 1.1 %keep.1.refs_0_.refs_1_ = f32[2,5,4,32,128]{4,3,2,1,0:T(8,128)S(1)} custom-call(f32[2,5,16,32,128]{4,3,2,1,0:T(8,128)} %history.7, f32[8,64,128]{2,1,0:T(8,128)S(1)} %collective-permute-done.1.halo._), custom_call_target="tpu_custom_call" | custom-call | flops 1048576 | bytes 1048576 | tf_op jit(solution)/shard_map/keep/pallas_call | solution.py:566
  15.8 1.6 %collective-permute-start.7 = (f32[2,5,4,32,128]{4,3,2,1,0:T(8,128)S(1)}, f32[2,5,4,32,128]{4,3,2,1,0:T(8,128)S(1)}, u32[]{:S(2)}, u32[]{:S(2)}) collective-permute-start(f32[2,5,4,32,128]{4,3,2,1,0:T(8,128)S(1)} %keep.1.refs_0_.refs_1_), channel_id=1, source_target_pairs={{1,0},{0,1},{3,2},{2,3},{5,4},{4,5},{7,6},{6,7},{9,8},{8,9},{11,10... | collective-permute-start | bytes 1966088 | tf_op jit(solution)/shard_map/ppermute | solution.py:609
  17.4 2.2 %local_1.1 = (f32[16,64,128]{2,1,0:T(8,128)S(1)}, f32[16,80,128]{2,1,0:T(8,128)S(1)}, f32[16,64,128]{2,1,0:T(8,128)S(1)}, f32[16,80,128]{2,1,0:T(8,128)S(1)}) custom-call(s32[1]{0:T(128)S(6)} %copy.64.cell, f32[1,4]{1,0:T(1,128)S(1)} %copy-done.2, f32[16,80,128]{2,1,0:T(8,128)S(1)} %get-tuple-element.90.wave.wave_old, ...), custom_call_target="tpu_custom_call" | custom-call | flops 1048576 | bytes 1048576 | tf_op jit(solution)/shard_map/local_1/pallas_call | solution.py:566
  19.6 0.0 collective-permute-done.3.halo
  19.6 0.0 copy-start
  19.7 0.1 join_core_1.1
  19.8 2.8 %collective-permute-start.5 = (f32[8,64,128]{2,1,0:T(8,128)S(1)}, f32[8,64,128]{2,1,0:T(8,128)S(1)}, u32[]{:S(2)}, u32[]{:S(2)}) collective-permute-start(f32[8,64,128]{2,1,0:T(8,128)S(1)} %get-tuple-element.102), channel_id=1, source_target_pairs={{0,2},{2,0},{4,6},{6,4},{8,10},{10,8},{12,14},{14,12},{16,18},{18,... | collective-permute-start | bytes 786440 | tf_op jit(solution)/shard_map/ppermute | solution.py:603
  22.5 0.0 collective-permute-done.2.halo
  22.6 0.1 join_chip_1.1
  22.7 0.7 %collective-permute-start.4 = (f32[8,64,128]{2,1,0:T(8,128)S(1)}, f32[8,64,128]{2,1,0:T(8,128)S(1)}, u32[]{:S(2)}, u32[]{:S(2)}) collective-permute-start(f32[8,64,128]{2,1,0:T(8,128)S(1)} %get-tuple-element.101), channel_id=1, source_target_pairs={{2,4},{4,2},{6,8},{8,6},{10,12},{12,10},{14,16},{16,14},{18,20},{2... | collective-permute-start | bytes 786440 | tf_op jit(solution)/shard_map/ppermute | solution.py:606
  23.4 0.7 %gram.1.outs_0_ = f32[30,8,128]{2,1,0:T(8,128)S(1)} custom-call(f32[2,5,16,32,128]{4,3,2,1,0:T(8,128)S(1)} %copy-done), custom_call_target="tpu_custom_call" | custom-call | flops 1048576 | bytes 1048576 | tf_op jit(solution)/shard_map/gram/pallas_call | solution.py:566
  24.1 2.3 %local_2.1 = (f32[16,64,128]{2,1,0:T(8,128)S(1)}, f32[16,80,128]{2,1,0:T(8,128)S(1)}, f32[16,64,128]{2,1,0:T(8,128)S(1)}, f32[16,80,128]{2,1,0:T(8,128)S(1)}) custom-call(s32[1]{0:T(128)S(6)} %copy.64.cell, f32[1,4]{1,0:T(1,128)S(1)} %copy-done.2, f32[16,80,128]{2,1,0:T(8,128)S(1)} %get-tuple-element.103.wave, ...), custom_call_target="tpu_custom_call" | custom-call | flops 1048576 | bytes 1048576 | tf_op jit(solution)/shard_map/local_2/pallas_call | solution.py:566
  26.5 0.0 collective-permute-done.5.halo
  26.5 0.7 %join_far.1 = (f32[16,64,128]{2,1,0:T(8,128)S(1)}, f32[16,80,128]{2,1,0:T(8,128)S(1)}, f32[16,64,128]{2,1,0:T(8,128)S(1)}, f32[16,80,128]{2,1,0:T(8,128)S(1)}, f...) custom-call(f32[8,64,128]{2,1,0:T(8,128)S(1)} %collective-permute-do, ...), custom_call_target="tpu_custom_call", output_to_operand_aliasing={{0}: (2, {}), {1}: (3, {}), {2}: (4, {}), {3}: (5, {})} | custom-call | flops 1048576 | bytes 1048576 | tf_op jit(solution)/shard_map/join_far/pallas_call | solution.py:566
  27.2 5.0 %collective-permute-start.8 = (f32[8,64,128]{2,1,0:T(8,128)S(1)}, f32[8,64,128]{2,1,0:T(8,128)S(1)}, u32[]{:S(2)}, u32[]{:S(2)}) collective-permute-start(f32[8,64,128]{2,1,0:T(8,128)S(1)} %get-tuple-element.124), channel_id=1, source_target_pairs={{0,2},{2,0},{4,6},{6,4},{8,10},{10,8},{12,14},{14,12},{16,18},{18,... | collective-permute-start | bytes 786440 | tf_op jit(solution)/shard_map/ppermute | solution.py:603
  32.1 0.0 collective-permute-done.4.halo
  32.2 0.1 join_chip_2.1
  32.3 0.7 %collective-permute-start.6 = (f32[8,64,128]{2,1,0:T(8,128)S(1)}, f32[8,64,128]{2,1,0:T(8,128)S(1)}, u32[]{:S(2)}, u32[]{:S(2)}) collective-permute-start(f32[8,64,128]{2,1,0:T(8,128)S(1)} %get-tuple-element.116), channel_id=1, source_target_pairs={{2,4},{4,2},{6,8},{8,6},{10,12},{12,10},{14,16},{16,14},{18,20},{2... | collective-permute-start | bytes 786440 | tf_op jit(solution)/shard_map/ppermute | solution.py:606
  33.0 0.3 collective-permute-done.8.from_core
  33.3 0.6 core.1
  33.9 1.6 %collective-permute-start.9 = (f32[4,32,128]{2,1,0:T(8,128)S(1)}, f32[4,32,128]{2,1,0:T(8,128)S(1)}, u32[]{:S(2)}, u32[]{:S(2)}) collective-permute-start(f32[4,32,128]{2,1,0:T(8,128)S(1)} %get-tuple-element.125), channel_id=1, source_target_pairs={{1,0},{0,1},{3,2},{2,3},{5,4},{4,5},{7,6},{6,7},{9,8},{8,9},{11,10... | collective-permute-start | bytes 196616 | tf_op jit(solution)/shard_map/ppermute | solution.py:609
  35.5 0.6 inner.1
  36.1 0.6 collective-permute-start.10
  36.7 0.5 chip.1
  37.2 1.0 %collective-permute-done.9.refs_0_.refs_3_ = f32[4,32,128]{2,1,0:T(8,128)S(1)} collective-permute-done((f32[4,32,128]{2,1,0:T(8,128)S(1)}, f32[4,32,128]{2,1,0:T(8,128)S(1)}, u32[]{:S(2)}, u32[]{:S(2)}) %collective-permute-start.9) | collective-permute-done | bytes 65568 | tf_op jit(solution)/shard_map/ppermute | solution.py:609
  38.3 0.1 last_join.1.grad.chip
  38.3 1.6 %collective-permute-start.11 = (f32[4,64,128]{2,1,0:T(8,128)S(1)}, f32[4,64,128]{2,1,0:T(8,128)S(1)}, u32[]{:S(2)}, u32[]{:S(2)}) collective-permute-start(f32[4,64,128]{2,1,0:T(8,128)S(1)} %last_join.1.grad.chip), channel_id=1, source_target_pairs={{1,0},{0,1},{3,2},{2,3},{5,4},{4,5},{7,6},{6,7},{9,8},{8,9},{11,10... | collective-permute-start | bytes 393224 | tf_op jit(solution)/shard_map/ppermute | solution.py:609
  39.9 1.2 %collective-permute-done.10.refs_2_.refs_1_ = f32[8,32,128]{2,1,0:T(8,128)S(1)} collective-permute-done((f32[8,32,128]{2,1,0:T(8,128)S(1)}, f32[8,32,128]{2,1,0:T(8,128)S(1)}, u32[]{:S(2)}, u32[]{:S(2)}) %collective-permute-start.10) | collective-permute-done | bytes 131104 | tf_op jit(solution)/shard_map/ppermute | solution.py:609
  41.2 0.1 chip_dots.1.chip
  41.3 0.0 copy-start.1
  41.3 0.3 line.1
  41.6 15.2 %all_to_all.11 = f32[32,1,128]{2,1,0:T(1,128)S(1)} all-to-all(f32[32,1,128]{2,1,0:T(1,128)S(1)} %bitcast.10), channel_id=1, replica_groups=mesh['depth'=16,'shot'=2] {'depth','shot'}, dimensions={0} | all-to-all | bytes 32768 | tf_op jit(solution)/shard_map/all_to_all | solution.py:775
  56.8 0.3 weights.1
  57.1 0.6 collective-permute-start.12
  57.7 1.1 %finish.1 = (f32[16,32,128]{2,1,0:T(8,128)}, f32[16,32,128]{2,1,0:T(8,128)}, f32[16,64,128]{2,1,0:T(8,128)}) custom-call(f32[11,8,128]{2,1,0:T(8,128)S(1)} %get-tuple-element.132.weight, f32[16,64,128]{2,1,0:T(8,128)S(1)} %copy-done.1, f32[12,32,128]{2,1,0:T(8,128)S(1)} %get-tuple-element.131.near, f32[12,32,128]{2,1,0:T(8,128)S(1)} %get-tuple-element.133.near_move, ...), custom_call_target="tpu_custom_call" | custom-call | flops 1048576 | bytes 1048576 | tf_op jit(solution)/shard_map/finish/pallas_call | solution.py:566
  58.9 4.9 %collective-permute-done.12.refs_0_ = f32[12,32,128]{2,1,0:T(8,128)S(1)} collective-permute-done((f32[12,32,128]{2,1,0:T(8,128)S(1)}, f32[12,32,128]{2,1,0:T(8,128)S(1)}, u32[]{:S(2)}, u32[]{:S(2)}) %collective-permute-start.12) | collective-permute-done | bytes 196640 | tf_op jit(solution)/shard_map/ppermute | solution.py:609
  63.8 0.7 %last_piece.1 = f32[16,64,128]{2,1,0:T(8,128)} custom-call(f32[16,64,128]{2,1,0:T(8,128)S(1)} %copy-done.1, f32[16,64,128]{2,1,0:T(8,128)} %get-tuple-element.136.done, f32[12,32,128]{2,1,0:T(8,128)S(1)} %collective-permute-done.12.refs_0_), custom_call_target="tpu_custom_call", output_to_operand_aliasing={{}: (1, {})} | custom-call | flops 1048576 | bytes 1048576 | tf_op jit(solution)/shard_map/last_piece/pallas_call | solution.py:566
  (12 shorter events, 0.0 us)
Async XLA Ops:
  0.6 5.0 %copy-start.3 = (f32[1,4,256]{2,1,0:T(4,128)S(1)}, f32[1,4,256]{2,1,0:T(4,128)}, u32[]{:S(2)}) copy-start(f32[1,4,256]{2,1,0:T(4,128)} %param.18) | copy-start | bytes 12292
  0.6 5.0 %copy-start.4 = (s32[1,256]{1,0:T(1,128)S(1)}, s32[1,256]{1,0:T(1,128)}, u32[]{:S(2)}) copy-start(s32[1,256]{1,0:T(1,128)} %receivers.3) | copy-start | bytes 3076
  2.0 5.5 %copy-start.2 = (f32[1,4]{1,0:T(1,128)S(1)}, f32[1,4]{1,0:T(1,128)}, u32[]{:S(2)}) copy-start(f32[1,4]{1,0:T(1,128)} %wavelet.5) | copy-start | bytes 52
  2.0 7.8 %collective-permute-start.1 = (f32[8,64,128]{2,1,0:T(8,128)S(1)}, f32[8,64,128]{2,1,0:T(8,128)S(1)}, u32[]{:S(2)}, u32[]{:S(2)}) collective-permute-start(f32[8,64,128]{2,1,0:T(8,128)S(1)} %get-tuple-element.72), channel_id=1, source_target_pairs={{0,2},{2,0},{4,6},{6,4},{8,10},{10,8},{12,14},{14,12},{16,18},{18,... | collective-permute-start | bytes 786440 | tf_op jit(solution)/shard_map/ppermute | solution.py:603
  2.5 11.4 %collective-permute-start = (f32[8,64,128]{2,1,0:T(8,128)S(1)}, f32[8,64,128]{2,1,0:T(8,128)S(1)}, u32[]{:S(2)}, u32[]{:S(2)}) collective-permute-start(f32[8,64,128]{2,1,0:T(8,128)S(1)} %get-tuple-element.70), channel_id=1, source_target_pairs={{2,4},{4,2},{6,8},{8,6},{10,12},{12,10},{14,16},{16,14},{18,20},{2... | collective-permute-start | bytes 786440 | tf_op jit(solution)/shard_map/ppermute | solution.py:606
  10.0 9.7 %collective-permute-start.3 = (f32[8,64,128]{2,1,0:T(8,128)S(1)}, f32[8,64,128]{2,1,0:T(8,128)S(1)}, u32[]{:S(2)}, u32[]{:S(2)}) collective-permute-start(f32[8,64,128]{2,1,0:T(8,128)S(1)} %get-tuple-element.89), channel_id=1, source_target_pairs={{0,2},{2,0},{4,6},{6,4},{8,10},{10,8},{12,14},{14,12},{16,18},{18,... | collective-permute-start | bytes 786440 | tf_op jit(solution)/shard_map/ppermute | solution.py:603
  14.0 8.5 %collective-permute-start.2 = (f32[8,64,128]{2,1,0:T(8,128)S(1)}, f32[8,64,128]{2,1,0:T(8,128)S(1)}, u32[]{:S(2)}, u32[]{:S(2)}) collective-permute-start(f32[8,64,128]{2,1,0:T(8,128)S(1)} %get-tuple-element.88), channel_id=1, source_target_pairs={{2,4},{4,2},{6,8},{8,6},{10,12},{12,10},{14,16},{16,14},{18,20},{2... | collective-permute-start | bytes 786440 | tf_op jit(solution)/shard_map/ppermute | solution.py:606
  15.8 20.9 %collective-permute-start.7 = (f32[2,5,4,32,128]{4,3,2,1,0:T(8,128)S(1)}, f32[2,5,4,32,128]{4,3,2,1,0:T(8,128)S(1)}, u32[]{:S(2)}, u32[]{:S(2)}) collective-permute-start(f32[2,5,4,32,128]{4,3,2,1,0:T(8,128)S(1)} %keep.1.refs_0_.refs_1_), channel_id=1, source_target_pairs={{1,0},{0,1},{3,2},{2,3},{5,4},{4,5},{7,6},{6,7},{9,8},{8,9},{11,10... | collective-permute-start | bytes 1966088 | tf_op jit(solution)/shard_map/ppermute | solution.py:609
  19.6 3.7 %copy-start = (f32[2,5,16,32,128]{4,3,2,1,0:T(8,128)S(1)}, f32[2,5,16,32,128]{4,3,2,1,0:T(8,128)}, u32[]{:S(2)}) copy-start(f32[2,5,16,32,128]{4,3,2,1,0:T(8,128)} %history.7) | copy-start | bytes 7864324
  19.8 6.7 %collective-permute-start.5 = (f32[8,64,128]{2,1,0:T(8,128)S(1)}, f32[8,64,128]{2,1,0:T(8,128)S(1)}, u32[]{:S(2)}, u32[]{:S(2)}) collective-permute-start(f32[8,64,128]{2,1,0:T(8,128)S(1)} %get-tuple-element.102), channel_id=1, source_target_pairs={{0,2},{2,0},{4,6},{6,4},{8,10},{10,8},{12,14},{14,12},{16,18},{18,... | collective-permute-start | bytes 786440 | tf_op jit(solution)/shard_map/ppermute | solution.py:603
  22.7 9.5 %collective-permute-start.4 = (f32[8,64,128]{2,1,0:T(8,128)S(1)}, f32[8,64,128]{2,1,0:T(8,128)S(1)}, u32[]{:S(2)}, u32[]{:S(2)}) collective-permute-start(f32[8,64,128]{2,1,0:T(8,128)S(1)} %get-tuple-element.101), channel_id=1, source_target_pairs={{2,4},{4,2},{6,8},{8,6},{10,12},{12,10},{14,16},{16,14},{18,20},{2... | collective-permute-start | bytes 786440 | tf_op jit(solution)/shard_map/ppermute | solution.py:606
  27.2 6.2 %collective-permute-start.8 = (f32[8,64,128]{2,1,0:T(8,128)S(1)}, f32[8,64,128]{2,1,0:T(8,128)S(1)}, u32[]{:S(2)}, u32[]{:S(2)}) collective-permute-start(f32[8,64,128]{2,1,0:T(8,128)S(1)} %get-tuple-element.124), channel_id=1, source_target_pairs={{0,2},{2,0},{4,6},{6,4},{8,10},{10,8},{12,14},{14,12},{16,18},{18,... | collective-permute-start | bytes 786440 | tf_op jit(solution)/shard_map/ppermute | solution.py:603
  32.3 4.9 %collective-permute-start.6 = (f32[8,64,128]{2,1,0:T(8,128)S(1)}, f32[8,64,128]{2,1,0:T(8,128)S(1)}, u32[]{:S(2)}, u32[]{:S(2)}) collective-permute-start(f32[8,64,128]{2,1,0:T(8,128)S(1)} %get-tuple-element.116), channel_id=1, source_target_pairs={{2,4},{4,2},{6,8},{8,6},{10,12},{12,10},{14,16},{16,14},{18,20},{2... | collective-permute-start | bytes 786440 | tf_op jit(solution)/shard_map/ppermute | solution.py:606
  33.9 4.3 %collective-permute-start.9 = (f32[4,32,128]{2,1,0:T(8,128)S(1)}, f32[4,32,128]{2,1,0:T(8,128)S(1)}, u32[]{:S(2)}, u32[]{:S(2)}) collective-permute-start(f32[4,32,128]{2,1,0:T(8,128)S(1)} %get-tuple-element.125), channel_id=1, source_target_pairs={{1,0},{0,1},{3,2},{2,3},{5,4},{4,5},{7,6},{6,7},{9,8},{8,9},{11,10... | collective-permute-start | bytes 196616 | tf_op jit(solution)/shard_map/ppermute | solution.py:609
  36.1 5.0 %collective-permute-start.10 = (f32[8,32,128]{2,1,0:T(8,128)S(1)}, f32[8,32,128]{2,1,0:T(8,128)S(1)}, u32[]{:S(2)}, u32[]{:S(2)}) collective-permute-start(f32[8,32,128]{2,1,0:T(8,128)S(1)} %get-tuple-element.128), channel_id=1, source_target_pairs={{1,0},{0,1},{3,2},{2,3},{5,4},{4,5},{7,6},{6,7},{9,8},{8,9},{11,10... | collective-permute-start | bytes 393224 | tf_op jit(solution)/shard_map/ppermute | solution.py:609
  38.3 18.5 %collective-permute-start.11 = (f32[4,64,128]{2,1,0:T(8,128)S(1)}, f32[4,64,128]{2,1,0:T(8,128)S(1)}, u32[]{:S(2)}, u32[]{:S(2)}) collective-permute-start(f32[4,64,128]{2,1,0:T(8,128)S(1)} %last_join.1.grad.chip), channel_id=1, source_target_pairs={{1,0},{0,1},{3,2},{2,3},{5,4},{4,5},{7,6},{6,7},{9,8},{8,9},{11,10... | collective-permute-start | bytes 393224 | tf_op jit(solution)/shard_map/ppermute | solution.py:609
  41.3 16.4 %copy-start.1 = (f32[16,64,128]{2,1,0:T(8,128)S(1)}, f32[16,64,128]{2,1,0:T(8,128)}, u32[]{:S(2)}) copy-start(f32[16,64,128]{2,1,0:T(8,128)} %courant.7) | copy-start | bytes 1572868
  57.1 6.7 %collective-permute-start.12 = (f32[12,32,128]{2,1,0:T(8,128)S(1)}, f32[12,32,128]{2,1,0:T(8,128)S(1)}, u32[]{:S(2)}, u32[]{:S(2)}) collective-permute-start(f32[12,32,128]{2,1,0:T(8,128)S(1)} %get-tuple-element.133.near_move), channel_id=1, source_target_pairs={{1,0},{0,1},{3,2},{2,3},{5,4},{4,5},{7,6},{6,7},{9,8},{8,9},{11,10... | collective-permute-start | bytes 589832 | tf_op jit(solution)/shard_map/ppermute | solution.py:609

commit v7 on v6

--- a/solution.py
+++ b/solution.py
@@ -24,6 +24,10 @@
 
 def in_hbm(value):
     return pltpu.with_memory_space_constraint(value, pltpu.HBM)
+
+
+def in_vmem(value):
+    return pltpu.with_memory_space_constraint(value, pltpu.VMEM)
 
 
 def shape(*dims):
@@ -682,7 +686,7 @@
         )
         sends = []
         for chip, came in ((False, from_core), (True, from_chip)):
-            arrays = (came, cour, lap, new_wave, new_adj, new_prod)
+            arrays = (came, cour, *(in_vmem(value) for value in (lap, new_wave, new_adj, new_prod)))
             if moment == STEPS - 2 and not chip:
                 lap, new_wave, new_adj, new_prod, send, far = call(
                     functools.partial(join_far_kernel, scale),

time: 64.9 us -> 64.9 us (level)
  transfers between devices with their start and end apart: 13 -> 13, of which waited for: 4 -> 4; matrix products, arithmetic and copies ran while one was open for 0% -> 0% of each run, Pallas kernels for 26% -> 27%
where the time goes in v7:
time: 64.9 us; the launch traced here: 64.5 us
  starting transfers between devices  20.8 us (32%)
  Pallas kernels  19.5 us (30%)
  blocking collectives  15.2 us (23%)
  waiting for transfers between devices  7.55 us (12%)
  between operations  1.52 us (2%)
    pallas_call x23, Pallas kernels, call(): pl.pallas_call(kernel, name=name, out_shape=outs, in_specs=specs or [VM]...  19.5 us
    all_to_all x1, blocking collectives, per_device(): lines = lax.all_to_all(line, ('depth', 'shot'), 0, 0, tiled=True)  15.2 us
    ppermute x4, starting transfers between devices, swap_core(): return lax.ppermute(value, 'depth', on_chip)  12.2 us
    ppermute x5, waiting for transfers between devices, from_shot(): lax.ppermute(value, 'shot', [((i + turn) % shots, i) for i in range(shots)])  7.2 us
    ppermute x5, starting transfers between devices, from_shot(): lax.ppermute(value, 'shot', [((i + turn) % shots, i) for i in range(shots)])  5.91 us
    ppermute x4, starting transfers between devices, swap_chip(): return lax.ppermute(value, 'depth', off_chip)  2.7 us
  transfers between devices with their start and end apart: 13, of which 4 were waited for; matrix products, arithmetic and copies ran while one was open for 0% of the time, Pallas kernels for 27%

profile of v7, /device:TPU:0, one launch (start us, length us, event | category | flops | bytes accessed | tf_op | source)
XLA Modules:
  0.0 64.5 jit_solution(2598114655369720194)
XLA Ops:
  0.7 1.3 %first_send.1 = (f32[8,64,128]{2,1,0:T(8,128)S(1)}, f32[8,64,128]{2,1,0:T(8,128)S(1)}) custom-call(f32[16,64,128]{2,1,0:T(8,128)} %bitcast.12, f32[16,64,128]{2,1,0:T(8,128)} %bitcast.14, f32[16,64,128]{2,1,0:T(8,128)} %courant.7), custom_call_target="tpu_custom_call" | custom-call | flops 1048576 | bytes 1048576 | tf_op jit(solution)/shard_map/first_send/pallas_call | solution.py:570
  2.0 0.0 copy-start.2
  2.0 0.5 collective-permute-start.1
  2.5 0.7 %collective-permute-start = (f32[8,64,128]{2,1,0:T(8,128)S(1)}, f32[8,64,128]{2,1,0:T(8,128)S(1)}, u32[]{:S(2)}, u32[]{:S(2)}) collective-permute-start(f32[8,64,128]{2,1,0:T(8,128)S(1)} %get-tuple-element.70), channel_id=1, source_target_pairs={{2,4},{4,2},{6,8},{8,6},{10,12},{12,10},{14,16},{16,14},{18,20},{2... | collective-permute-start | bytes 786440 | tf_op jit(solution)/shard_map/ppermute | solution.py:610
  3.8 1.8 %stage.1 = (f32[16,80,128]{2,1,0:T(8,128)S(1)}, f32[16,80,128]{2,1,0:T(8,128)S(1)}, f32[16,64,128]{2,1,0:T(8,128)S(1)}, f32[16,64,128]{2,1,0:T(8,128)S(1)}, f32[...) custom-call(f32[16,64,128]{2,1,0:T(8,128)} %bitcast.13, ...), custom_call_target="tpu_custom_call" | custom-call | flops 1048576 | bytes 1048576 | tf_op jit(solution)/shard_map/stage/pallas_call | solution.py:570
  5.6 1.8 %receivers.2.injected = f32[4,1024,128]{2,1,0:T(8,128)S(1)} custom-call(s32[1,256]{1,0:T(1,128)S(1)} %copy-done.4, f32[4,256]{1,0:T(4,128)S(1)} %bitcast.11), custom_call_target="tpu_custom_call" | custom-call | flops 1048576 | bytes 1048576 | tf_op jit(solution)/shard_map/receivers/pallas_call | solution.py:570
  7.5 2.3 %local_0.1 = (f32[16,64,128]{2,1,0:T(8,128)S(1)}, f32[16,80,128]{2,1,0:T(8,128)S(1)}, f32[16,64,128]{2,1,0:T(8,128)S(1)}, f32[16,80,128]{2,1,0:T(8,128)S(1)}) custom-call(s32[1]{0:T(128)S(6)} %copy.64.cell, f32[1,4]{1,0:T(1,128)S(1)} %copy-done.2, f32[16,80,128]{2,1,0:T(8,128)S(1)} %get-tuple-element.73.wave.wave_old, ...), custom_call_target="tpu_custom_call" | custom-call | flops 1048576 | bytes 1048576 | tf_op jit(solution)/shard_map/local_0/pallas_call | solution.py:570
  9.8 0.1 join_core_0.1
  10.0 3.9 %collective-permute-start.3 = (f32[8,64,128]{2,1,0:T(8,128)S(1)}, f32[8,64,128]{2,1,0:T(8,128)S(1)}, u32[]{:S(2)}, u32[]{:S(2)}) collective-permute-start(f32[8,64,128]{2,1,0:T(8,128)S(1)} %get-tuple-element.89), channel_id=1, source_target_pairs={{0,2},{2,0},{4,6},{6,4},{8,10},{10,8},{12,14},{14,12},{16,18},{18,... | collective-permute-start | bytes 786440 | tf_op jit(solution)/shard_map/ppermute | solution.py:607
  13.9 0.1 join_chip_0.1
  14.0 0.7 %collective-permute-start.2 = (f32[8,64,128]{2,1,0:T(8,128)S(1)}, f32[8,64,128]{2,1,0:T(8,128)S(1)}, u32[]{:S(2)}, u32[]{:S(2)}) collective-permute-start(f32[8,64,128]{2,1,0:T(8,128)S(1)} %get-tuple-element.88), channel_id=1, source_target_pairs={{2,4},{4,2},{6,8},{8,6},{10,12},{12,10},{14,16},{16,14},{18,20},{2... | collective-permute-start | bytes 786440 | tf_op jit(solution)/shard_map/ppermute | solution.py:610
  14.7 1.1 %keep.1.refs_0_.refs_1_ = f32[2,5,4,32,128]{4,3,2,1,0:T(8,128)S(1)} custom-call(f32[2,5,16,32,128]{4,3,2,1,0:T(8,128)} %history.7, f32[8,64,128]{2,1,0:T(8,128)S(1)} %collective-permute-done.1.halo._), custom_call_target="tpu_custom_call" | custom-call | flops 1048576 | bytes 1048576 | tf_op jit(solution)/shard_map/keep/pallas_call | solution.py:570
  15.8 1.6 %collective-permute-start.7 = (f32[2,5,4,32,128]{4,3,2,1,0:T(8,128)S(1)}, f32[2,5,4,32,128]{4,3,2,1,0:T(8,128)S(1)}, u32[]{:S(2)}, u32[]{:S(2)}) collective-permute-start(f32[2,5,4,32,128]{4,3,2,1,0:T(8,128)S(1)} %keep.1.refs_0_.refs_1_), channel_id=1, source_target_pairs={{1,0},{0,1},{3,2},{2,3},{5,4},{4,5},{7,6},{6,7},{9,8},{8,9},{11,10... | collective-permute-start | bytes 1966088 | tf_op jit(solution)/shard_map/ppermute | solution.py:613
  17.4 2.2 %local_1.1 = (f32[16,64,128]{2,1,0:T(8,128)S(1)}, f32[16,80,128]{2,1,0:T(8,128)S(1)}, f32[16,64,128]{2,1,0:T(8,128)S(1)}, f32[16,80,128]{2,1,0:T(8,128)S(1)}) custom-call(s32[1]{0:T(128)S(6)} %copy.64.cell, f32[1,4]{1,0:T(1,128)S(1)} %copy-done.2, f32[16,80,128]{2,1,0:T(8,128)S(1)} %get-tuple-element.90.wave.wave_old, ...), custom_call_target="tpu_custom_call" | custom-call | flops 1048576 | bytes 1048576 | tf_op jit(solution)/shard_map/local_1/pallas_call | solution.py:570
  19.6 0.0 collective-permute-done.3.halo
  19.6 0.0 copy-start
  19.7 0.1 join_core_1.1
  19.8 2.7 %collective-permute-start.5 = (f32[8,64,128]{2,1,0:T(8,128)S(1)}, f32[8,64,128]{2,1,0:T(8,128)S(1)}, u32[]{:S(2)}, u32[]{:S(2)}) collective-permute-start(f32[8,64,128]{2,1,0:T(8,128)S(1)} %get-tuple-element.102), channel_id=1, source_target_pairs={{0,2},{2,0},{4,6},{6,4},{8,10},{10,8},{12,14},{14,12},{16,18},{18,... | collective-permute-start | bytes 786440 | tf_op jit(solution)/shard_map/ppermute | solution.py:607
  22.5 0.0 collective-permute-done.2.halo
  22.6 0.1 join_chip_1.1
  22.7 0.7 %collective-permute-start.4 = (f32[8,64,128]{2,1,0:T(8,128)S(1)}, f32[8,64,128]{2,1,0:T(8,128)S(1)}, u32[]{:S(2)}, u32[]{:S(2)}) collective-permute-start(f32[8,64,128]{2,1,0:T(8,128)S(1)} %get-tuple-element.101), channel_id=1, source_target_pairs={{2,4},{4,2},{6,8},{8,6},{10,12},{12,10},{14,16},{16,14},{18,20},{2... | collective-permute-start | bytes 786440 | tf_op jit(solution)/shard_map/ppermute | solution.py:610
  23.4 0.7 %gram.1.outs_0_ = f32[30,8,128]{2,1,0:T(8,128)S(1)} custom-call(f32[2,5,16,32,128]{4,3,2,1,0:T(8,128)S(1)} %copy-done), custom_call_target="tpu_custom_call" | custom-call | flops 1048576 | bytes 1048576 | tf_op jit(solution)/shard_map/gram/pallas_call | solution.py:570
  24.1 2.3 %local_2.1 = (f32[16,64,128]{2,1,0:T(8,128)S(1)}, f32[16,80,128]{2,1,0:T(8,128)S(1)}, f32[16,64,128]{2,1,0:T(8,128)S(1)}, f32[16,80,128]{2,1,0:T(8,128)S(1)}) custom-call(s32[1]{0:T(128)S(6)} %copy.64.cell, f32[1,4]{1,0:T(1,128)S(1)} %copy-done.2, f32[16,80,128]{2,1,0:T(8,128)S(1)} %get-tuple-element.103.wave, ...), custom_call_target="tpu_custom_call" | custom-call | flops 1048576 | bytes 1048576 | tf_op jit(solution)/shard_map/local_2/pallas_call | solution.py:570
  26.5 0.0 collective-permute-done.5.halo
  26.5 0.7 %join_far.1 = (f32[16,64,128]{2,1,0:T(8,128)S(1)}, f32[16,80,128]{2,1,0:T(8,128)S(1)}, f32[16,64,128]{2,1,0:T(8,128)S(1)}, f32[16,80,128]{2,1,0:T(8,128)S(1)}, f...) custom-call(f32[8,64,128]{2,1,0:T(8,128)S(1)} %collective-permute-do, ...), custom_call_target="tpu_custom_call", output_to_operand_aliasing={{0}: (2, {}), {1}: (3, {}), {2}: (4, {}), {3}: (5, {})} | custom-call | flops 1048576 | bytes 1048576 | tf_op jit(solution)/shard_map/join_far/pallas_call | solution.py:570
  27.2 5.0 %collective-permute-start.8 = (f32[8,64,128]{2,1,0:T(8,128)S(1)}, f32[8,64,128]{2,1,0:T(8,128)S(1)}, u32[]{:S(2)}, u32[]{:S(2)}) collective-permute-start(f32[8,64,128]{2,1,0:T(8,128)S(1)} %get-tuple-element.124), channel_id=1, source_target_pairs={{0,2},{2,0},{4,6},{6,4},{8,10},{10,8},{12,14},{14,12},{16,18},{18,... | collective-permute-start | bytes 786440 | tf_op jit(solution)/shard_map/ppermute | solution.py:607
  32.1 0.0 collective-permute-done.4.halo
  32.2 0.1 join_chip_2.1
  32.3 0.7 %collective-permute-start.6 = (f32[8,64,128]{2,1,0:T(8,128)S(1)}, f32[8,64,128]{2,1,0:T(8,128)S(1)}, u32[]{:S(2)}, u32[]{:S(2)}) collective-permute-start(f32[8,64,128]{2,1,0:T(8,128)S(1)} %get-tuple-element.116), channel_id=1, source_target_pairs={{2,4},{4,2},{6,8},{8,6},{10,12},{12,10},{14,16},{16,14},{18,20},{2... | collective-permute-start | bytes 786440 | tf_op jit(solution)/shard_map/ppermute | solution.py:610
  33.0 0.3 collective-permute-done.8.from_core
  33.3 0.6 core.1
  33.9 1.6 %collective-permute-start.9 = (f32[4,32,128]{2,1,0:T(8,128)S(1)}, f32[4,32,128]{2,1,0:T(8,128)S(1)}, u32[]{:S(2)}, u32[]{:S(2)}) collective-permute-start(f32[4,32,128]{2,1,0:T(8,128)S(1)} %get-tuple-element.125), channel_id=1, source_target_pairs={{1,0},{0,1},{3,2},{2,3},{5,4},{4,5},{7,6},{6,7},{9,8},{8,9},{11,10... | collective-permute-start | bytes 196616 | tf_op jit(solution)/shard_map/ppermute | solution.py:613
  35.5 0.6 inner.1
  36.1 0.6 collective-permute-start.10
  36.7 0.5 chip.1
  37.2 1.0 %collective-permute-done.9.refs_0_.refs_3_ = f32[4,32,128]{2,1,0:T(8,128)S(1)} collective-permute-done((f32[4,32,128]{2,1,0:T(8,128)S(1)}, f32[4,32,128]{2,1,0:T(8,128)S(1)}, u32[]{:S(2)}, u32[]{:S(2)}) %collective-permute-start.9) | collective-permute-done | bytes 65568 | tf_op jit(solution)/shard_map/ppermute | solution.py:613
  38.3 0.1 last_join.1.grad.chip
  38.3 1.6 %collective-permute-start.11 = (f32[4,64,128]{2,1,0:T(8,128)S(1)}, f32[4,64,128]{2,1,0:T(8,128)S(1)}, u32[]{:S(2)}, u32[]{:S(2)}) collective-permute-start(f32[4,64,128]{2,1,0:T(8,128)S(1)} %last_join.1.grad.chip), channel_id=1, source_target_pairs={{1,0},{0,1},{3,2},{2,3},{5,4},{4,5},{7,6},{6,7},{9,8},{8,9},{11,10... | collective-permute-start | bytes 393224 | tf_op jit(solution)/shard_map/ppermute | solution.py:613
  39.9 1.2 %collective-permute-done.10.refs_2_.refs_1_ = f32[8,32,128]{2,1,0:T(8,128)S(1)} collective-permute-done((f32[8,32,128]{2,1,0:T(8,128)S(1)}, f32[8,32,128]{2,1,0:T(8,128)S(1)}, u32[]{:S(2)}, u32[]{:S(2)}) %collective-permute-start.10) | collective-permute-done | bytes 131104 | tf_op jit(solution)/shard_map/ppermute | solution.py:613
  41.2 0.1 chip_dots.1.chip
  41.3 0.0 copy-start.1
  41.3 0.3 line.1
  41.6 15.2 %all_to_all.11 = f32[32,1,128]{2,1,0:T(1,128)S(1)} all-to-all(f32[32,1,128]{2,1,0:T(1,128)S(1)} %bitcast.10), channel_id=1, replica_groups=mesh['depth'=16,'shot'=2] {'depth','shot'}, dimensions={0} | all-to-all | bytes 32768 | tf_op jit(solution)/shard_map/all_to_all | solution.py:779
  56.8 0.3 weights.1
  57.1 0.6 collective-permute-start.12
  57.7 1.1 %finish.1 = (f32[16,32,128]{2,1,0:T(8,128)}, f32[16,32,128]{2,1,0:T(8,128)}, f32[16,64,128]{2,1,0:T(8,128)}) custom-call(f32[11,8,128]{2,1,0:T(8,128)S(1)} %get-tuple-element.132.weight, f32[16,64,128]{2,1,0:T(8,128)S(1)} %copy-done.1, f32[12,32,128]{2,1,0:T(8,128)S(1)} %get-tuple-element.131.near, f32[12,32,128]{2,1,0:T(8,128)S(1)} %get-tuple-element.133.near_move, ...), custom_call_target="tpu_custom_call" | custom-call | flops 1048576 | bytes 1048576 | tf_op jit(solution)/shard_map/finish/pallas_call | solution.py:570
  58.9 4.9 %collective-permute-done.12.refs_0_ = f32[12,32,128]{2,1,0:T(8,128)S(1)} collective-permute-done((f32[12,32,128]{2,1,0:T(8,128)S(1)}, f32[12,32,128]{2,1,0:T(8,128)S(1)}, u32[]{:S(2)}, u32[]{:S(2)}) %collective-permute-start.12) | collective-permute-done | bytes 196640 | tf_op jit(solution)/shard_map/ppermute | solution.py:613
  63.8 0.7 %last_piece.1 = f32[16,64,128]{2,1,0:T(8,128)} custom-call(f32[16,64,128]{2,1,0:T(8,128)S(1)} %copy-done.1, f32[16,64,128]{2,1,0:T(8,128)} %get-tuple-element.136.done, f32[12,32,128]{2,1,0:T(8,128)S(1)} %collective-permute-done.12.refs_0_), custom_call_target="tpu_custom_call", output_to_operand_aliasing={{}: (1, {})} | custom-call | flops 1048576 | bytes 1048576 | tf_op jit(solution)/shard_map/last_piece/pallas_call | solution.py:570
  (12 shorter events, 0.0 us)
Async XLA Ops:
  0.6 5.0 %copy-start.3 = (f32[1,4,256]{2,1,0:T(4,128)S(1)}, f32[1,4,256]{2,1,0:T(4,128)}, u32[]{:S(2)}) copy-start(f32[1,4,256]{2,1,0:T(4,128)} %param.18) | copy-start | bytes 12292
  0.6 5.0 %copy-start.4 = (s32[1,256]{1,0:T(1,128)S(1)}, s32[1,256]{1,0:T(1,128)}, u32[]{:S(2)}) copy-start(s32[1,256]{1,0:T(1,128)} %receivers.3) | copy-start | bytes 3076
  2.0 5.5 %copy-start.2 = (f32[1,4]{1,0:T(1,128)S(1)}, f32[1,4]{1,0:T(1,128)}, u32[]{:S(2)}) copy-start(f32[1,4]{1,0:T(1,128)} %wavelet.5) | copy-start | bytes 52
  2.0 7.8 %collective-permute-start.1 = (f32[8,64,128]{2,1,0:T(8,128)S(1)}, f32[8,64,128]{2,1,0:T(8,128)S(1)}, u32[]{:S(2)}, u32[]{:S(2)}) collective-permute-start(f32[8,64,128]{2,1,0:T(8,128)S(1)} %get-tuple-element.72), channel_id=1, source_target_pairs={{0,2},{2,0},{4,6},{6,4},{8,10},{10,8},{12,14},{14,12},{16,18},{18,... | collective-permute-start | bytes 786440 | tf_op jit(solution)/shard_map/ppermute | solution.py:607
  2.5 11.4 %collective-permute-start = (f32[8,64,128]{2,1,0:T(8,128)S(1)}, f32[8,64,128]{2,1,0:T(8,128)S(1)}, u32[]{:S(2)}, u32[]{:S(2)}) collective-permute-start(f32[8,64,128]{2,1,0:T(8,128)S(1)} %get-tuple-element.70), channel_id=1, source_target_pairs={{2,4},{4,2},{6,8},{8,6},{10,12},{12,10},{14,16},{16,14},{18,20},{2... | collective-permute-start | bytes 786440 | tf_op jit(solution)/shard_map/ppermute | solution.py:610
  10.0 9.7 %collective-permute-start.3 = (f32[8,64,128]{2,1,0:T(8,128)S(1)}, f32[8,64,128]{2,1,0:T(8,128)S(1)}, u32[]{:S(2)}, u32[]{:S(2)}) collective-permute-start(f32[8,64,128]{2,1,0:T(8,128)S(1)} %get-tuple-element.89), channel_id=1, source_target_pairs={{0,2},{2,0},{4,6},{6,4},{8,10},{10,8},{12,14},{14,12},{16,18},{18,... | collective-permute-start | bytes 786440 | tf_op jit(solution)/shard_map/ppermute | solution.py:607
  14.0 8.5 %collective-permute-start.2 = (f32[8,64,128]{2,1,0:T(8,128)S(1)}, f32[8,64,128]{2,1,0:T(8,128)S(1)}, u32[]{:S(2)}, u32[]{:S(2)}) collective-permute-start(f32[8,64,128]{2,1,0:T(8,128)S(1)} %get-tuple-element.88), channel_id=1, source_target_pairs={{2,4},{4,2},{6,8},{8,6},{10,12},{12,10},{14,16},{16,14},{18,20},{2... | collective-permute-start | bytes 786440 | tf_op jit(solution)/shard_map/ppermute | solution.py:610
  15.8 20.9 %collective-permute-start.7 = (f32[2,5,4,32,128]{4,3,2,1,0:T(8,128)S(1)}, f32[2,5,4,32,128]{4,3,2,1,0:T(8,128)S(1)}, u32[]{:S(2)}, u32[]{:S(2)}) collective-permute-start(f32[2,5,4,32,128]{4,3,2,1,0:T(8,128)S(1)} %keep.1.refs_0_.refs_1_), channel_id=1, source_target_pairs={{1,0},{0,1},{3,2},{2,3},{5,4},{4,5},{7,6},{6,7},{9,8},{8,9},{11,10... | collective-permute-start | bytes 1966088 | tf_op jit(solution)/shard_map/ppermute | solution.py:613
  19.6 3.7 %copy-start = (f32[2,5,16,32,128]{4,3,2,1,0:T(8,128)S(1)}, f32[2,5,16,32,128]{4,3,2,1,0:T(8,128)}, u32[]{:S(2)}) copy-start(f32[2,5,16,32,128]{4,3,2,1,0:T(8,128)} %history.7) | copy-start | bytes 7864324
  19.8 6.7 %collective-permute-start.5 = (f32[8,64,128]{2,1,0:T(8,128)S(1)}, f32[8,64,128]{2,1,0:T(8,128)S(1)}, u32[]{:S(2)}, u32[]{:S(2)}) collective-permute-start(f32[8,64,128]{2,1,0:T(8,128)S(1)} %get-tuple-element.102), channel_id=1, source_target_pairs={{0,2},{2,0},{4,6},{6,4},{8,10},{10,8},{12,14},{14,12},{16,18},{18,... | collective-permute-start | bytes 786440 | tf_op jit(solution)/shard_map/ppermute | solution.py:607
  22.7 9.5 %collective-permute-start.4 = (f32[8,64,128]{2,1,0:T(8,128)S(1)}, f32[8,64,128]{2,1,0:T(8,128)S(1)}, u32[]{:S(2)}, u32[]{:S(2)}) collective-permute-start(f32[8,64,128]{2,1,0:T(8,128)S(1)} %get-tuple-element.101), channel_id=1, source_target_pairs={{2,4},{4,2},{6,8},{8,6},{10,12},{12,10},{14,16},{16,14},{18,20},{2... | collective-permute-start | bytes 786440 | tf_op jit(solution)/shard_map/ppermute | solution.py:610
  27.2 6.2 %collective-permute-start.8 = (f32[8,64,128]{2,1,0:T(8,128)S(1)}, f32[8,64,128]{2,1,0:T(8,128)S(1)}, u32[]{:S(2)}, u32[]{:S(2)}) collective-permute-start(f32[8,64,128]{2,1,0:T(8,128)S(1)} %get-tuple-element.124), channel_id=1, source_target_pairs={{0,2},{2,0},{4,6},{6,4},{8,10},{10,8},{12,14},{14,12},{16,18},{18,... | collective-permute-start | bytes 786440 | tf_op jit(solution)/shard_map/ppermute | solution.py:607
  32.3 4.9 %collective-permute-start.6 = (f32[8,64,128]{2,1,0:T(8,128)S(1)}, f32[8,64,128]{2,1,0:T(8,128)S(1)}, u32[]{:S(2)}, u32[]{:S(2)}) collective-permute-start(f32[8,64,128]{2,1,0:T(8,128)S(1)} %get-tuple-element.116), channel_id=1, source_target_pairs={{2,4},{4,2},{6,8},{8,6},{10,12},{12,10},{14,16},{16,14},{18,20},{2... | collective-permute-start | bytes 786440 | tf_op jit(solution)/shard_map/ppermute | solution.py:610
  33.9 4.3 %collective-permute-start.9 = (f32[4,32,128]{2,1,0:T(8,128)S(1)}, f32[4,32,128]{2,1,0:T(8,128)S(1)}, u32[]{:S(2)}, u32[]{:S(2)}) collective-permute-start(f32[4,32,128]{2,1,0:T(8,128)S(1)} %get-tuple-element.125), channel_id=1, source_target_pairs={{1,0},{0,1},{3,2},{2,3},{5,4},{4,5},{7,6},{6,7},{9,8},{8,9},{11,10... | collective-permute-start | bytes 196616 | tf_op jit(solution)/shard_map/ppermute | solution.py:613
  36.1 5.0 %collective-permute-start.10 = (f32[8,32,128]{2,1,0:T(8,128)S(1)}, f32[8,32,128]{2,1,0:T(8,128)S(1)}, u32[]{:S(2)}, u32[]{:S(2)}) collective-permute-start(f32[8,32,128]{2,1,0:T(8,128)S(1)} %get-tuple-element.128), channel_id=1, source_target_pairs={{1,0},{0,1},{3,2},{2,3},{5,4},{4,5},{7,6},{6,7},{9,8},{8,9},{11,10... | collective-permute-start | bytes 393224 | tf_op jit(solution)/shard_map/ppermute | solution.py:613
  38.3 18.5 %collective-permute-start.11 = (f32[4,64,128]{2,1,0:T(8,128)S(1)}, f32[4,64,128]{2,1,0:T(8,128)S(1)}, u32[]{:S(2)}, u32[]{:S(2)}) collective-permute-start(f32[4,64,128]{2,1,0:T(8,128)S(1)} %last_join.1.grad.chip), channel_id=1, source_target_pairs={{1,0},{0,1},{3,2},{2,3},{5,4},{4,5},{7,6},{6,7},{9,8},{8,9},{11,10... | collective-permute-start | bytes 393224 | tf_op jit(solution)/shard_map/ppermute | solution.py:613
  41.3 16.4 %copy-start.1 = (f32[16,64,128]{2,1,0:T(8,128)S(1)}, f32[16,64,128]{2,1,0:T(8,128)}, u32[]{:S(2)}) copy-start(f32[16,64,128]{2,1,0:T(8,128)} %courant.7) | copy-start | bytes 1572868
  57.1 6.7 %collective-permute-start.12 = (f32[12,32,128]{2,1,0:T(8,128)S(1)}, f32[12,32,128]{2,1,0:T(8,128)S(1)}, u32[]{:S(2)}, u32[]{:S(2)}) collective-permute-start(f32[12,32,128]{2,1,0:T(8,128)S(1)} %get-tuple-element.133.near_move), channel_id=1, source_target_pairs={{1,0},{0,1},{3,2},{2,3},{5,4},{4,5},{7,6},{6,7},{9,8},{8,9},{11,10... | collective-permute-start | bytes 589832 | tf_op jit(solution)/shard_map/ppermute | solution.py:613
